TPU v7x, 32 devices: a whole 2x2x4 slice. The times are simulated.
32 devices in a mesh: member: 2 (over y), tile: 4 (over z), nest: 2 (over x), lev: 2 (over core).
Axes of the slice: x: 2, y: 2, z: 4, core: 2. Of those that a mesh axis runs over, the one named last changes fastest.
Arguments:
- parent_field: float32 [10, 2, 256, 512], P('member', None, 'tile', ('nest', 'lev')), parts along dimension 0, may hold values from -6 to 6
- nest_fields: float32 [12, 5, 2, 384, 384], P(('member', 'nest'), None, None, 'tile', 'lev'), parts along dimension 0, may hold values from -6 to 6
- lateral_rate: float32 [5], replicated, may hold values from 0.02 to 0.12
- vertical_rate: float32 [5], replicated, may hold values from 0.02 to 0.12
- centres: int32 [6, 6, 2], P('member'), parts along dimension 0, may hold values from 64 to 448, as said below
- slot_storm: int32 [12], P('member'), parts along dimension 0, may hold values from 0 to 5, each once
Outputs:
- parent_final: float32 [10, 2, 256, 512], P('member', None, 'tile', ('nest', 'lev')), parts along dimension 0
- nest_final: float32 [12, 5, 2, 384, 384], P(('member', 'nest'), None, None, 'tile', 'lev'), parts along dimension 0
There are 2 independent parts, one for each index of `member`. A program takes and returns all parts, laid end to end along the dimension named above; an argument that names none is the same for every part. Nothing has to cross between parts.
Inputs may be any that keep to these rules, and one draw needn't show every extreme that they name: `centres`: from one step to the next the row of a centre changes by 1 to 2 cells in either direction and the column by at most 2 cells; rows stay within 64 to 192 and columns within 64 to 448. `slot_storm`: every storm occupies exactly one nest position.
All inputs are finite; a program needn't handle non-finite values.
Results may differ from a plain program's by a relative error of at most 0.0003.
Values sent between devices are 32-bit elements; how exact they have to be, the bound alone decides.
No kernel may reach another device: no remote copies, remote signals or barrier semaphores. Data moves between devices by JAX's collectives and lax.ppermute only.
A program may use at most 128 MiB of HBM per device.

v0:
```python
import jax
import jax.numpy as jnp
from jax import lax
from jax.sharding import PartitionSpec as P

FP = 128
BWP = 2
MOVE = 2


def extended(cells, sides, width):
    for axis, dim in sides:
        count = lax.axis_size(axis)
        ends = count - 1
        head = lax.slice_in_dim(cells, 0, width, axis=dim)
        tail = lax.slice_in_dim(cells, cells.shape[dim] - width, cells.shape[dim], axis=dim)
        cells = jnp.concatenate(
            [
                lax.ppermute(tail, axis, [(i, (i + 1) % count) for i in range(ends)]),
                cells,
                lax.ppermute(head, axis, [((i + 1) % count, i) for i in range(ends)]),
            ],
            axis=dim,
        )
    return cells


def tendency(padded, lateral_rate, vertical_rate):
    centre = padded[..., 1:-1, 1:-1, 1:-1]
    lateral = (
        padded[..., 1:-1, 2:, 1:-1]
        + padded[..., 1:-1, :-2, 1:-1]
        + padded[..., 1:-1, 1:-1, 2:]
        + padded[..., 1:-1, 1:-1, :-2]
        - 4.0 * centre
    )
    upright = padded[..., 2:, 1:-1, 1:-1] + padded[..., :-2, 1:-1, 1:-1] - 2.0 * centre
    change = (
        lateral_rate[:, None, None, None] * lateral + vertical_rate[:, None, None, None] * upright
    )
    return (centre, change)


def select_rows(picker, table):
    return jnp.sum(picker[:, :, None] * table[None, :, :], axis=1)


def column_block():
    return lax.axis_index("nest") * lax.axis_size("lev") + lax.axis_index("lev")


def extract(parent_now, anchors):
    fields, level_count, parent_rows, parent_cols = parent_now.shape
    padded = jnp.pad(parent_now, ((0, 0), (0, 0), (FP, FP), (FP, FP)))
    rel_rows = anchors[:, 0] - lax.axis_index("tile") * parent_rows + FP
    rel_cols = anchors[:, 1] - column_block() * parent_cols + FP
    zero_index = jnp.zeros((), jnp.int32)

    def single(corner):
        row_at = corner[0]
        col_at = corner[1]
        within = (
            (row_at >= 0)
            & (row_at <= FP + parent_rows)
            & (col_at >= 0)
            & (col_at <= FP + parent_cols)
        )
        row_at = jnp.clip(row_at, 0, FP + parent_rows)
        col_at = jnp.clip(col_at, 0, FP + parent_cols)
        south = lax.dynamic_slice(
            padded, (zero_index, zero_index, row_at, col_at), (fields, level_count, BWP, FP)
        )
        north = lax.dynamic_slice(
            padded,
            (zero_index, zero_index, row_at + FP - BWP, col_at),
            (fields, level_count, BWP, FP),
        )
        west = lax.dynamic_slice(
            padded, (zero_index, zero_index, row_at, col_at), (fields, level_count, FP, BWP)
        )
        east = lax.dynamic_slice(
            padded,
            (zero_index, zero_index, row_at, col_at + FP - BWP),
            (fields, level_count, FP, BWP),
        )
        sides = jnp.stack(
            [south, north, jnp.swapaxes(west, 2, 3), jnp.swapaxes(east, 2, 3)], axis=2
        )
        return jnp.where(within, sides.reshape(fields, level_count, 4 * BWP * FP), 0.0)

    corners = jnp.stack([rel_rows, rel_cols], axis=1)
    return lax.map(single, corners)


def per_device(parent_field, nest_fields, lateral_rate, vertical_rate, centres, slot_storm):
    fields, level_count, parent_rows, parent_cols = parent_field.shape
    slot_count = nest_fields.shape[0]
    strip_rows = nest_fields.shape[3]
    strip_cols = nest_fields.shape[4]
    storm_count = slot_storm.shape[0]
    steps_total = centres.shape[0] - 1
    tile_at = lax.axis_index("tile")
    nest_at = lax.axis_index("nest")
    lev_at = lax.axis_index("lev")
    nest_span = 3 * FP
    reach_rows = 3 * MOVE
    border = 3 * BWP
    zero_index = jnp.zeros((), jnp.int32)
    storm_ids = jnp.arange(storm_count, dtype=jnp.int32)
    pick_all = (slot_storm[:, None] == storm_ids[None, :]).astype(jnp.int32)
    owned = lax.dynamic_slice_in_dim(slot_storm, nest_at * slot_count, slot_count)
    pick_own = (owned[:, None] == storm_ids[None, :]).astype(jnp.int32)
    global_rows = tile_at * strip_rows + jnp.arange(strip_rows, dtype=jnp.int32)
    global_cols = lev_at * strip_cols + jnp.arange(strip_cols, dtype=jnp.int32)
    row_gap = jnp.minimum(global_rows, nest_span - 1 - global_rows)
    col_gap = jnp.minimum(global_cols, nest_span - 1 - global_cols)
    distance = jnp.minimum(row_gap[:, None], col_gap[None, :])
    weight = jnp.maximum(border - distance, 0).astype(jnp.float32) / jnp.float32(border)
    inside = (distance >= 1).astype(jnp.float32)
    coarse_rows = global_rows // 3
    coarse_cols = global_cols // 3
    south_index = jnp.clip(coarse_rows, 0, BWP - 1)
    north_index = jnp.clip(coarse_rows - (FP - BWP), 0, BWP - 1)
    west_index = jnp.clip(coarse_cols, 0, BWP - 1)
    east_index = jnp.clip(coarse_cols - (FP - BWP), 0, BWP - 1)
    near_south = (coarse_rows < BWP)[:, None]
    near_north = (coarse_rows >= FP - BWP)[:, None]
    near_west = (coarse_cols < BWP)[None, :]
    near_east = (coarse_cols >= FP - BWP)[None, :]

    def relocate(single, offset):
        return lax.dynamic_slice(
            single,
            (zero_index, zero_index, reach_rows + offset[0], reach_rows + offset[1]),
            (fields, level_count, strip_rows, strip_cols),
        )

    def across(zone, zone_index):
        picked = jnp.take(zone, zone_index, axis=3)
        return jnp.take(picked, coarse_cols, axis=4)

    def along(zone, zone_index):
        picked = jnp.take(zone, zone_index, axis=3)
        picked = jnp.take(picked, coarse_rows, axis=4)
        return jnp.swapaxes(picked, 3, 4)

    parent_now = parent_field
    nests_now = nest_fields
    for step_index in range(steps_total):
        padded = extended(parent_now, (("tile", 2), (("nest", "lev"), 3)), 1)
        padded = jnp.pad(padded, ((0, 0), (1, 1), (0, 0), (0, 0)))
        centre, change = tendency(padded, lateral_rate, vertical_rate)
        parent_now = centre + change
        later_pos = select_rows(pick_all, centres[step_index + 1])
        anchors = later_pos - FP // 2
        terms = extract(parent_now, anchors)
        totals = lax.psum(terms, ("tile", "nest", "lev"))
        boundary = lax.dynamic_slice_in_dim(totals, nest_at * slot_count, slot_count, 0)
        boundary = boundary.reshape(slot_count, fields, level_count, 4, BWP, FP)
        south_full = across(boundary[:, :, :, 0], south_index)
        north_full = across(boundary[:, :, :, 1], north_index)
        west_full = along(boundary[:, :, :, 2], west_index)
        east_full = along(boundary[:, :, :, 3], east_index)
        sides_full = jnp.where(near_west, west_full, jnp.where(near_east, east_full, 0.0))
        driving = jnp.where(near_south, south_full, jnp.where(near_north, north_full, sides_full))
        own_later = select_rows(pick_own, centres[step_index + 1])
        own_before = select_rows(pick_own, centres[step_index])
        offsets = 3 * (own_later - own_before)
        widened_nests = extended(nests_now, (("tile", 3), ("lev", 4)), reach_rows)
        shifted = jax.vmap(relocate)(widened_nests, offsets)
        source_rows = global_rows[None, :] + offsets[:, 0:1]
        source_cols = global_cols[None, :] + offsets[:, 1:2]
        rows_fine = (source_rows >= 0) & (source_rows < nest_span)
        cols_fine = (source_cols >= 0) & (source_cols < nest_span)
        keep_mask = (rows_fine[:, :, None] & cols_fine[:, None, :])[:, None, None, :, :]
        retained = jnp.where(keep_mask, shifted, driving)
        relaxed = retained + weight * (driving - retained)
        bordered = extended(relaxed, (("tile", 3), ("lev", 4)), 1)
        bordered = jnp.pad(bordered, ((0, 0), (0, 0), (1, 1), (0, 0), (0, 0)))
        centre, change = tendency(bordered, lateral_rate, vertical_rate)
        nests_now = relaxed + inside * change
    return (parent_now, nests_now)


def solution(mesh):
    placed = (
        P("member", None, "tile", ("nest", "lev")),
        P(("member", "nest"), None, None, "tile", "lev"),
        P(),
        P(),
        P("member", None, None),
        P("member"),
    )
    return jax.shard_map(
        per_device,
        mesh=mesh,
        in_specs=placed,
        out_specs=(
            P("member", None, "tile", ("nest", "lev")),
            P(("member", "nest"), None, None, "tile", "lev"),
        ),
        check_vma=False,
    )
```

profile of v0, /device:TPU:16, one launch (start us, length us, event | category | flops | bytes accessed | tf_op | source)
XLA Modules:
  0.0 789.5 jit_solution(10287252542518076452)
XLA Ops:
  46.2 5.5 copy.328
  57.2 6.2 collective-permute-start.7
  63.5 50.7 %while.32 = (s32[]{:T(128)}, f32[6,5,2,1024]{3,2,1,0:T(2,128)S(1)}, s32[6,2]{0,1:T(2,128)S(1)}, f32[5,2,320,384]{2,3,1,0:T(8,128)}, s32[]{:T(128)}, /*index=5*/s...) while((s32[]{:T(128)}, f32[6,5,2,1024]{3,2,1,0:T(2,128)S(1)}, ...), condition=%wide.region_5.6_spmd, body=%wide.region_4.5_spmd.sunk | while | flops 40981 | bytes 450935 | solution.py:92
  130.8 6.1 collective-permute-start.10
  137.0 50.4 %while.33 = (s32[]{:T(128)}, f32[6,5,2,1024]{3,2,1,0:T(2,128)S(1)}, s32[6,2]{0,1:T(2,128)S(1)}, f32[5,2,320,384]{2,3,1,0:T(8,128)}, s32[]{:T(128)}, /*index=5*/s...) while((s32[]{:T(128)}, f32[6,5,2,1024]{3,2,1,0:T(2,128)S(1)}, ...), condition=%wide.region_9.14_spmd, body=%wide.region_8.13_spmd.sunk | while | flops 40981 | bytes 450935 | solution.py:92
  188.1 8.2 %pad_maximum_fusion = f32[3,5,2,108,204]{3,2,4,1,0:T(2,128)S(1)} fusion(f32[3,5,2,108,6]{3,2,4,1,0:T(2,128)S(1)} %collective-permute-done.11, f32[3,5,2,6,192]{3,2,4,1,0:T(2,128)} %copy.329, f32[3,5,2,96,192]{3,2,4,1,0:T(2,128)} %copy.328, f32[3,5,2,6,192]{3,2,4,1,0:T(2,128)} %copy.327, f32[3,5,2,108,6]{3,2,4,1,0:T(2,128)} %collective-permute-done.10), kind=kLoop, calls=%fused_computation.46 | loop fusion | flops 2643840 | bytes 5287680 | tf_op jit(solution)/shard_map/concatenate | solution.py:17
  198.7 13.3 %while.34 = (s32[]{:T(128)}, f32[3,5,2,108,204]{3,2,4,1,0:T(2,128)S(1)}, s32[3,5]{1,0:T(4,128)S(1)}, f32[3,5,2,96,192]{3,2,1,0,4:T(2,128)}, s32[]{:T(128)}) while((s32[]{:T(128)}, f32[3,5,2,108,204]{3,2,4,1,0:T(2,128)S(1)}, s32[3,5]{1,0:T(4,128)S(1)}, f32[3,5,2,96,192]{3,2,1,0,4:T(2,128)}, s32[]{:T(128)}) %tuple.212), condition=%wide.while_cond, body=%wide.while_body.sunk | while | flops 2 | bytes 1967757 | solution.py:132
  212.0 66.8 %all-reduce.9.cloned.1.call-done = (f32[6,5,2,1024]{3,2,1,0:T(2,128)}, f32[6,5,2,1024]{3,2,1,0:T(2,128)}) async-done(((f32[6,5,2,1024]{3,2,1,0:T(2,128)}, f32[6,5,2,1024]{3,2,1,0:T(2,128)}), (f32[6,5,2,1024]{3,2,1,0:T(2,128)}, f32[6,5,2,1024]{3,2,1,0:T(2,128)})) %all-reduce.9.cloned.1.call-update) | async-done | bytes 491536 | tf_op jit(solution)/shard_map/psum | solution.py:157
  280.3 12.2 %gather_fusion.14 = f32[192,3,5,2,128]{4,3,2,1,0:T(2,128)S(1)} fusion(f32[3,5,2,2,128]{4,2,3,1,0:T(2,128)S(1)} %bitcast.166, s32[1024]{0:T(1024)S(1)} %pad_clamp_fusion), kind=kCustom, calls=%fused_computation.12.clone | custom fusion | bytes 5899008 | tf_op jit(solution)/shard_map/jit(_take)/gather | solution.py:143
  292.5 11.2 %gather_fusion.6 = f32[192,3,5,2,128]{4,3,2,1,0:T(2,128)} fusion(f32[3,5,2,2,128]{4,2,3,1,0:T(2,128)S(1)} %bitcast.167, s32[1024]{0:T(1024)S(1)} %pad_clamp_fusion), kind=kCustom, calls=%fused_computation.10.clone | custom fusion | bytes 5899008 | tf_op jit(solution)/shard_map/jit(_take)/gather | solution.py:143
  303.7 6.8 select_bitcast_fusion
  310.5 7.9 %copy.342 = f32[3,5,2,192,128]{3,2,4,1,0:T(2,128)} copy(f32[3,5,2,192,128]{4,2,1,0,3:T(2,128)} %get-tuple-element.471) | data formatting | bytes 5898240 | tf_op jit(solution)/shard_map/jit(_take)/select_n | solution.py:143
  318.4 11.0 %gather_fusion.7 = f32[96,3,5,2,192]{4,3,2,1,0:T(2,128)S(1)} fusion(f32[3,5,2,192,128]{3,2,4,1,0:T(2,128)} %copy.342, s32[1024]{0:T(1024)S(1)} %pad_clamp_fusion.1), kind=kCustom, calls=%fused_computation.13.clone | custom fusion | bytes 4424064 | tf_op jit(solution)/shard_map/jit(_take)/gather | solution.py:144
  329.4 5.2 copy.343
  334.7 12.1 %gather_fusion.12 = f32[192,3,5,2,128]{4,3,2,1,0:T(2,128)S(1)} fusion(f32[3,5,2,2,128]{4,2,3,1,0:T(2,128)S(1)} %bitcast.169, s32[1024]{0:T(1024)S(1)} %pad_clamp_fusion.2), kind=kCustom, calls=%fused_computation.11.clone | custom fusion | bytes 5899008 | tf_op jit(solution)/shard_map/jit(_take)/gather | solution.py:143
  346.7 10.6 %gather_fusion.4 = f32[192,3,5,2,128]{4,3,2,1,0:T(2,128)} fusion(f32[3,5,2,2,128]{4,2,3,1,0:T(2,128)S(1)} %bitcast.168, s32[1024]{0:T(1024)S(1)} %pad_clamp_fusion.2), kind=kCustom, calls=%fused_computation.2.clone | custom fusion | bytes 5899008 | tf_op jit(solution)/shard_map/jit(_take)/gather | solution.py:143
  357.4 6.8 select_bitcast_fusion.1
  364.2 8.0 %copy.339 = f32[3,5,2,192,128]{3,2,4,1,0:T(2,128)} copy(f32[3,5,2,192,128]{4,2,1,0,3:T(2,128)} %get-tuple-element.469) | data formatting | bytes 5898240 | tf_op jit(solution)/shard_map/jit(_take)/select_n | solution.py:143
  372.1 11.4 %gather_fusion.5 = f32[96,3,5,2,192]{4,3,2,1,0:T(2,128)S(1)} fusion(f32[3,5,2,192,128]{3,2,4,1,0:T(2,128)} %copy.339, s32[1024]{0:T(1024)S(1)} %pad_clamp_fusion.1), kind=kCustom, calls=%fused_computation.3.clone | custom fusion | bytes 4424064 | tf_op jit(solution)/shard_map/jit(_take)/gather | solution.py:144
  383.5 5.2 copy.340
  407.5 4.8 select_bitcast_fusion.5
  412.3 4.5 copy.335
  416.8 12.1 %gather_fusion.3 = f32[192,3,5,2,96]{4,3,2,1,0:T(2,128)} fusion(f32[3,5,2,96,128]{3,2,4,1,0:T(2,128)S(1)} %copy.337, s32[1024]{0:T(1024)S(1)} %pad_clamp_fusion.4), kind=kCustom, calls=%fused_computation.7.clone | custom fusion | bytes 4424448 | tf_op jit(solution)/shard_map/jit(_take)/gather | solution.py:140
  429.0 14.0 %gather_fusion.1 = f32[192,3,5,2,96]{4,3,2,1,0:T(2,128)} fusion(f32[3,5,2,96,128]{3,2,4,1,0:T(2,128)} %copy.335, s32[1024]{0:T(1024)S(1)} %pad_clamp_fusion.4), kind=kCustom, calls=%fused_computation.1.clone | custom fusion | bytes 4424448 | tf_op jit(solution)/shard_map/jit(_take)/gather | solution.py:140
  443.0 9.3 %multiply_add_fusion.3 = f32[3,5,2,96,192]{3,2,1,0,4:T(2,128)S(1)} fusion(f32[3,5,2,96,192]{3,2,1,0,4:T(2,128)} %get-tuple-element.219, pred[3,96,192]{1,0,2:T(4,128)(4,1)S(1)} %copy-done.13, f32[96,3,5,2,192]{0,3,2,1,4:T(2,128)} %copy.343, pred[192]{0:T(512)(128)(4,1)S(1)} %copy-done.18, f32[96,3,5,2,192]{0,3,2,1,4:T(2,128)} %copy.340, ...), kind=kLoop, calls=%fused_computation.97 | loop fusion | flops 6635520 | bytes 13400928 | tf_op jit(solution)/shard_map/add | solution.py:177
  452.3 6.7 fusion.56
  485.9 8.6 %select_maximum_fusion.4 = f32[3,5,4,98,194]{3,2,1,0,4:T(4,128)S(1)} fusion(f32[3,5,2,98,1]{3,2,1,0,4:T(2,128)S(1)} %collective-permute-done.14, f32[3,5,2,98,1]{3,2,1,0,4:T(2,128)S(1)} %collective-permute-done.15, f32[3,5,2,1,192]{3,2,1,0,4:T(2,128)S(1)} %copy-done.2, f32[3,5,2,96,192]{3,2,1,0,4:T(2,128)S(1)} %multiply_add_fusion.3, ...), kind=kLoop, calls=%fused_computation.41 | loop fusion | flops 13688640 | bytes 6844320 | tf_op jit(solution)/shard_map/concatenate | solution.py:17
  494.5 37.4 %multiply_add_fusion.2 = f32[3,5,2,96,192]{3,2,1,0,4:T(2,128)S(1)} fusion(f32[3,5,2,96,192]{3,2,1,0,4:T(2,128)S(1)} %multiply_add_fusion.3, f32[3,5,4,98,194]{3,2,1,0,4:T(4,128)S(1)} %select_maximum_fusion.4, f32[3,5,2,1,192]{3,2,1,0,4:T(2,128)S(1)} %copy-done.2, f32[3,5,2,1,192]{3,2,1,0,4:T(2,128)S(1)} %copy-done.4, ...), kind=kLoop, calls=%fused_computation.96 | loop fusion | flops 11612160 | bytes 8990728 | tf_op jit(solution)/shard_map/add | solution.py:181
  531.9 5.6 fusion.55
  568.6 8.2 %copy.367 = f32[3,5,2,192,128]{3,2,4,1,0:T(2,128)} copy(f32[3,5,2,192,128]{4,2,1,0,3:T(2,128)} %get-tuple-element.470) | data formatting | bytes 5898240 | tf_op jit(solution)/shard_map/jit(_take)/select_n | solution.py:143
  576.8 10.8 %gather_fusion.15 = f32[96,3,5,2,192]{4,3,2,1,0:T(2,128)} fusion(f32[3,5,2,192,128]{3,2,4,1,0:T(2,128)} %copy.367, s32[1024]{0:T(1024)S(1)} %pad_clamp_fusion.1), kind=kCustom, calls=%fused_computation.15.clone | custom fusion | bytes 4424064 | tf_op jit(solution)/shard_map/jit(_take)/gather | solution.py:144
  587.5 7.3 copy.368
  594.8 8.0 %copy.364 = f32[3,5,2,192,128]{3,2,4,1,0:T(2,128)} copy(f32[3,5,2,192,128]{4,2,1,0,3:T(2,128)} %get-tuple-element.468) | data formatting | bytes 5898240 | tf_op jit(solution)/shard_map/jit(_take)/select_n | solution.py:143
  602.8 10.8 %gather_fusion.13 = f32[96,3,5,2,192]{4,3,2,1,0:T(2,128)} fusion(f32[3,5,2,192,128]{3,2,4,1,0:T(2,128)} %copy.364, s32[1024]{0:T(1024)S(1)} %pad_clamp_fusion.1), kind=kCustom, calls=%fused_computation.14.clone | custom fusion | bytes 4424064 | tf_op jit(solution)/shard_map/jit(_take)/gather | solution.py:144
  613.6 7.3 copy.365
  620.9 4.5 copy.362
  625.4 13.9 %gather_fusion.11 = f32[192,3,5,2,96]{4,3,2,1,0:T(2,128)} fusion(f32[3,5,2,96,128]{3,2,4,1,0:T(2,128)} %copy.362, s32[1024]{0:T(1024)S(1)} %pad_clamp_fusion.4), kind=kCustom, calls=%fused_computation.9.clone | custom fusion | bytes 4424448 | tf_op jit(solution)/shard_map/jit(_take)/gather | solution.py:140
  643.8 13.6 %gather_fusion.9 = f32[192,3,5,2,96]{4,3,2,1,0:T(2,128)} fusion(f32[3,5,2,96,128]{3,2,4,1,0:T(2,128)} %copy.360, s32[1024]{0:T(1024)S(1)} %pad_clamp_fusion.4), kind=kCustom, calls=%fused_computation.8.clone | custom fusion | bytes 4424448 | tf_op jit(solution)/shard_map/jit(_take)/gather | solution.py:140
  657.5 9.3 %pad_maximum_fusion.1 = f32[3,5,2,108,204]{3,2,1,0,4:T(2,128)} fusion(f32[3,5,2,108,6]{3,2,1,0,4:T(2,128)S(1)} %collective-permute-done.19, f32[3,5,2,6,192]{3,2,1,0,4:T(2,128)} %copy.354, f32[3,5,2,96,192]{3,2,1,0,4:T(2,128)S(1)} %copy-done.1, f32[3,5,2,6,192]{3,2,1,0,4:T(2,128)} %copy.353, f32[3,5,2,108,6]{3,2,1,0,4:T(2,128)} %collective-permute-done.18), kind=kLoop, calls=%fused_computation.47 | loop fusion | flops 2643840 | bytes 5287680 | tf_op jit(solution)/shard_map/concatenate | solution.py:17
  667.6 18.0 %while.35 = (s32[]{:T(128)}, f32[3,5,2,108,204]{3,2,1,0,4:T(2,128)}, s32[3,5]{1,0:T(4,128)}, f32[3,5,2,96,192]{3,2,1,0,4:T(2,128)S(1)}, s32[]{:T(128)}) while((s32[]{:T(128)}, f32[3,5,2,108,204]{3,2,1,0,4:T(2,128)}, s32[3,5]{1,0:T(4,128)}, f32[3,5,2,96,192]{3,2,1,0,4:T(2,128)S(1)}, s32[]{:T(128)}) %tuple.221), condition=%wide.while_cond.1, body=%wide.while_body.1.sunk | while | flops 2 | bytes 1720473 | solution.py:132
  668.9 4.6 dynamic-slice_dynamic-update-slice_fusion.2
  674.9 4.6 dynamic-slice_dynamic-update-slice_fusion.2
  680.9 4.7 dynamic-slice_dynamic-update-slice_fusion.2
  687.2 9.3 %multiply_add_fusion.1 = f32[3,5,2,96,192]{3,2,1,0,4:T(2,128)S(1)} fusion(f32[3,5,2,96,192]{3,2,1,0,4:T(2,128)} %copy-done.7, pred[3,96,192]{1,0,2:T(4,128)(4,1)S(1)} %broadcast_and_fusion.1, f32[96,3,5,2,192]{0,3,2,1,4:T(2,128)} %copy.368, pred[192]{0:T(512)(128)(4,1)S(1)} %copy-done.19, f32[96,3,5,2,192]{0,3,2,1,4:T(2,128)} %copy.365, ...), kind=kLoop, calls=%fused_computation.95 | loop fusion | flops 6635520 | bytes 13400928 | tf_op jit(solution)/shard_map/add | solution.py:177
  696.5 6.6 fusion.54
  730.0 8.5 %select_maximum_fusion = f32[3,5,4,98,194]{3,2,1,0,4:T(4,128)S(1)} fusion(f32[3,5,2,98,1]{3,2,1,0,4:T(2,128)S(1)} %collective-permute-done.22, f32[3,5,2,98,1]{3,2,1,0,4:T(2,128)S(1)} %collective-permute-done.23, f32[3,5,2,1,192]{3,2,1,0,4:T(2,128)S(1)} %copy-done.3, f32[3,5,2,96,192]{3,2,1,0,4:T(2,128)S(1)} %multiply_add_fusion.1, ...), kind=kLoop, calls=%fused_computation.37 | loop fusion | flops 13688640 | bytes 6844320 | tf_op jit(solution)/shard_map/concatenate | solution.py:17
  738.4 38.3 %multiply_add_fusion = f32[3,5,2,96,192]{3,2,1,0,4:T(2,128)} fusion(f32[3,5,2,96,192]{3,2,1,0,4:T(2,128)S(1)} %multiply_add_fusion.1, f32[3,5,4,98,194]{3,2,1,0,4:T(4,128)S(1)} %select_maximum_fusion, f32[3,5,2,1,192]{3,2,1,0,4:T(2,128)S(1)} %copy-done.3, f32[3,5,2,1,192]{3,2,1,0,4:T(2,128)S(1)} %copy-done.5, ...), kind=kLoop, calls=%fused_computation.94 | loop fusion | flops 11612160 | bytes 8990728 | tf_op jit(solution)/shard_map/add | solution.py:181
  776.7 5.5 copy.376
  (360 shorter events, 247.6 us)
Async XLA Ops:
  7.2 32.1 %copy-start.8 = (f32[5,2,64,128]{3,2,1,0:T(8,128)S(1)}, f32[5,2,64,128]{3,2,1,0:T(8,128)}, u32[]{:S(2)}) copy-start(f32[5,2,64,128]{3,2,1,0:T(8,128)} %param.18) | copy-start | bytes 983044
  7.2 271.7 %all-reduce.9.cloned.1.call-start = ((), (), s32[]{:S(2)}) async-start(), calls=%async_computation | async-start | bytes 983040 | tf_op jit(solution)/shard_map/psum | solution.py:157
  8.1 24.3 %collective-permute-start = (f32[5,2,1,128]{3,2,1,0:T(1,128)S(1)}, f32[5,2,1,128]{3,2,1,0:T(1,128)S(1)}, u32[]{:S(2)}, u32[]{:S(2)}) collective-permute-start(f32[5,2,1,128]{3,2,1,0:T(1,128)S(1)} %get-tuple-element.438), channel_id=1, source_target_pairs={{4,0},{8,4},{12,8},{5,1},{9,5},{13,9},{6,2},{10,6},{14,10},{7,3},{... | collective-permute-start | bytes 15368 | tf_op jit(solution)/shard_map/ppermute | solution.py:21
  10.4 22.0 %collective-permute-start.1 = (f32[5,2,1,128]{3,2,1,0:T(1,128)S(1)}, f32[5,2,1,128]{3,2,1,0:T(1,128)S(1)}, u32[]{:S(2)}, u32[]{:S(2)}) collective-permute-start(f32[5,2,1,128]{3,2,1,0:T(1,128)S(1)} %get-tuple-element.437), channel_id=1, source_target_pairs={{0,4},{4,8},{8,12},{1,5},{5,9},{9,13},{2,6},{6,10},{10,14},{3,7},{... | collective-permute-start | bytes 15368 | tf_op jit(solution)/shard_map/ppermute | solution.py:19
  15.1 24.5 %copy-start.14 = (f32[5]{0:T(128)S(1)}, f32[5]{0:T(128)}, u32[]{:S(2)}) copy-start(f32[5]{0:T(128)} %param.21) | copy-start | bytes 64
  15.2 24.5 %copy-start.15 = (f32[5]{0:T(128)S(1)}, f32[5]{0:T(128)}, u32[]{:S(2)}) copy-start(f32[5]{0:T(128)} %param.20) | copy-start | bytes 64
  15.2 104.0 %collective-permute-start.9 = (f32[3,5,2,6,192]{4,2,3,1,0:T(2,128)S(1)}, f32[3,5,2,6,192]{4,2,3,1,0:T(2,128)}, u32[]{:S(2)}, u32[]{:S(2)}) collective-permute-start(f32[3,5,2,6,192]{4,2,3,1,0:T(2,128)S(1)} %copy.384), channel_id=1, source_target_pairs={{4,0},{8,4},{12,8},{5,1},{9,5},{13,9},{6,2},{10,6},{14,10},{7,3},{... | collective-permute-start | bytes 414728 | tf_op jit(solution)/shard_map/ppermute | solution.py:21
  18.3 105.1 %collective-permute-start.8 = (f32[3,5,2,6,192]{4,2,3,1,0:T(2,128)}, f32[3,5,2,6,192]{4,2,3,1,0:T(2,128)}, u32[]{:S(2)}, u32[]{:S(2)}) collective-permute-start(f32[3,5,2,6,192]{4,2,3,1,0:T(2,128)} %copy.383), channel_id=1, source_target_pairs={{0,4},{4,8},{8,12},{1,5},{5,9},{9,13},{2,6},{6,10},{10,14},{3,7},{... | collective-permute-start | bytes 414728 | tf_op jit(solution)/shard_map/ppermute | solution.py:19
  24.9 15.3 %copy-start.28 = (s32[96]{0:T(128)}, s32[96]{0:T(128)S(1)}, u32[]{:S(2)}) copy-start(s32[96]{0:T(128)S(1)} %get-tuple-element.495) | copy-start | bytes 1156
  33.6 4.4 collective-permute-start.2
  34.9 4.3 collective-permute-start.3
  38.0 405.0 %copy-start.24 = (pred[192]{0:T(512)(128)(4,1)}, pred[192]{0:T(512)(128)(4,1)S(1)}, u32[]{:S(2)}) copy-start(pred[192]{0:T(512)(128)(4,1)S(1)} %broadcast_compare_fusion.1) | copy-start | bytes 580
  40.3 14.7 %collective-permute-start.4 = (f32[5,2,1,128]{3,2,1,0:T(1,128)S(1)}, f32[5,2,1,128]{3,2,1,0:T(1,128)S(1)}, u32[]{:S(2)}, u32[]{:S(2)}) collective-permute-start(f32[5,2,1,128]{3,2,1,0:T(1,128)S(1)} %get-tuple-element.436), channel_id=1, source_target_pairs={{4,0},{8,4},{12,8},{5,1},{9,5},{13,9},{6,2},{10,6},{14,10},{7,3},{... | collective-permute-start | bytes 15368 | tf_op jit(solution)/shard_map/ppermute | solution.py:21
  42.2 12.8 %collective-permute-start.5 = (f32[5,2,1,128]{3,2,1,0:T(1,128)S(1)}, f32[5,2,1,128]{3,2,1,0:T(1,128)S(1)}, u32[]{:S(2)}, u32[]{:S(2)}) collective-permute-start(f32[5,2,1,128]{3,2,1,0:T(1,128)S(1)} %get-tuple-element.435), channel_id=1, source_target_pairs={{0,4},{4,8},{8,12},{1,5},{5,9},{9,13},{2,6},{6,10},{10,14},{3,7},{... | collective-permute-start | bytes 15368 | tf_op jit(solution)/shard_map/ppermute | solution.py:19
  46.2 396.8 %copy-start.26 = (pred[96]{0:T(512)(128)(4,1)}, pred[96]{0:T(512)(128)(4,1)S(1)}, u32[]{:S(2)}) copy-start(pred[96]{0:T(512)(128)(4,1)S(1)} %broadcast_compare_fusion.3) | copy-start | bytes 292
  55.9 58.4 %collective-permute-start.6 = (f32[5,2,66,1]{3,2,1,0:T(8,128)}, f32[5,2,66,1]{3,2,1,0:T(8,128)S(1)}, u32[]{:S(2)}, u32[]{:S(2)}) collective-permute-start(f32[5,2,66,1]{3,2,1,0:T(8,128)} %get-tuple-element.432), channel_id=1, source_target_pairs={{1,0},{2,1},{3,2},{5,4},{6,5},{7,6},{9,8},{10,9},{11,10},{13,12},{... | collective-permute-start | bytes 7928 | tf_op jit(solution)/shard_map/ppermute | solution.py:21
  57.2 57.1 %collective-permute-start.7 = (f32[5,2,66,1]{3,2,1,0:T(8,128)S(1)}, f32[5,2,66,1]{3,2,1,0:T(8,128)S(1)}, u32[]{:S(2)}, u32[]{:S(2)}) collective-permute-start(f32[5,2,66,1]{3,2,1,0:T(8,128)S(1)} %get-tuple-element.431), channel_id=1, source_target_pairs={{0,1},{1,2},{2,3},{4,5},{5,6},{6,7},{8,9},{9,10},{10,11},{12,13},{... | collective-permute-start | bytes 7928 | tf_op jit(solution)/shard_map/ppermute | solution.py:19
  119.2 8.2 %copy-start.6 = (f32[3,5,2,96,192]{3,2,4,1,0:T(2,128)S(1)}, f32[3,5,2,96,192]{3,2,4,1,0:T(2,128)}, u32[]{:S(2)}) copy-start(f32[3,5,2,96,192]{3,2,4,1,0:T(2,128)} %copy.328) | copy-start | bytes 6635524
  129.5 58.6 %collective-permute-start.11 = (f32[3,5,2,108,6]{3,2,4,1,0:T(2,128)}, f32[3,5,2,108,6]{3,2,4,1,0:T(2,128)S(1)}, u32[]{:S(2)}, u32[]{:S(2)}) collective-permute-start(f32[3,5,2,108,6]{3,2,4,1,0:T(2,128)} %get-tuple-element.422), channel_id=1, source_target_pairs={{1,0},{3,2},{5,4},{7,6},{9,8},{11,10},{13,12},{15,14},{17,16},{19,... | collective-permute-start | bytes 233288 | tf_op jit(solution)/shard_map/ppermute | solution.py:21
  130.8 57.3 %collective-permute-start.10 = (f32[3,5,2,108,6]{3,2,4,1,0:T(2,128)S(1)}, f32[3,5,2,108,6]{3,2,4,1,0:T(2,128)}, u32[]{:S(2)}, u32[]{:S(2)}) collective-permute-start(f32[3,5,2,108,6]{3,2,4,1,0:T(2,128)S(1)} %get-tuple-element.421), channel_id=1, source_target_pairs={{0,1},{2,3},{4,5},{6,7},{8,9},{10,11},{12,13},{14,15},{16,17},{18,... | collective-permute-start | bytes 233288 | tf_op jit(solution)/shard_map/ppermute | solution.py:19
  292.5 11.2 %copy-start.34 = (pred[192]{0:T(512)(128)(4,1)S(1)}, pred[192]{0:T(512)(128)(4,1)}, u32[]{:S(2)}) copy-start(pred[192]{0:T(512)(128)(4,1)} %get-tuple-element.490) | copy-start | bytes 580
  346.7 10.6 %copy-start.33 = (pred[192]{0:T(512)(128)(4,1)S(1)}, pred[192]{0:T(512)(128)(4,1)}, u32[]{:S(2)}) copy-start(pred[192]{0:T(512)(128)(4,1)} %get-tuple-element.491) | copy-start | bytes 580
  428.9 14.0 %copy-start.12 = (f32[96,192]{0,1:T(8,128)S(1)}, f32[96,192]{0,1:T(8,128)}, u32[]{:S(2)}) copy-start(f32[96,192]{0,1:T(8,128)} %fusion.42) | copy-start | bytes 221188
  429.0 14.0 %copy-start.13 = (pred[3,96,192]{1,0,2:T(4,128)(4,1)S(1)}, pred[3,96,192]{1,0,2:T(4,128)(4,1)}, u32[]{:S(2)}) copy-start(pred[3,96,192]{1,0,2:T(4,128)(4,1)} %broadcast_and_fusion) | copy-start | bytes 165892
  429.0 14.0 %copy-start.16 = (pred[192]{0:T(512)(128)(4,1)S(1)}, pred[192]{0:T(512)(128)(4,1)}, u32[]{:S(2)}) copy-start(pred[192]{0:T(512)(128)(4,1)} %get-tuple-element.492) | copy-start | bytes 580
  429.0 14.0 %copy-start.18 = (pred[192]{0:T(512)(128)(4,1)S(1)}, pred[192]{0:T(512)(128)(4,1)}, u32[]{:S(2)}) copy-start(pred[192]{0:T(512)(128)(4,1)} %get-tuple-element.493) | copy-start | bytes 580
  429.0 14.0 %copy-start.20 = (pred[96]{0:T(512)(128)(4,1)S(1)}, pred[96]{0:T(512)(128)(4,1)}, u32[]{:S(2)}) copy-start(pred[96]{0:T(512)(128)(4,1)} %get-tuple-element.476) | copy-start | bytes 292
  429.0 14.0 %copy-start.22 = (pred[96]{0:T(512)(128)(4,1)S(1)}, pred[96]{0:T(512)(128)(4,1)}, u32[]{:S(2)}) copy-start(pred[96]{0:T(512)(128)(4,1)} %get-tuple-element.479) | copy-start | bytes 292
  463.0 9.9 %collective-permute-start.12 = (f32[3,5,2,1,192]{4,2,3,1,0:T(2,128)S(1)}, f32[3,5,2,1,192]{4,2,3,1,0:T(2,128)S(1)}, u32[]{:S(2)}, u32[]{:S(2)}) collective-permute-start(f32[3,5,2,1,192]{4,2,3,1,0:T(2,128)S(1)} %copy.345), channel_id=1, source_target_pairs={{4,0},{8,4},{12,8},{5,1},{9,5},{13,9},{6,2},{10,6},{14,10},{7,3},{... | collective-permute-start | bytes 69128 | tf_op jit(solution)/shard_map/ppermute | solution.py:21
  470.4 5.8 collective-permute-start.13
  480.7 4.6 collective-permute-start.14
  482.1 3.9 collective-permute-start.15
  541.5 10.0 %collective-permute-start.17 = (f32[3,5,2,6,192]{4,2,3,1,0:T(2,128)S(1)}, f32[3,5,2,6,192]{4,2,3,1,0:T(2,128)S(1)}, u32[]{:S(2)}, u32[]{:S(2)}) collective-permute-start(f32[3,5,2,6,192]{4,2,3,1,0:T(2,128)S(1)} %copy.352), channel_id=1, source_target_pairs={{4,0},{8,4},{12,8},{5,1},{9,5},{13,9},{6,2},{10,6},{14,10},{7,3},{... | collective-permute-start | bytes 414728 | tf_op jit(solution)/shard_map/ppermute | solution.py:21
  548.2 8.8 %collective-permute-start.16 = (f32[3,5,2,6,192]{4,2,3,1,0:T(2,128)}, f32[3,5,2,6,192]{4,2,3,1,0:T(2,128)}, u32[]{:S(2)}, u32[]{:S(2)}) collective-permute-start(f32[3,5,2,6,192]{4,2,3,1,0:T(2,128)} %copy.351), channel_id=1, source_target_pairs={{0,4},{4,8},{8,12},{1,5},{5,9},{9,13},{2,6},{6,10},{10,14},{3,7},{... | collective-permute-start | bytes 414728 | tf_op jit(solution)/shard_map/ppermute | solution.py:19
  551.5 9.8 %copy-start.1 = (f32[3,5,2,96,192]{3,2,1,0,4:T(2,128)S(1)}, f32[3,5,2,96,192]{3,2,1,0,4:T(2,128)}, u32[]{:S(2)}) copy-start(f32[3,5,2,96,192]{3,2,1,0,4:T(2,128)} %copy-done) | copy-start | bytes 6635524
  561.3 7.1 copy-start.30
  563.4 94.1 %collective-permute-start.19 = (f32[3,5,2,108,6]{3,2,1,0,4:T(2,128)}, f32[3,5,2,108,6]{3,2,1,0,4:T(2,128)S(1)}, u32[]{:S(2)}, u32[]{:S(2)}) collective-permute-start(f32[3,5,2,108,6]{3,2,1,0,4:T(2,128)} %get-tuple-element.418), channel_id=1, source_target_pairs={{1,0},{3,2},{5,4},{7,6},{9,8},{11,10},{13,12},{15,14},{17,16},{19,... | collective-permute-start | bytes 233288 | tf_op jit(solution)/shard_map/ppermute | solution.py:21
  564.7 92.8 %collective-permute-start.18 = (f32[3,5,2,108,6]{3,2,1,0,4:T(2,128)S(1)}, f32[3,5,2,108,6]{3,2,1,0,4:T(2,128)}, u32[]{:S(2)}, u32[]{:S(2)}) collective-permute-start(f32[3,5,2,108,6]{3,2,1,0,4:T(2,128)S(1)} %get-tuple-element.417), channel_id=1, source_target_pairs={{0,1},{2,3},{4,5},{6,7},{8,9},{10,11},{12,13},{14,15},{16,17},{18,... | collective-permute-start | bytes 233288 | tf_op jit(solution)/shard_map/ppermute | solution.py:19
  667.5 19.6 %copy-start.17 = (pred[192]{0:T(512)(128)(4,1)S(1)}, pred[192]{0:T(512)(128)(4,1)}, u32[]{:S(2)}) copy-start(pred[192]{0:T(512)(128)(4,1)} %get-tuple-element.492) | copy-start | bytes 580
  667.5 19.6 %copy-start.19 = (pred[192]{0:T(512)(128)(4,1)S(1)}, pred[192]{0:T(512)(128)(4,1)}, u32[]{:S(2)}) copy-start(pred[192]{0:T(512)(128)(4,1)} %get-tuple-element.493) | copy-start | bytes 580
  667.5 19.6 %copy-start.21 = (pred[96]{0:T(512)(128)(4,1)S(1)}, pred[96]{0:T(512)(128)(4,1)}, u32[]{:S(2)}) copy-start(pred[96]{0:T(512)(128)(4,1)} %get-tuple-element.476) | copy-start | bytes 292
  667.6 19.6 %copy-start.23 = (pred[96]{0:T(512)(128)(4,1)S(1)}, pred[96]{0:T(512)(128)(4,1)}, u32[]{:S(2)}) copy-start(pred[96]{0:T(512)(128)(4,1)} %get-tuple-element.479) | copy-start | bytes 292
  667.6 19.6 %copy-start.25 = (pred[192]{0:T(512)(128)(4,1)S(1)}, pred[192]{0:T(512)(128)(4,1)}, u32[]{:S(2)}) copy-start(pred[192]{0:T(512)(128)(4,1)} %copy-done.24) | copy-start | bytes 580
  667.6 19.6 %copy-start.27 = (pred[96]{0:T(512)(128)(4,1)S(1)}, pred[96]{0:T(512)(128)(4,1)}, u32[]{:S(2)}) copy-start(pred[96]{0:T(512)(128)(4,1)} %copy-done.26) | copy-start | bytes 292
  707.1 9.9 %collective-permute-start.20 = (f32[3,5,2,1,192]{4,2,3,1,0:T(2,128)S(1)}, f32[3,5,2,1,192]{4,2,3,1,0:T(2,128)S(1)}, u32[]{:S(2)}, u32[]{:S(2)}) collective-permute-start(f32[3,5,2,1,192]{4,2,3,1,0:T(2,128)S(1)} %copy.370), channel_id=1, source_target_pairs={{4,0},{8,4},{12,8},{5,1},{9,5},{13,9},{6,2},{10,6},{14,10},{7,3},{... | collective-permute-start | bytes 69128 | tf_op jit(solution)/shard_map/ppermute | solution.py:21
  713.6 6.6 collective-permute-start.21
  724.7 4.5 collective-permute-start.22
  726.1 3.9 collective-permute-start.23
  (12 other events, 56.0 us)
Sparse Core Ops, SparseCore 0:
  188.2 90.5 all-reduce.8
where the time goes:
time: 802 us; the launch traced here: 790 us
  local copies, waits for them, and re-layouts  418 us (52%)
  other arithmetic  168 us (21%)
  waiting for transfers between devices  71.8 us (9%)
  starting transfers between devices  68.8 us (9%)
  loops' own time  46.6 us (6%)
  between operations  15.6 us (2%)
    add x2, other arithmetic, per_device(): nests_now = relaxed + inside * change  75.6 us
    gather x8, local copies, waits for them, and re-layouts, along(): picked = jnp.take(picked, coarse_rows, axis=4)  68.9 us
    psum x1, waiting for transfers between devices, per_device(): totals = lax.psum(terms, ('tile', 'nest', 'lev'))  66.8 us
    gather x4, local copies, waits for them, and re-layouts, across(): return jnp.take(picked, coarse_cols, axis=4)  53.6 us
    another operation x2, loops' own time, extract(): return lax.map(single, corners)  46.6 us
    gather x4, local copies, waits for them, and re-layouts, along(): picked = jnp.take(zone, zone_index, axis=3)  46.1 us
    ppermute x12, starting transfers between devices, extended(): lax.ppermute(tail, axis, [(i, (i + 1) % count) for i in range(ends)])  44.9 us
    concatenate x10, other arithmetic, extended(): jnp.concatenate([lax.ppermute(tail, axis, [(i, (i + 1) % count) for i in...  38.6 us
  transfers between devices with their start and end apart: 25, of which 5 were waited for; matrix products, arithmetic and copies ran while one was open for 28% of the time, Pallas kernels for 0%

commit v1 on v0

v1 whole, which is shorter than its diff:
```python
import jax
import jax.numpy as jnp
from jax import lax
from jax.experimental import pallas as pl
from jax.experimental.pallas import tpu as pltpu
from jax.sharding import PartitionSpec as P

FP = 128
BWP = 2
MOVE = 2
STEPS = 2
BORDER = 3 * BWP
SPAN = 3 * FP
HALO = STEPS * (3 * MOVE + 1)
PAD = 16
LANES = 128
RING = STEPS
ROW_AT = 32
ZONE_AT = 72
SPLIT = -(FP // 4)
VMEM_LIMIT = 40 * 1024 * 1024

SMEM_SPEC = pl.BlockSpec(memory_space=pltpu.SMEM)
VMEM_SPEC = pl.BlockSpec(memory_space=pltpu.VMEM)


def params(**more):
    return pltpu.CompilerParams(vmem_limit_bytes=VMEM_LIMIT, **more)


def lane_iota(rows=1, lanes=LANES):
    return lax.broadcasted_iota(jnp.int32, (rows, lanes), 1)


def row_iota(rows, lanes=LANES):
    return lax.broadcasted_iota(jnp.int32, (rows, lanes), 0)


def beside(x, first_lane, last_lane):
    left = [pltpu.roll(v, 1, 1) for v in x]
    right = [pltpu.roll(v, LANES - 1, 1) for v in x]
    return [
        jnp.where(first_lane, left[1 - a], left[a]) + jnp.where(last_lane, right[1 - a], right[a])
        for a in range(2)
    ]


def third(values):
    return (values * 21846) >> 16


def strips_kernel(
    fields, rows, cols, storms, centres, slots, lateral, vertical, parent,
    send, keep, ring_out, plain0, plain1, plain2, turned0, turned1, turned2, block, gather,
):
    planes = 2 * fields
    tile_at, tiles = lax.axis_index("tile"), lax.axis_size("tile")
    lev_at, levs = lax.axis_index("lev"), lax.axis_size("lev")
    col_at = lax.axis_index("nest") * levs + lev_at
    col_blocks = lax.axis_size("nest") * levs
    top = 8
    height = rows + 16
    width = cols + 16

    lane = lane_iota()
    first_lane, last_lane = lane == 0, lane == LANES - 1
    row = tile_at * rows + row_iota(height) - top
    tile_cols = (lane, jnp.where(lane < LANES // 2, lane + LANES, lane - LANES))
    within = [
        (
            (row >= 0) & (row < tiles * rows)
            & (col_at * cols + c >= 0) & (col_at * cols + c < col_blocks * cols)
        ).astype(jnp.float32)
        for c in tile_cols
    ]
    plain0[...] = jnp.zeros_like(plain0)
    turned0[...] = jnp.zeros_like(turned0)
    block[...] = jnp.zeros_like(block)
    for p in range(planes):
        plain0[p, 0, top : top + rows, :] = parent[p // 2, p % 2]
        block[ROW_AT : ROW_AT + rows, :] = parent[p // 2, p % 2]
        turned0[p, top : top + cols, :] = block[...].T

    inner = slice(1, height - 1)

    def plain_step(source, target, mask):
        for f in range(fields):
            lat, ver = lateral[f], vertical[f]
            for v in range(2):
                x = [source[2 * f + v, a, inner, :] for a in range(2)]
                sideways = beside(x, first_lane, last_lane)
                for a in range(2):
                    near = (
                        sideways[a]
                        + source[2 * f + v, a, 2:height, :]
                        + source[2 * f + v, a, 0 : height - 2, :]
                    )
                    other = source[2 * f + 1 - v, a, inner, :]
                    new = x[a] + lat * (near - 4.0 * x[a]) + ver * (other - 2.0 * x[a])
                    if mask is not None:
                        new = new * mask[a][inner, :]
                    target[2 * f + v, a, inner, :] = new
                    for edge in (0, height - 1):
                        target[2 * f + v, a, edge : edge + 1, :] = jnp.zeros(
                            (1, LANES), jnp.float32
                        )

    plain_step(plain0, plain1, within)
    plain_step(plain1, plain2, None)

    row_t = tile_at * rows + lane_iota() - ROW_AT
    col_t = col_at * cols + row_iota(width) - top
    within_t = (
        (row_t >= 0) & (row_t < tiles * rows) & (col_t >= 0) & (col_t < col_blocks * cols)
    ).astype(jnp.float32)

    def turned_step(source, target, mask):
        for f in range(fields):
            lat, ver = lateral[f], vertical[f]
            for v in range(2):
                x = source[2 * f + v, 1 : width - 1, :]
                near = (
                    source[2 * f + v, 2:width, :]
                    + source[2 * f + v, 0 : width - 2, :]
                    + pltpu.roll(x, 1, 1)
                    + pltpu.roll(x, LANES - 1, 1)
                )
                other = source[2 * f + 1 - v, 1 : width - 1, :]
                new = x + lat * (near - 4.0 * x) + ver * (other - 2.0 * x)
                if mask is not None:
                    new = new * mask[1 : width - 1, :]
                target[2 * f + v, 1 : width - 1, :] = new
                target[2 * f + v, 0:1, :] = jnp.zeros((1, LANES), jnp.float32)
                target[2 * f + v, width - 1 : width, :] = jnp.zeros((1, LANES), jnp.float32)

    turned_step(turned0, turned1, within_t)
    turned_step(turned1, turned2, None)

    share = storms * STEPS * planes * BWP
    for j in range(storms):
        storm = slots[j]
        for s in range(STEPS):
            at = (j * STEPS + s) * planes * BWP
            corner_row = centres[s + 1, storm, 0] - FP // 2 - tile_at * rows
            corner_col = centres[s + 1, storm, 1] - FP // 2 - col_at * cols
            plain = (plain1, plain2)[s]
            turned = (turned1, turned2)[s]
            first = jnp.where(corner_row >= SPLIT, corner_row, corner_row + FP - BWP)
            first = jnp.clip(first + top, 0, height - BWP)
            for p in range(planes):
                for a in range(2):
                    gather[a, BWP * p : BWP * (p + 1), :] = plain[p, a, pl.ds(first, BWP), :]
            shift = (64 * LANES - corner_col) % LANES
            window = [pltpu.roll(gather[a], shift, 1) for a in range(2)]
            place = lane + corner_col
            main = (place >= 0) & (place < cols)
            rim = (place >= -RING) & (place < cols + RING)
            window = jnp.where(main, window[0], jnp.where(rim, window[1], 0.0))[: planes * BWP]
            send[at : at + planes * BWP, :] = window
            keep[at : at + planes * BWP, :] = window
            mine = corner_col + (FP - BWP) * lev_at
            theirs = corner_col + (FP - BWP) * (levs - 1 - lev_at)
            for target, start in ((keep, mine), (send, theirs)):
                start = jnp.clip(start + top, 0, width - BWP)
                for p in range(planes):
                    target[share + at + BWP * p : share + at + BWP * (p + 1), :] = turned[
                        p, pl.ds(start, BWP), :
                    ]
    for p in range(planes):
        send[2 * share + BWP * p : 2 * share + BWP * (p + 1), :] = turned2[p, top - RING : top, :]
        at = 2 * share + planes * BWP + BWP * p
        send[at : at + BWP, :] = turned2[p, top + cols : top + cols + RING, :]
        ring_out[p] = turned2[p, top : top + cols, :]


def pair_up_kernel(own, share, rim, keep, got, kept, *sends):
    nest_at = lax.axis_index("nest")
    lev_at = lax.axis_index("lev")
    for k in range(len(sends) + 1):
        group = lax.bitwise_xor(nest_at, k)
        target = kept if k == 0 else sends[k - 1]
        for part in range(2):
            rows = pl.ds(pl.multiple_of(part * share + group * own, 8), own)
            target[part * own : (part + 1) * own, :] = keep[rows, :] + got[rows, :]
        if k > 0:
            west = got[2 * share : 2 * share + rim, :]
            east = got[2 * share + rim : 2 * share + 2 * rim, :]
            target[2 * own : 2 * own + rim, :] = jnp.where(lev_at == 0, east, west)


def aim_kernel(
    fields, rows, cols, strip_rows, strip_cols, slot_count, moves, share, touching,
    centres, slots, ring, first_got, kept, *refs,
):
    crossing = lax.axis_size("nest") - 1
    nest_gots, rest = refs[:crossing], refs[crossing:]
    partial, zone_self, zone_sends, total = rest[0], rest[1], rest[2:-1], rest[-1]
    planes = 2 * fields
    rim = planes * BWP
    own = slot_count * STEPS * rim
    tile_at, tiles = lax.axis_index("tile"), lax.axis_size("tile")
    nest_at = lax.axis_index("nest")
    lev_at = lax.axis_index("lev")

    sums = kept[...]
    for got in nest_gots:
        sums = sums + got[0 : 2 * own, :]
    total[...] = sums

    lane = lane_iota()
    col_base = lev_at * (strip_cols // 3 - 3)
    for j in range(slot_count):
        storm = slots[nest_at * slot_count + j]
        at = j * STEPS * rim
        both = STEPS * rim
        strip = pltpu.roll(total[at : at + both, :], (LANES - col_base) % LANES, 1)
        side = total[own + at : own + at + both, :]
        second = row_iota(both) >= rim
        origins = [centres[s + 1, storm, 0] - FP // 2 - tile_at * rows for s in range(STEPS)]
        for k in moves:
            dest = lax.bitwise_xor(tile_at, k)
            parts = []
            for s in range(STEPS):
                south = origins[s] >= SPLIT
                wanted = ((dest == 0) & south) | ((dest == tiles - 1) & jnp.logical_not(south))
                offset = ROW_AT + origins[s] + (strip_rows // 3) * dest - 3 - ZONE_AT
                source = lane + offset
                fits = (source >= ROW_AT - RING) & (source < ROW_AT + rows + RING)
                turned = pltpu.roll(side, (64 * LANES - offset) % LANES, 1)
                turned = jnp.where(fits, turned, 0.0)
                parts.append(
                    jnp.where(lane < ZONE_AT, strip * wanted.astype(jnp.float32), turned)
                )
            target = zone_self if k == 0 else zone_sends[moves.index(k) - 1]
            target[at : at + both, :] = jnp.where(second, parts[1], parts[0])

    from_west = first_got[2 * share + rim : 2 * share + 2 * rim, :]
    from_east = first_got[2 * share : 2 * share + rim, :]
    far_west = jnp.zeros((rim, LANES), jnp.float32)
    far_east = jnp.zeros((rim, LANES), jnp.float32)
    for i, got in enumerate(nest_gots):
        other = lax.bitwise_xor(nest_at, i + 1)
        edge = got[2 * own : 2 * own + rim, :]
        far_west = far_west + jnp.where(other == nest_at - 1, edge, 0.0)
        far_east = far_east + jnp.where(other == nest_at + 1, edge, 0.0)
    from_west = jnp.where(lev_at == 0, far_west, from_west)
    from_east = jnp.where(lev_at == 0, from_east, far_east)
    for p in range(planes):
        two = slice(BWP * p, BWP * (p + 1))
        total[0:cols, :] = ring[p]
        total[0:RING, :] = total[0:RING, :] + from_west[two]
        total[cols - RING : cols, :] = total[cols - RING : cols, :] + from_east[two]
        total[0:LANES, :] = total[0:cols, :].T
        partial[p // 2, p % 2] = total[ROW_AT : ROW_AT + rows, :]
        below = total[ROW_AT - RING : ROW_AT, :]
        above = total[ROW_AT + rows : ROW_AT + rows + RING, :]
        for i, k in enumerate(moves[1:]):
            if k in touching:
                dest = lax.bitwise_xor(tile_at, k)
                zone_sends[i][own + BWP * p : own + BWP * (p + 1), :] = jnp.where(
                    dest > tile_at, above, below
                )


def edge_rows_kernel(fields, strip_rows, nests, to_pair, to_cross):
    even = lax.rem(lax.axis_index("tile"), 2) == 0
    for f in range(fields):
        for v in range(2):
            low = nests[0, f, v, 0:HALO, 0:LANES]
            high = nests[0, f, v, strip_rows - HALO : strip_rows, 0:LANES]
            at = (2 * f + v) * HALO
            to_pair[0, at : at + HALO, :] = jnp.where(even, high, low)
            to_cross[0, at : at + HALO, :] = jnp.where(even, low, high)
        half = nests.shape[4] - LANES
        low = jnp.concatenate([nests[0, f, v, 0:HALO, LANES : LANES + half] for v in range(2)], 1)
        high = jnp.concatenate(
            [nests[0, f, v, strip_rows - HALO : strip_rows, LANES : LANES + half] for v in range(2)],
            1,
        )
        at = (2 * fields + f) * HALO
        to_pair[0, at : at + HALO, :] = jnp.where(even, high, low)
        to_cross[0, at : at + HALO, :] = jnp.where(even, low, high)


def edge_cols_kernel(fields, strip_rows, slot_count, nests, pair, cross, packed, wide):
    even = lax.rem(lax.axis_index("tile"), 2) == 0
    west_most = lax.axis_index("lev") == 0
    planes = 2 * fields
    half = nests.shape[4] - LANES
    packed[...] = jnp.zeros_like(packed)
    wide[...] = jnp.zeros_like(wide)
    lane = lane_iota()
    for q in range(slot_count * planes):
        j, f, v = q // planes, (q % planes) // 2, q % 2
        spot = (q % 8) * 16
        mask = (lane >= spot) & (lane < spot + HALO)
        wide[:, 0:half] = nests[j, f, v, :, LANES : LANES + half]
        cells = jnp.where(west_most, wide[...], nests[j, f, v, :, 0:LANES])
        shift = jnp.where(west_most, spot + 2 * LANES - (half - HALO), spot + 2 * LANES) % LANES
        cells = pltpu.roll(cells, shift, 1)
        rows = slice(PAD, PAD + strip_rows)
        packed[q // 8, rows, :] = jnp.where(mask, cells, packed[q // 8, rows, :])
        at, rest = (2 * f + v) * HALO, (2 * fields + f) * HALO
        shift = (
            jnp.where(west_most, spot + 2 * LANES - (half - HALO) - half * v, spot + 2 * LANES) % LANES
        )
        halos = []
        for got in (pair, cross):
            cells = jnp.where(west_most, got[j, rest : rest + HALO, :], got[j, at : at + HALO, :])
            halos.append(pltpu.roll(cells, shift, 1))
        high = jnp.where(even, halos[0], halos[1])
        low = jnp.where(even, halos[1], halos[0])
        rows = slice(PAD - HALO, PAD)
        packed[q // 8, rows, :] = jnp.where(mask, low, packed[q // 8, rows, :])
        rows = slice(PAD + strip_rows, PAD + strip_rows + HALO)
        packed[q // 8, rows, :] = jnp.where(mask, high, packed[q // 8, rows, :])


def nests_kernel(
    fields, strip_rows, strip_cols, rows, moves, touching,
    centres, slots, lateral, vertical, nests, pair, cross, packed, partial, zone_self, *refs,
):
    count = len(moves) - 1
    zone_gots = refs[:count]
    nest_out, parent_out = refs[count : count + 2]
    cells, mixed, weight, inner, strips, sides = refs[count + 2 :]
    planes = 2 * fields
    rim = planes * BWP
    both = STEPS * rim
    half = strip_cols - LANES
    height = strip_rows + 2 * PAD
    tile_at, tiles = lax.axis_index("tile"), lax.axis_size("tile")
    nest_at = lax.axis_index("nest")
    lev_at = lax.axis_index("lev")
    even = lax.rem(tile_at, 2) == 0
    j = pl.program_id(0)
    own = pl.num_programs(0) * both

    @pl.when(j == 0)
    def _():
        below = jnp.zeros((rim, LANES), jnp.float32)
        above = jnp.zeros((rim, LANES), jnp.float32)
        for i, k in enumerate(moves[1:]):
            if k in touching:
                other = lax.bitwise_xor(tile_at, k)
                edge = zone_gots[i][zone_self.shape[0] : zone_self.shape[0] + rim, :]
                below = below + jnp.where(other == tile_at - 1, edge, 0.0)
                above = above + jnp.where(other == tile_at + 1, edge, 0.0)
        for p in range(planes):
            f, v = p // 2, p % 2
            two = slice(BWP * p, BWP * (p + 1))
            parent_out[f, v] = partial[f, v]
            parent_out[f, v, 0:RING, :] = partial[f, v, 0:RING, :] + below[two]
            parent_out[f, v, rows - RING : rows, :] = partial[f, v, rows - RING : rows, :] + above[two]

    storm = slots[nest_at * pl.num_programs(0) + j]
    spots = [[centres[n, storm, d] for d in range(2)] for n in range(STEPS + 1)]
    down = [3 * (spots[n + 1][0] - spots[0][0]) for n in range(STEPS)]
    right = [3 * (spots[n + 1][1] - spots[0][1]) for n in range(STEPS)]

    lane = lane_iota()
    row_from = tile_at * strip_rows - PAD
    col_from = lev_at * strip_cols
    gap = (half + LANES) // 2
    lane_cols = (lane, jnp.where(lane < gap, lane + LANES, lane - LANES))

    at = pl.multiple_of(j * both, 8)
    zone = zone_self[pl.ds(at, both), :]
    for got in zone_gots:
        zone = zone + got[pl.ds(at, both), :]
    second = row_iota(both) >= rim
    col_base = lev_at * (strip_cols // 3 - 3)
    for a in range(2):
        picks = []
        for s in range(STEPS):
            fine = jnp.clip(lane_cols[a] + col_from - right[s], 0, SPAN - 1)
            picks.append(jnp.clip(third(fine) - col_base, 0, ZONE_AT - 1))
        pick = jnp.where(second, picks[1], picks[0])
        strips[a] = jnp.take_along_axis(zone, pick, axis=1)
    picks = []
    for s in range(STEPS):
        fine = jnp.clip(lane + row_from - down[s], 0, SPAN - 1)
        picks.append(
            jnp.clip(third(fine) - ((strip_rows // 3) * tile_at - 3) + ZONE_AT, ZONE_AT, LANES - 1)
        )
    pick = jnp.where(second, picks[1], picks[0])
    sides[:, 0:both] = jnp.take_along_axis(zone, pick, axis=1).T

    i_rows = row_iota(height) + row_from
    keep = [None, None]
    for s in range(STEPS):
        for a in range(2):
            i = i_rows - down[s]
            c = lane_cols[a] + col_from - right[s]
            distance = jnp.minimum(jnp.minimum(i, SPAN - 1 - i), jnp.minimum(c, SPAN - 1 - c))
            if s == 0:
                i0, c0 = i_rows, lane_cols[a] + col_from
                stays = (
                    (i0 >= 0) & (i0 < SPAN) & (c0 >= 0) & (c0 < SPAN)
                )
            else:
                stays = keep[a]
            share = jnp.clip(BORDER - distance, 0, BORDER).astype(jnp.float32) / jnp.float32(BORDER)
            weight[s, a] = jnp.where(stays, share, 1.0)
            inner[s, a] = (distance >= 1).astype(jnp.float32)
            keep[a] = distance >= 0

    chunk = 32 if height % 32 == 0 else 8
    first_lane, last_lane = lane == 0, lane == LANES - 1
    cells[...] = jnp.zeros_like(cells)

    for f in range(fields):
        lat, ver = lateral[f], vertical[f]
        for v in range(2):
            q = j * planes + 2 * f + v
            a_row, rest = (2 * f + v) * HALO, (2 * fields + f) * HALO
            cells[v, 0, PAD : PAD + strip_rows, :] = nests[0, f, v, :, 0:LANES]
            cells[v, 1, PAD : PAD + strip_rows, 0:half] = nests[0, f, v, :, LANES : LANES + half]
            ends = []
            for got in (pair, cross):
                tail = got[0, rest : rest + HALO, :]
                if v == 1:
                    tail = pltpu.roll(tail, LANES - half, 1)
                ends.append((got[0, a_row : a_row + HALO, :], tail))
            for a in range(2):
                low = jnp.where(even, ends[1][a], ends[0][a])
                high = jnp.where(even, ends[0][a], ends[1][a])
                lanes = slice(0, LANES if a == 0 else half)
                cells[v, a, PAD - HALO : PAD, lanes] = low[:, lanes]
                cells[v, a, PAD + strip_rows : PAD + strip_rows + HALO, lanes] = high[:, lanes]
            spot = lax.rem(q, 8) * 16
            goal = jnp.where(lev_at == 0, half, LANES - HALO)
            got = pltpu.roll(packed[lax.div(q, 8)], (goal - spot + 2 * LANES) % LANES, 1)
            got = jnp.where((lane >= goal) & (lane < goal + HALO), got, 0.0)
            cells[v, 1, :, half:LANES] = got[:, half:LANES]

        for s in range(STEPS):
            edge_cols = [
                (lane_cols[a] + col_from - right[s] < 3)
                | ((lane_cols[a] + col_from - right[s] >= SPAN // 2)
                   & (lane_cols[a] + col_from - right[s] < SPAN - 3))
                for a in range(2)
            ]
            for c in range(0, height, chunk):
                i = row_iota(chunk) + (row_from + c - down[s])
                in_rows = (i < BORDER) | (i >= SPAN - BORDER)
                early = (i < 3) | ((i >= SPAN // 2) & (i < SPAN - 3))
                for v in range(2):
                    n = s * rim + (2 * f + v) * BWP
                    near = jnp.broadcast_to(sides[c : c + chunk, n : n + 1], (chunk, LANES))
                    far = jnp.broadcast_to(sides[c : c + chunk, n + 1 : n + 2], (chunk, LANES))
                    for a in range(2):
                        side = jnp.where(edge_cols[a], near, far)
                        strip = jnp.where(early, strips[a, n : n + 1, :], strips[a, n + 1 : n + 2, :])
                        driving = jnp.where(in_rows, strip, side)
                        w = weight[s, a, c : c + chunk, :]
                        x = cells[v, a, c : c + chunk, :]
                        mixed[v, a, 8 + c : 8 + c + chunk, :] = (1.0 - w) * x + w * driving
            for c in range(0, height, chunk):
                x = [[mixed[v, a, 8 + c : 8 + c + chunk, :] for a in range(2)] for v in range(2)]
                for v in range(2):
                    sideways = beside(x[v], first_lane, last_lane)
                    for a in range(2):
                        near = (
                            sideways[a]
                            + mixed[v, a, 7 + c : 7 + c + chunk, :]
                            + mixed[v, a, 9 + c : 9 + c + chunk, :]
                        )
                        change = lat * (near - 4.0 * x[v][a]) + ver * (x[1 - v][a] - 2.0 * x[v][a])
                        cells[v, a, c : c + chunk, :] = (
                            x[v][a] + inner[s, a, c : c + chunk, :] * change
                        )

        start = PAD + down[STEPS - 1]
        slide = right[STEPS - 1]
        for v in range(2):
            moved = [
                pltpu.roll(cells[v, a, pl.ds(start, strip_rows), :], (LANES - slide) % LANES, 1)
                for a in range(2)
            ]
            same = (lane + slide >= 0) & (lane + slide < LANES)
            nest_out[0, f, v, :, 0:LANES] = jnp.where(same, moved[0], moved[1])
            nest_out[0, f, v, :, LANES : LANES + half] = jnp.where(same, moved[1], moved[0])[:, :half]


def per_device(parent_field, nest_fields, lateral_rate, vertical_rate, centres, slot_storm):
    fields, _, rows, cols = parent_field.shape
    slot_count, _, _, strip_rows, strip_cols = nest_fields.shape
    storms = slot_storm.shape[0]
    tiles, groups, levs = lax.axis_size("tile"), lax.axis_size("nest"), lax.axis_size("lev")
    planes = 2 * fields
    rim = planes * BWP
    share = storms * STEPS * rim
    own = slot_count * STEPS * rim
    height = strip_rows + 2 * PAD
    half = strip_cols - LANES
    f32 = jnp.float32

    def shaped(*dims):
        return jax.ShapeDtypeStruct(dims, f32)

    pair_list = [(t, t ^ 1) for t in range(tiles) if t ^ 1 < tiles]
    cross_list = [(t, t - 1 if t % 2 == 0 else t + 1) for t in range(1, tiles - 1)]
    edge_block = pl.BlockSpec((1, 3 * fields * HALO, LANES), lambda j: (j, 0, 0))
    nest_block = pl.BlockSpec((1, fields, 2, strip_rows, strip_cols), lambda j: (j, 0, 0, 0, 0))
    to_pair, to_cross = pl.pallas_call(
        lambda *refs: edge_rows_kernel(fields, strip_rows, *refs),
        grid=(slot_count,),
        in_specs=[nest_block],
        out_specs=[edge_block, edge_block],
        out_shape=[shaped(slot_count, 3 * fields * HALO, LANES)] * 2,
        compiler_params=params(),
        name="edge_rows",
    )(nest_fields)
    pair = lax.ppermute(to_pair, "tile", pair_list)
    cross = lax.ppermute(to_cross, "tile", cross_list)

    send, keep, ring = pl.pallas_call(
        lambda *refs: strips_kernel(fields, rows, cols, storms, *refs),
        in_specs=[SMEM_SPEC] * 4 + [VMEM_SPEC],
        out_specs=[VMEM_SPEC] * 3,
        out_shape=[shaped(2 * share + 2 * rim, LANES), shaped(2 * share, LANES), shaped(planes, cols, LANES)],
        scratch_shapes=[pltpu.VMEM((planes, 2, rows + 16, LANES), f32)] * 3
        + [pltpu.VMEM((planes, cols + 16, LANES), f32)] * 3
        + [pltpu.VMEM((LANES, LANES), f32), pltpu.VMEM((2, 24, LANES), f32)],
        compiler_params=params(),
        name="strips",
    )(centres, slot_storm, lateral_rate, vertical_rate, parent_field)
    got = lax.ppermute(send, "lev", [(l, l ^ 1) for l in range(levs)])

    kept, *sends = pl.pallas_call(
        lambda *refs: pair_up_kernel(own, share, rim, *refs),
        in_specs=[VMEM_SPEC] * 2,
        out_specs=[VMEM_SPEC] * groups,
        out_shape=[shaped(2 * own, LANES)] + [shaped(2 * own + rim, LANES)] * (groups - 1),
        compiler_params=params(),
        name="pair_up",
    )(keep, got)
    nest_gots = [
        lax.ppermute(x, "nest", [(n, n ^ (i + 1)) for n in range(groups)])
        for i, x in enumerate(sends)
    ]

    def holds(source, dest):
        low = max((strip_rows // 3) * dest - 3, 0)
        high = tiles * rows - FP + min((strip_rows // 3) * (dest + 1) + 3, FP)
        return rows * source - RING < high and rows * (source + 1) + RING > low

    routes = {}
    for k in range(1, tiles):
        pairs = [
            (t, t ^ k)
            for t in range(tiles)
            if t ^ k < tiles and (holds(t, t ^ k) or holds(t ^ k, t) or abs(t - (t ^ k)) == 1)
        ]
        if pairs:
            routes[k] = pairs
    touching = tuple(k for k in routes if any(abs(a - b) == 1 for a, b in routes[k]))
    moves = (0, *routes)
    zone_shapes = [shaped(own + (rim if k in touching else 0), LANES) for k in moves]
    partial, zone_self, *zone_sends = pl.pallas_call(
        lambda *refs: aim_kernel(
            fields, rows, cols, strip_rows, strip_cols, slot_count, moves, share, touching, *refs
        ),
        in_specs=[SMEM_SPEC] * 2 + [VMEM_SPEC] * (2 + groups),
        out_specs=[VMEM_SPEC] * (1 + len(moves)),
        out_shape=[shaped(fields, 2, rows, cols), *zone_shapes],
        scratch_shapes=[pltpu.VMEM((2 * own, LANES), f32)],
        compiler_params=params(),
        name="aim",
    )(centres, slot_storm, ring, got, kept, *nest_gots)
    zone_gots = [lax.ppermute(x, "tile", routes[k]) for k, x in zip(moves[1:], zone_sends)]

    bundles = -(-slot_count * planes // 8)
    packed = pl.pallas_call(
        lambda *refs: edge_cols_kernel(fields, strip_rows, slot_count, *refs),
        in_specs=[VMEM_SPEC] * 3,
        out_specs=VMEM_SPEC,
        out_shape=shaped(bundles, height, LANES),
        scratch_shapes=[pltpu.VMEM((strip_rows, LANES), f32)],
        compiler_params=params(),
        name="edge_cols",
    )(nest_fields, pair, cross)
    packed = lax.ppermute(packed, "lev", [(l, l ^ 1) for l in range(levs)])

    whole = lambda *dims: pl.BlockSpec(dims, lambda j: (0,) * len(dims))
    nest_final, parent_final = pl.pallas_call(
        lambda *refs: nests_kernel(fields, strip_rows, strip_cols, rows, moves, touching, *refs),
        grid=(slot_count,),
        in_specs=[SMEM_SPEC] * 4
        + [nest_block, edge_block, edge_block, whole(bundles, height, LANES), whole(fields, 2, rows, cols)]
        + [whole(*s.shape) for s in zone_shapes],
        out_specs=[nest_block, whole(fields, 2, rows, cols)],
        out_shape=[
            jax.ShapeDtypeStruct(nest_fields.shape, f32),
            jax.ShapeDtypeStruct(parent_field.shape, f32),
        ],
        scratch_shapes=[
            pltpu.VMEM((2, 2, height, LANES), f32),
            pltpu.VMEM((2, 2, height + 16, LANES), f32),
            pltpu.VMEM((STEPS, 2, height, LANES), f32),
            pltpu.VMEM((STEPS, 2, height, LANES), f32),
            pltpu.VMEM((2, STEPS * rim, LANES), f32),
            pltpu.VMEM((LANES, LANES), f32),
        ],
        compiler_params=params(dimension_semantics=("arbitrary",)),
        name="nests",
    )(
        centres, slot_storm, lateral_rate, vertical_rate,
        nest_fields, pair, cross, packed, partial, zone_self, *zone_gots,
    )
    return (parent_final, nest_final)


def solution(mesh):
    placed = (
        P("member", None, "tile", ("nest", "lev")),
        P(("member", "nest"), None, None, "tile", "lev"),
        P(),
        P(),
        P("member", None, None),
        P("member"),
    )
    return jax.shard_map(
        per_device,
        mesh=mesh,
        in_specs=placed,
        out_specs=(
            P("member", None, "tile", ("nest", "lev")),
            P(("member", "nest"), None, None, "tile", "lev"),
        ),
        check_vma=False,
    )
```

time: 802 us -> 49.1 us (0.06)
  the two profiles are of different devices: /device:TPU:16 before, /device:TPU:0 now
where the time goes in v1:
time: 49.1 us; the launch traced here: 48.8 us
  Pallas kernels  20 us (41%)
  starting transfers between devices  14.7 us (30%)
  waiting for transfers between devices  9.87 us (20%)
  local copies, waits for them, and re-layouts  3.59 us (7%)
  between operations  0.73 us (1%)
    pallas_call x1, Pallas kernels, per_device(): pl.pallas_call(lambda *refs: nests_kernel(fields, strip_rows, strip_cols,...  12.6 us
    ppermute x3, starting transfers between devices, per_device(): lax.ppermute(x, 'tile', routes[k])  8.38 us
    ppermute x1, waiting for transfers between devices, per_device(): lax.ppermute(x, 'nest', [(n, n ^ i + 1) for n in range(groups)])  4.31 us
    ppermute x3, waiting for transfers between devices, per_device(): lax.ppermute(x, 'tile', routes[k])  3.73 us
    unnamed x13, local copies, waits for them, and re-layouts  3.59 us
    ppermute x1, starting transfers between devices, per_device(): pair = lax.ppermute(to_pair, 'tile', pair_list)  3.02 us
    pallas_call x1, Pallas kernels, per_device(): pl.pallas_call(lambda *refs: strips_kernel(fields, rows, cols, storms, *r...  2.94 us
    ppermute x1, waiting for transfers between devices, per_device(): pair = lax.ppermute(to_pair, 'tile', pair_list)  1.83 us
  transfers between devices with their start and end apart: 8, of which 3 were waited for; matrix products, arithmetic and copies ran while one was open for 2% of the time, Pallas kernels for 12%

profile of v1, /device:TPU:0, one launch (start us, length us, event | category | flops | bytes accessed | tf_op | source)
XLA Modules:
  0.0 48.8 jit_solution(3727255624035498091)
XLA Ops:
  0.6 0.0 copy-start
  0.6 1.8 %copy-done = f32[3,5,2,96,192]{4,3,2,1,0:T(8,128)S(1)} copy-done((f32[3,5,2,96,192]{4,3,2,1,0:T(8,128)S(1)}, f32[3,5,2,96,192]{4,3,2,1,0:T(8,128)}, u32[]{:S(2)}) %copy-start) | copy-done | bytes 2211864
  2.5 0.0 copy-start.3
  2.5 0.0 copy-start.4
  2.5 0.0 copy-start.5
  2.5 0.0 copy-start.1
  2.5 1.6 %edge_rows.1 = (f32[3,210,128]{2,1,0:T(8,128)}, f32[3,210,128]{2,1,0:T(8,128)}) custom-call(f32[3,5,2,96,192]{4,3,2,1,0:T(8,128)S(1)} %copy-done), custom_call_target="tpu_custom_call" | custom-call | tf_op jit(solution)/shard_map/edge_rows/pallas_call | solution.py:506
  4.0 3.0 %collective-permute-start = (f32[3,210,128]{2,1,0:T(8,128)}, f32[3,210,128]{2,1,0:T(8,128)S(1)}, u32[]{:S(2)}, u32[]{:S(2)}) collective-permute-start(f32[3,210,128]{2,1,0:T(8,128)} %get-tuple-element.16), channel_id=1, source_target_pairs={{0,4},{4,0},{8,12},{12,8},{1,5},{5,1},{9,13},{13,9},{2,6},{6,2},{1... | collective-permute-start | bytes 967688 | tf_op jit(solution)/shard_map/ppermute | solution.py:515
  7.1 1.4 %collective-permute-start.1 = (f32[3,210,128]{2,1,0:T(8,128)}, f32[3,210,128]{2,1,0:T(8,128)}, u32[]{:S(2)}, u32[]{:S(2)}) collective-permute-start(f32[3,210,128]{2,1,0:T(8,128)} %get-tuple-element.17), channel_id=1, source_target_pairs={{4,8},{8,4},{5,9},{9,5},{6,10},{10,6},{7,11},{11,7},{20,24},{24,20... | collective-permute-start | bytes 967688 | tf_op jit(solution)/shard_map/ppermute | solution.py:516
  8.5 0.8 %copy.10.refs_0_ = s32[3,6,2]{2,1,0:T(8,128)S(1)} copy(s32[3,6,2]{1,2,0:T(2,128)} %param.10) | data formatting | bytes 288 | tf_op args[4]
  9.2 0.0 copy-done.3
  9.2 0.0 copy-done.4
  9.2 0.0 copy-done.5
  9.2 0.0 copy-start.2
  9.3 1.0 %copy-done.2 = f32[5,2,64,128]{3,2,1,0:T(8,128)S(1)} copy-done((f32[5,2,64,128]{3,2,1,0:T(8,128)S(1)}, f32[5,2,64,128]{3,2,1,0:T(8,128)}, u32[]{:S(2)}) %copy-start.2) | copy-done | bytes 327704
  10.2 2.9 %strips.1 = (f32[520,128]{1,0:T(8,128)S(1)}, f32[480,128]{1,0:T(8,128)S(1)}, f32[10,128,128]{2,1,0:T(8,128)S(1)}) custom-call(s32[3,6,2]{2,1,0:T(8,128)S(1)} %copy.10.refs_0_, s32[6]{0:T(128)S(1)} %copy-done.3, f32[5]{0:T(128)S(1)} %copy-done.4, f32[5]{0:T(128)S(1)} %copy-done.5, f32[5,2,64,128]{3,2,1,0:T(8,128)S(1)} %copy-done.2), custom_call_target="tpu_custom_call" | custom-call | tf_op jit(solution)/shard_map/strips/pallas_call | solution.py:518
  13.2 0.1 collective-permute-start.3
  13.3 1.8 %collective-permute-done.refs_1_.refs_5_ = f32[3,210,128]{2,1,0:T(8,128)S(1)} collective-permute-done((f32[3,210,128]{2,1,0:T(8,128)}, f32[3,210,128]{2,1,0:T(8,128)S(1)}, u32[]{:S(2)}, u32[]{:S(2)}) %collective-permute-start) | collective-permute-done | bytes 322592 | tf_op jit(solution)/shard_map/ppermute | solution.py:515
  15.1 0.0 collective-permute-done.1.refs_2_.refs_6_
  15.1 0.0 copy-done.1
  15.1 1.6 %edge_cols.1 = f32[4,128,128]{2,1,0:T(8,128)S(1)} custom-call(f32[3,5,2,96,192]{4,3,2,1,0:T(8,128)S(1)} %copy-done.1, f32[3,210,128]{2,1,0:T(8,128)S(1)} %collective-permute-done.refs_1_.refs_5_, f32[3,210,128]{2,1,0:T(8,128)} %collective-permute-done.1.refs_2_.refs_6_), custom_call_target="tpu_custom_call" | custom-call | tf_op jit(solution)/shard_map/edge_cols/pallas_call | solution.py:575
  16.7 0.1 collective-permute-start.2
  16.8 0.0 collective-permute-done.3.refs_1_.refs_3_
  16.8 1.7 %collective-permute-start.4 = (f32[260,128]{1,0:T(8,128)S(1)}, f32[260,128]{1,0:T(8,128)S(1)}, u32[]{:S(2)}, u32[]{:S(2)}) collective-permute-start(f32[260,128]{1,0:T(8,128)S(1)} %get-tuple-element.22), channel_id=1, source_target_pairs={{0,2},{2,0},{1,3},{3,1},{4,6},{6,4},{5,7},{7,5},{8,10},{10,8},{9,1... | collective-permute-start | bytes 399368 | tf_op jit(solution)/shard_map/ppermute | solution.py:540
  18.6 4.3 %collective-permute-done.4.refs_5_ = f32[260,128]{1,0:T(8,128)S(1)} collective-permute-done((f32[260,128]{1,0:T(8,128)S(1)}, f32[260,128]{1,0:T(8,128)S(1)}, u32[]{:S(2)}, u32[]{:S(2)}) %collective-permute-start.4) | collective-permute-done | bytes 133152 | tf_op jit(solution)/shard_map/ppermute | solution.py:540
  22.9 1.3 %aim.1 = (f32[5,2,64,128]{3,2,1,0:T(8,128)S(1)}, f32[120,128]{1,0:T(8,128)S(1)}, f32[140,128]{1,0:T(8,128)S(1)}, f32[120,128]{1,0:T(8,128)S(1)}, f32[140,128]{1,0:T(8,128)S(1)}) custom-call(s32[3,6,2]{2,1,0:T(8,128)S(1)} %copy.10.refs_0_, s32[6]{0:T(128)S(1)} %copy-done.3, f32[10,128,128]{2,1,0:T(8,128)S(1)} %get-tuple-element.18.refs_2_, ...), custom_call_target="tpu_custom_call" | custom-call | tf_op jit(solution)/shard_map/aim/pallas_call | solution.py:561
  24.1 4.9 %collective-permute-start.5 = (f32[140,128]{1,0:T(8,128)S(1)}, f32[140,128]{1,0:T(8,128)S(1)}, u32[]{:S(2)}, u32[]{:S(2)}) collective-permute-start(f32[140,128]{1,0:T(8,128)S(1)} %get-tuple-element.25), channel_id=1, source_target_pairs={{0,4},{4,0},{8,12},{12,8},{1,5},{5,1},{9,13},{13,9},{2,6},{6,2},{1... | collective-permute-start | bytes 215048 | tf_op jit(solution)/shard_map/ppermute | solution.py:572
  29.1 0.7 %collective-permute-start.7 = (f32[140,128]{1,0:T(8,128)S(1)}, f32[140,128]{1,0:T(8,128)S(1)}, u32[]{:S(2)}, u32[]{:S(2)}) collective-permute-start(f32[140,128]{1,0:T(8,128)S(1)} %get-tuple-element.27), channel_id=1, source_target_pairs={{4,8},{8,4},{5,9},{9,5},{6,10},{10,6},{7,11},{11,7},{20,24},{24,20... | collective-permute-start | bytes 215048 | tf_op jit(solution)/shard_map/ppermute | solution.py:572
  29.7 2.8 %collective-permute-start.6 = (f32[120,128]{1,0:T(8,128)S(1)}, f32[120,128]{1,0:T(8,128)S(1)}, u32[]{:S(2)}, u32[]{:S(2)}) collective-permute-start(f32[120,128]{1,0:T(8,128)S(1)} %get-tuple-element.26), channel_id=1, source_target_pairs={{0,8},{4,12},{8,0},{12,4},{1,9},{5,13},{9,1},{13,5},{2,10},{6,14},... | collective-permute-start | bytes 184328 | tf_op jit(solution)/shard_map/ppermute | solution.py:572
  32.5 3.7 %collective-permute-done.6.refs_11_ = f32[120,128]{1,0:T(8,128)S(1)} collective-permute-done((f32[120,128]{1,0:T(8,128)S(1)}, f32[120,128]{1,0:T(8,128)S(1)}, u32[]{:S(2)}, u32[]{:S(2)}) %collective-permute-start.6) | collective-permute-done | bytes 61472 | tf_op jit(solution)/shard_map/ppermute | solution.py:572
  36.3 0.0 collective-permute-done.5.refs_10_
  36.3 0.0 collective-permute-done.7.refs_12_
  36.3 0.0 collective-permute-done.2.refs_7_
  36.3 12.6 %nests.1 = (f32[3,5,2,96,192]{4,3,2,1,0:T(8,128)}, f32[5,2,64,128]{3,2,1,0:T(8,128)}) custom-call(s32[3,6,2]{2,1,0:T(8,128)S(1)} %copy.10.refs_0_, s32[6]{0:T(128)S(1)} %copy-done.3, f32[5]{0:T(128)S(1)} %copy-done.4, f32[5]{0:T(128)S(1)} %copy-done.5, f32[3,5,2,96,192]{4,3,2,1,0:T(8,128)S(1)} %copy-done.1, ...), custom_call_target="tpu_custom_call" | custom-call | tf_op jit(solution)/shard_map/nests/pallas_call | solution.py:587
  (1 shorter events, 0.0 us)
Async XLA Ops:
  0.6 1.8 %copy-start = (f32[3,5,2,96,192]{4,3,2,1,0:T(8,128)S(1)}, f32[3,5,2,96,192]{4,3,2,1,0:T(8,128)}, u32[]{:S(2)}) copy-start(f32[3,5,2,96,192]{4,3,2,1,0:T(8,128)} %refs_4_.3) | copy-start | bytes 6635524
  2.5 6.8 %copy-start.3 = (s32[6]{0:T(128)S(1)}, s32[6]{0:T(128)}, u32[]{:S(2)}) copy-start(s32[6]{0:T(128)} %refs_1_.5) | copy-start | bytes 76
  2.5 6.8 %copy-start.4 = (f32[5]{0:T(128)S(1)}, f32[5]{0:T(128)}, u32[]{:S(2)}) copy-start(f32[5]{0:T(128)} %refs_2_.3) | copy-start | bytes 64
  2.5 6.8 %copy-start.5 = (f32[5]{0:T(128)S(1)}, f32[5]{0:T(128)}, u32[]{:S(2)}) copy-start(f32[5]{0:T(128)} %refs_3_.3) | copy-start | bytes 64
  2.5 12.6 %copy-start.1 = (f32[3,5,2,96,192]{4,3,2,1,0:T(8,128)S(1)}, f32[3,5,2,96,192]{4,3,2,1,0:T(8,128)}, u32[]{:S(2)}) copy-start(f32[3,5,2,96,192]{4,3,2,1,0:T(8,128)} %refs_4_.3) | copy-start | bytes 6635524
  4.0 11.0 %collective-permute-start = (f32[3,210,128]{2,1,0:T(8,128)}, f32[3,210,128]{2,1,0:T(8,128)S(1)}, u32[]{:S(2)}, u32[]{:S(2)}) collective-permute-start(f32[3,210,128]{2,1,0:T(8,128)} %get-tuple-element.16), channel_id=1, source_target_pairs={{0,4},{4,0},{8,12},{12,8},{1,5},{5,1},{9,13},{13,9},{2,6},{6,2},{1... | collective-permute-start | bytes 967688 | tf_op jit(solution)/shard_map/ppermute | solution.py:515
  7.1 8.0 %collective-permute-start.1 = (f32[3,210,128]{2,1,0:T(8,128)}, f32[3,210,128]{2,1,0:T(8,128)}, u32[]{:S(2)}, u32[]{:S(2)}) collective-permute-start(f32[3,210,128]{2,1,0:T(8,128)} %get-tuple-element.17), channel_id=1, source_target_pairs={{4,8},{8,4},{5,9},{9,5},{6,10},{10,6},{7,11},{11,7},{20,24},{24,20... | collective-permute-start | bytes 967688 | tf_op jit(solution)/shard_map/ppermute | solution.py:516
  9.2 1.0 %copy-start.2 = (f32[5,2,64,128]{3,2,1,0:T(8,128)S(1)}, f32[5,2,64,128]{3,2,1,0:T(8,128)}, u32[]{:S(2)}) copy-start(f32[5,2,64,128]{3,2,1,0:T(8,128)} %refs_4_.2) | copy-start | bytes 983044
  13.2 3.6 %collective-permute-start.3 = (f32[520,128]{1,0:T(8,128)S(1)}, f32[520,128]{1,0:T(8,128)S(1)}, u32[]{:S(2)}, u32[]{:S(2)}) collective-permute-start(f32[520,128]{1,0:T(8,128)S(1)} %get-tuple-element.19), channel_id=1, source_target_pairs={{0,1},{1,0},{2,3},{3,2},{4,5},{5,4},{6,7},{7,6},{8,9},{9,8},{10,11... | collective-permute-start | bytes 798728 | tf_op jit(solution)/shard_map/ppermute | solution.py:529
  16.7 19.6 %collective-permute-start.2 = (f32[4,128,128]{2,1,0:T(8,128)S(1)}, f32[4,128,128]{2,1,0:T(8,128)S(1)}, u32[]{:S(2)}, u32[]{:S(2)}) collective-permute-start(f32[4,128,128]{2,1,0:T(8,128)S(1)} %edge_cols.1), channel_id=1, source_target_pairs={{0,1},{1,0},{2,3},{3,2},{4,5},{5,4},{6,7},{7,6},{8,9},{9,8},{10,11... | collective-permute-start | bytes 786440 | tf_op jit(solution)/shard_map/ppermute | solution.py:584
  16.8 6.0 %collective-permute-start.4 = (f32[260,128]{1,0:T(8,128)S(1)}, f32[260,128]{1,0:T(8,128)S(1)}, u32[]{:S(2)}, u32[]{:S(2)}) collective-permute-start(f32[260,128]{1,0:T(8,128)S(1)} %get-tuple-element.22), channel_id=1, source_target_pairs={{0,2},{2,0},{1,3},{3,1},{4,6},{6,4},{5,7},{7,5},{8,10},{10,8},{9,1... | collective-permute-start | bytes 399368 | tf_op jit(solution)/shard_map/ppermute | solution.py:540
  24.1 12.1 %collective-permute-start.5 = (f32[140,128]{1,0:T(8,128)S(1)}, f32[140,128]{1,0:T(8,128)S(1)}, u32[]{:S(2)}, u32[]{:S(2)}) collective-permute-start(f32[140,128]{1,0:T(8,128)S(1)} %get-tuple-element.25), channel_id=1, source_target_pairs={{0,4},{4,0},{8,12},{12,8},{1,5},{5,1},{9,13},{13,9},{2,6},{6,2},{1... | collective-permute-start | bytes 215048 | tf_op jit(solution)/shard_map/ppermute | solution.py:572
  29.1 7.2 %collective-permute-start.7 = (f32[140,128]{1,0:T(8,128)S(1)}, f32[140,128]{1,0:T(8,128)S(1)}, u32[]{:S(2)}, u32[]{:S(2)}) collective-permute-start(f32[140,128]{1,0:T(8,128)S(1)} %get-tuple-element.27), channel_id=1, source_target_pairs={{4,8},{8,4},{5,9},{9,5},{6,10},{10,6},{7,11},{11,7},{20,24},{24,20... | collective-permute-start | bytes 215048 | tf_op jit(solution)/shard_map/ppermute | solution.py:572
  29.7 6.5 %collective-permute-start.6 = (f32[120,128]{1,0:T(8,128)S(1)}, f32[120,128]{1,0:T(8,128)S(1)}, u32[]{:S(2)}, u32[]{:S(2)}) collective-permute-start(f32[120,128]{1,0:T(8,128)S(1)} %get-tuple-element.26), channel_id=1, source_target_pairs={{0,8},{4,12},{8,0},{12,4},{1,9},{5,13},{9,1},{13,5},{2,10},{6,14},... | collective-permute-start | bytes 184328 | tf_op jit(solution)/shard_map/ppermute | solution.py:572

commit v2 on v1

v2 whole, which is shorter than its diff:
```python
import jax
import jax.numpy as jnp
from jax import lax
from jax.experimental import pallas as pl
from jax.experimental.pallas import tpu as pltpu
from jax.sharding import PartitionSpec as P

FP = 128
BWP = 2
MOVE = 2
STEPS = 2
BORDER = 3 * BWP
SPAN = 3 * FP
HALO = STEPS * (3 * MOVE + 1)
PAD = 16
LANES = 128
PLAN = 8
RING = STEPS
ROW_AT = 32
ZONE_AT = 72
SPLIT = -(FP // 4)
SLOT = 24
VMEM_LIMIT = 40 * 1024 * 1024

SMEM_SPEC = pl.BlockSpec(memory_space=pltpu.SMEM)
VMEM_SPEC = pl.BlockSpec(memory_space=pltpu.VMEM)
HBM_SPEC = pl.BlockSpec(memory_space=pltpu.HBM)
ANY_SPEC = pl.BlockSpec(memory_space=pl.ANY)


def params(**more):
    return pltpu.CompilerParams(vmem_limit_bytes=VMEM_LIMIT, **more)


def lane_iota(rows=1, lanes=LANES):
    return lax.broadcasted_iota(jnp.int32, (rows, lanes), 1)


def row_iota(rows, lanes=LANES):
    return lax.broadcasted_iota(jnp.int32, (rows, lanes), 0)


def beside(x, first_lane, last_lane):
    left = [pltpu.roll(v, 1, 1) for v in x]
    right = [pltpu.roll(v, LANES - 1, 1) for v in x]
    return [
        jnp.where(first_lane, left[1 - a], left[a]) + jnp.where(last_lane, right[1 - a], right[a])
        for a in range(2)
    ]


def third(values):
    return (values * 21846) >> 16


def strips_kernel(
    fields, rows, cols, storms, slot_count, strip_rows,
    centres_in, slots_in, lateral_in, vertical_in, parent_in, nests,
    send, keep, ring_out, to_pair, to_cross, plan, rates,
    plain0, plain1, plain2, turned0, turned1, turned2, block, gather,
    centres, slots, lateral, vertical, parent, low_rows, high_rows, arrived,
):
    sources = (
        (centres_in, centres),
        (slots_in, slots),
        (lateral_in, lateral),
        (vertical_in, vertical),
        (parent_in, parent),
        (nests.at[:, :, :, pl.ds(0, PAD), :], low_rows),
        (nests.at[:, :, :, pl.ds(strip_rows - PAD, PAD), :], high_rows),
    )
    copies = [
        pltpu.make_async_copy(source, target, arrived.at[i])
        for i, (source, target) in enumerate(sources)
    ]
    for copy in copies:
        copy.start()
    planes = 2 * fields
    tile_at, tiles = lax.axis_index("tile"), lax.axis_size("tile")
    lev_at, levs = lax.axis_index("lev"), lax.axis_size("lev")
    col_at = lax.axis_index("nest") * levs + lev_at
    col_blocks = lax.axis_size("nest") * levs
    top = 8
    height = rows + 16
    width = cols + 16

    lane = lane_iota()
    first_lane, last_lane = lane == 0, lane == LANES - 1
    row = tile_at * rows + row_iota(height) - top
    tile_cols = (lane, jnp.where(lane < LANES // 2, lane + LANES, lane - LANES))
    within = [
        (
            (row >= 0) & (row < tiles * rows)
            & (col_at * cols + c >= 0) & (col_at * cols + c < col_blocks * cols)
        ).astype(jnp.float32)
        for c in tile_cols
    ]
    plain0[...] = jnp.zeros_like(plain0)
    turned0[...] = jnp.zeros_like(turned0)
    block[...] = jnp.zeros_like(block)
    for copy in copies[:5]:
        copy.wait()
    for f in range(fields):
        rates[f : f + 1, :] = jnp.full((1, LANES), lateral[f], jnp.float32)
        rates[fields + f : fields + f + 1, :] = jnp.full((1, LANES), vertical[f], jnp.float32)
    for j in range(slot_count):
        storm = slots[lax.axis_index("nest") * slot_count + j]
        at = [[centres[n, d, storm] for d in range(2)] for n in range(STEPS + 1)]
        for d in range(2):
            plan[j * PLAN + d] = at[d + 1][0] - FP // 2
            plan[j * PLAN + 2 + d] = 3 * (at[STEPS][d] - at[0][d])
            plan[j * PLAN + 4 + d] = 3 * (at[STEPS][d] - at[STEPS - 1][d])
    for p in range(planes):
        plain0[p, 0, top : top + rows, :] = parent[p // 2, p % 2]
        block[ROW_AT : ROW_AT + rows, :] = parent[p // 2, p % 2]
        turned0[p, top : top + cols, :] = block[...].T

    inner = slice(1, height - 1)

    def plain_step(source, target, mask):
        for f in range(fields):
            lat, ver = lateral[f], vertical[f]
            for v in range(2):
                x = [source[2 * f + v, a, inner, :] for a in range(2)]
                sideways = beside(x, first_lane, last_lane)
                for a in range(2):
                    near = (
                        sideways[a]
                        + source[2 * f + v, a, 2:height, :]
                        + source[2 * f + v, a, 0 : height - 2, :]
                    )
                    other = source[2 * f + 1 - v, a, inner, :]
                    new = x[a] + lat * (near - 4.0 * x[a]) + ver * (other - 2.0 * x[a])
                    if mask is not None:
                        new = new * mask[a][inner, :]
                    target[2 * f + v, a, inner, :] = new
                    for edge in (0, height - 1):
                        target[2 * f + v, a, edge : edge + 1, :] = jnp.zeros(
                            (1, LANES), jnp.float32
                        )

    plain_step(plain0, plain1, within)
    plain_step(plain1, plain2, None)

    row_t = tile_at * rows + lane_iota() - ROW_AT
    col_t = col_at * cols + row_iota(width) - top
    within_t = (
        (row_t >= 0) & (row_t < tiles * rows) & (col_t >= 0) & (col_t < col_blocks * cols)
    ).astype(jnp.float32)

    def turned_step(source, target, mask):
        for f in range(fields):
            lat, ver = lateral[f], vertical[f]
            for v in range(2):
                x = source[2 * f + v, 1 : width - 1, :]
                near = (
                    source[2 * f + v, 2:width, :]
                    + source[2 * f + v, 0 : width - 2, :]
                    + pltpu.roll(x, 1, 1)
                    + pltpu.roll(x, LANES - 1, 1)
                )
                other = source[2 * f + 1 - v, 1 : width - 1, :]
                new = x + lat * (near - 4.0 * x) + ver * (other - 2.0 * x)
                if mask is not None:
                    new = new * mask[1 : width - 1, :]
                target[2 * f + v, 1 : width - 1, :] = new
                target[2 * f + v, 0:1, :] = jnp.zeros((1, LANES), jnp.float32)
                target[2 * f + v, width - 1 : width, :] = jnp.zeros((1, LANES), jnp.float32)

    turned_step(turned0, turned1, within_t)
    turned_step(turned1, turned2, None)

    share = storms * STEPS * planes * BWP
    for j in range(storms):
        storm = slots[j]
        for s in range(STEPS):
            at = (j * STEPS + s) * planes * BWP
            corner_row = centres[s + 1, 0, storm] - FP // 2 - tile_at * rows
            corner_col = centres[s + 1, 1, storm] - FP // 2 - col_at * cols
            plain = (plain1, plain2)[s]
            turned = (turned1, turned2)[s]
            first = jnp.where(corner_row >= SPLIT, corner_row, corner_row + FP - BWP)
            first = jnp.clip(first + top, 0, height - BWP)
            for p in range(planes):
                for a in range(2):
                    gather[a, BWP * p : BWP * (p + 1), :] = plain[p, a, pl.ds(first, BWP), :]
            shift = (64 * LANES - corner_col) % LANES
            window = [pltpu.roll(gather[a], shift, 1) for a in range(2)]
            place = lane + corner_col
            main = (place >= 0) & (place < cols)
            rim = (place >= -RING) & (place < cols + RING)
            window = jnp.where(main, window[0], jnp.where(rim, window[1], 0.0))[: planes * BWP]
            send[at : at + planes * BWP, :] = window
            keep[at : at + planes * BWP, :] = window
            mine = corner_col + (FP - BWP) * lev_at
            theirs = corner_col + (FP - BWP) * (levs - 1 - lev_at)
            for target, start in ((keep, mine), (send, theirs)):
                start = jnp.clip(start + top, 0, width - BWP)
                for p in range(planes):
                    target[share + at + BWP * p : share + at + BWP * (p + 1), :] = turned[
                        p, pl.ds(start, BWP), :
                    ]
    for p in range(planes):
        send[2 * share + BWP * p : 2 * share + BWP * (p + 1), :] = turned2[p, top - RING : top, :]
        at = 2 * share + planes * BWP + BWP * p
        send[at : at + BWP, :] = turned2[p, top + cols : top + cols + RING, :]
        ring_out[p] = turned2[p, top : top + cols, :]

    for copy in copies[5:]:
        copy.wait()
    even = lax.rem(tile_at, 2) == 0
    half = nests.shape[4] - LANES
    lows, highs, tail = slice(0, HALO), slice(PAD - HALO, PAD), slice(LANES, LANES + half)
    for j in range(slot_count):
        for f in range(fields):
            for v in range(2):
                low, high = low_rows[j, f, v, lows, 0:LANES], high_rows[j, f, v, highs, 0:LANES]
                at = (2 * f + v) * HALO
                to_pair[j, at : at + HALO, :] = jnp.where(even, high, low)
                to_cross[j, at : at + HALO, :] = jnp.where(even, low, high)
            low = jnp.concatenate([low_rows[j, f, v, lows, tail] for v in range(2)], 1)
            high = jnp.concatenate([high_rows[j, f, v, highs, tail] for v in range(2)], 1)
            at = (2 * fields + f) * HALO
            to_pair[j, at : at + HALO, :] = jnp.where(even, high, low)
            to_cross[j, at : at + HALO, :] = jnp.where(even, low, high)


def pair_up_kernel(own, share, rim, keep, got, kept, *sends):
    nest_at = lax.axis_index("nest")
    lev_at = lax.axis_index("lev")
    for k in range(len(sends) + 1):
        group = lax.bitwise_xor(nest_at, k)
        target = kept if k == 0 else sends[k - 1]
        for part in range(2):
            rows = pl.ds(pl.multiple_of(part * share + group * own, 8), own)
            target[part * own : (part + 1) * own, :] = keep[rows, :] + got[rows, :]
        if k > 0:
            west = got[2 * share : 2 * share + rim, :]
            east = got[2 * share + rim : 2 * share + 2 * rim, :]
            target[2 * own : 2 * own + rim, :] = jnp.where(lev_at == 0, east, west)


def aim_kernel(
    fields, rows, cols, strip_rows, strip_cols, slot_count, moves, share, touching,
    plan, ring, first_got, kept, *refs,
):
    crossing = lax.axis_size("nest") - 1
    nest_gots, rest = refs[:crossing], refs[crossing:]
    partial, zone_self, zone_sends, total = rest[0], rest[1], rest[2:-1], rest[-1]
    planes = 2 * fields
    rim = planes * BWP
    own = slot_count * STEPS * rim
    tile_at, tiles = lax.axis_index("tile"), lax.axis_size("tile")
    nest_at = lax.axis_index("nest")
    lev_at = lax.axis_index("lev")

    sums = kept[...]
    for got in nest_gots:
        sums = sums + got[0 : 2 * own, :]
    total[...] = sums

    lane = lane_iota()
    col_base = lev_at * (strip_cols // 3 - 3)
    for j in range(slot_count):
        at = j * STEPS * rim
        both = STEPS * rim
        strip = pltpu.roll(total[at : at + both, :], (LANES - col_base) % LANES, 1)
        side = total[own + at : own + at + both, :]
        second = row_iota(both) >= rim
        origins = [plan[j * PLAN + s] - tile_at * rows for s in range(STEPS)]
        for k in moves:
            dest = lax.bitwise_xor(tile_at, k)
            parts = []
            for s in range(STEPS):
                south = origins[s] >= SPLIT
                wanted = ((dest == 0) & south) | ((dest == tiles - 1) & jnp.logical_not(south))
                offset = ROW_AT + origins[s] + (strip_rows // 3) * dest - 3 - ZONE_AT
                source = lane + offset
                fits = (source >= ROW_AT - RING) & (source < ROW_AT + rows + RING)
                turned = pltpu.roll(side, (64 * LANES - offset) % LANES, 1)
                turned = jnp.where(fits, turned, 0.0)
                parts.append(
                    jnp.where(lane < ZONE_AT, strip * wanted.astype(jnp.float32), turned)
                )
            target = zone_self if k == 0 else zone_sends[moves.index(k) - 1]
            target[at : at + both, :] = jnp.where(second, parts[1], parts[0])

    from_west = first_got[2 * share + rim : 2 * share + 2 * rim, :]
    from_east = first_got[2 * share : 2 * share + rim, :]
    far_west = jnp.zeros((rim, LANES), jnp.float32)
    far_east = jnp.zeros((rim, LANES), jnp.float32)
    for i, got in enumerate(nest_gots):
        other = lax.bitwise_xor(nest_at, i + 1)
        edge = got[2 * own : 2 * own + rim, :]
        far_west = far_west + jnp.where(other == nest_at - 1, edge, 0.0)
        far_east = far_east + jnp.where(other == nest_at + 1, edge, 0.0)
    from_west = jnp.where(lev_at == 0, far_west, from_west)
    from_east = jnp.where(lev_at == 0, from_east, far_east)
    for p in range(planes):
        two = slice(BWP * p, BWP * (p + 1))
        total[0:cols, :] = ring[p]
        total[0:RING, :] = total[0:RING, :] + from_west[two]
        total[cols - RING : cols, :] = total[cols - RING : cols, :] + from_east[two]
        total[0:LANES, :] = total[0:cols, :].T
        partial[p // 2, p % 2] = total[ROW_AT : ROW_AT + rows, :]
        below = total[ROW_AT - RING : ROW_AT, :]
        above = total[ROW_AT + rows : ROW_AT + rows + RING, :]
        for i, k in enumerate(moves[1:]):
            if k in touching:
                dest = lax.bitwise_xor(tile_at, k)
                zone_sends[i][own + BWP * p : own + BWP * (p + 1), :] = jnp.where(
                    dest > tile_at, above, below
                )


def edge_cols_kernel(fields, strip_rows, slot_count, nests, pair, cross, after, packed, wide):
    del after
    even = lax.rem(lax.axis_index("tile"), 2) == 0
    west_most = lax.axis_index("lev") == 0
    planes = 2 * fields
    half = nests.shape[4] - LANES
    packed[...] = jnp.zeros_like(packed)
    wide[...] = jnp.zeros_like(wide)
    lane = lane_iota()
    for q in range(slot_count * planes):
        j, f, v = q // planes, (q % planes) // 2, q % 2
        spot = (q % 8) * 16
        mask = (lane >= spot) & (lane < spot + HALO)
        wide[:, 0:half] = nests[j, f, v, :, LANES : LANES + half]
        cells = jnp.where(west_most, wide[...], nests[j, f, v, :, 0:LANES])
        shift = jnp.where(west_most, spot + 2 * LANES - (half - HALO), spot + 2 * LANES) % LANES
        cells = pltpu.roll(cells, shift, 1)
        rows = slice(PAD, PAD + strip_rows)
        packed[q // 8, rows, :] = jnp.where(mask, cells, packed[q // 8, rows, :])
        at, rest = (2 * f + v) * HALO, (2 * fields + f) * HALO
        shift = (
            jnp.where(west_most, spot + 2 * LANES - (half - HALO) - half * v, spot + 2 * LANES) % LANES
        )
        halos = []
        for got in (pair, cross):
            cells = jnp.where(west_most, got[j, rest : rest + HALO, :], got[j, at : at + HALO, :])
            halos.append(pltpu.roll(cells, shift, 1))
        high = jnp.where(even, halos[0], halos[1])
        low = jnp.where(even, halos[1], halos[0])
        rows = slice(PAD - HALO, PAD)
        packed[q // 8, rows, :] = jnp.where(mask, low, packed[q // 8, rows, :])
        rows = slice(PAD + strip_rows, PAD + strip_rows + HALO)
        packed[q // 8, rows, :] = jnp.where(mask, high, packed[q // 8, rows, :])


def advance_kernel(
    fields, strip_rows, strip_cols, slot_count,
    plan, rates, nests, pair, cross, packed,
    inner_out, side_out, row_out, cells, first, second,
):
    planes = 2 * fields
    half = strip_cols - LANES
    room = PAD + 8
    height = strip_rows + 16
    tile_at, tiles = lax.axis_index("tile"), lax.axis_size("tile")
    nest_at = lax.axis_index("nest")
    lev_at = lax.axis_index("lev")
    even = lax.rem(tile_at, 2) == 0
    lane = lane_iota()
    first_lane, last_lane = lane == 0, lane == LANES - 1
    chunk = 16 if height % 16 == 0 and strip_rows % 16 == 0 else 8
    row_start = pl.multiple_of(jnp.where(tile_at == 0, 0, strip_rows - 16), 8)
    west_lanes = lane < jnp.where(lev_at == 0, LANES // 2, 0)

    cells[...] = jnp.zeros_like(cells)

    lats = [rates[f : f + 1, :] for f in range(fields)]
    vers = [rates[fields + f : fields + f + 1, :] for f in range(fields)]
    stays = [1.0 - 4.0 * lats[f] - 2.0 * vers[f] for f in range(fields)]

    def stencil(f, source, at, size):
        x = [[source[f, v, a, at : at + size, :] for a in range(2)] for v in range(2)]
        new = [[None] * 2, [None] * 2]
        for v in range(2):
            sideways = beside(x[v], first_lane, last_lane)
            for a in range(2):
                near = (
                    sideways[a]
                    + source[f, v, a, at - 1 : at + size - 1, :]
                    + source[f, v, a, at + 1 : at + size + 1, :]
                )
                new[v][a] = stays[f] * x[v][a] + lats[f] * near + vers[f] * x[1 - v][a]
        return new

    def one(j, _):
        down, right = plan[j * PLAN + 2], plan[j * PLAN + 3]
        shift = (LANES - right) % LANES
        same = (lane + right >= 0) & (lane + right < LANES)
        start = room - 8 + down
        goal = jnp.where(lev_at == 0, half, LANES - HALO)
        in_goal = (lane >= goal) & (lane < goal + HALO)
        for f in range(fields):
            for v in range(2):
                cells[f, v, 0, room : room + strip_rows, :] = nests[j, f, v, :, 0:LANES]
                cells[f, v, 1, room : room + strip_rows, 0:half] = nests[j, f, v, :, LANES : LANES + half]
                ends = []
                for got in (pair, cross):
                    tail = got[j, (planes + f) * HALO : (planes + f + 1) * HALO, :]
                    if v == 1:
                        tail = pltpu.roll(tail, LANES - half, 1)
                    ends.append((got[j, (2 * f + v) * HALO : (2 * f + v + 1) * HALO, :], tail))
                for a in range(2):
                    low = jnp.where(even, ends[1][a], ends[0][a])
                    high = jnp.where(even, ends[0][a], ends[1][a])
                    lanes = slice(0, LANES if a == 0 else half)
                    cells[f, v, a, room - HALO : room, lanes] = low[:, lanes]
                    cells[f, v, a, room + strip_rows : room + strip_rows + HALO, lanes] = high[:, lanes]
                n = j * planes + 2 * f + v
                got = pltpu.roll(
                    packed[lax.div(n, 8)], (goal - lax.rem(n, 8) * 16 + 2 * LANES) % LANES, 1
                )
                got = jnp.where(in_goal, got, 0.0)
                cells[f, v, 1, room - PAD : room + strip_rows + PAD, half:LANES] = got[:, half:LANES]

        sides = [None, None]
        for f in range(fields):
            for v in range(2):
                both = [
                    pltpu.roll(cells[f, v, a, pl.ds(start, height), :], shift, 1) for a in range(2)
                ]
                both = [jnp.where(same, both[a], both[1 - a]) for a in range(2)]
                for a in range(2):
                    first[f, v, a, 8 : 8 + height, :] = both[a]
                near = jnp.where(west_lanes, both[0], both[1])
                turn = jnp.where(lev_at == 0, 8, LANES + 16 - half) + f * SLOT
                near = pltpu.roll(near, turn % LANES, 1)
                sides[v] = near if f == 0 else jnp.where(lane >= f * SLOT, near, sides[v])
        for v in range(2):
            side_out[v, j] = sides[v]
        for f in range(fields):
            for v in range(2):
                for a in range(2):
                    row_out[j, f, v, a] = first[f, v, a, pl.ds(8 + row_start, 32), :]
            for c in range(0, height, chunk):
                new = stencil(f, first, 8 + c, chunk)
                for v in range(2):
                    for a in range(2):
                        second[f, v, a, 8 + c : 8 + c + chunk, :] = new[v][a]
        for f in range(fields):
            for c in range(0, strip_rows, chunk):
                new = stencil(f, second, 16 + c, chunk)
                for v in range(2):
                    inner_out[j, f, v, c : c + chunk, 0:LANES] = new[v][0]
                    inner_out[j, f, v, c : c + chunk, LANES : LANES + half] = new[v][1][:, :half]
        return 0

    lax.fori_loop(0, slot_count, one, 0)


def gaps(i):
    return jnp.minimum(i, SPAN - 1 - i)


def settle_kernel(
    fields, strip_rows, strip_cols, rows, slot_count, moves, touching,
    plan, rates, inner, side_in, row_in, partial, zone_self, *refs,
):
    count = len(moves) - 1
    zone_gots = refs[:count]
    nest_out, parent_out = refs[count : count + 2]
    zone, turned, sides, strips, side_new, mixed, rows_mixed, rows_new, whole, done = refs[count + 2 :]
    planes = 2 * fields
    rim = planes * BWP
    both = STEPS * rim
    own = slot_count * both
    half = strip_cols - LANES
    height = strip_rows + 16
    tile_at, tiles = lax.axis_index("tile"), lax.axis_size("tile")
    nest_at = lax.axis_index("nest")
    lev_at = lax.axis_index("lev")
    lane = lane_iota()
    first_lane, last_lane = lane == 0, lane == LANES - 1

    below = jnp.zeros((rim, LANES), jnp.float32)
    above = jnp.zeros((rim, LANES), jnp.float32)
    for i, k in enumerate(moves[1:]):
        if k in touching:
            other = lax.bitwise_xor(tile_at, k)
            edge = zone_gots[i][own : own + rim, :]
            below = below + jnp.where(other == tile_at - 1, edge, 0.0)
            above = above + jnp.where(other == tile_at + 1, edge, 0.0)
    for p in range(planes):
        f, v = p // 2, p % 2
        two = slice(BWP * p, BWP * (p + 1))
        parent_out[f, v] = partial[f, v]
        parent_out[f, v, 0:RING, :] = partial[f, v, 0:RING, :] + below[two]
        parent_out[f, v, rows - RING : rows, :] = partial[f, v, rows - RING : rows, :] + above[two]

    whole_move = [[plan[j * PLAN + 2 + d] for d in range(2)] for j in range(slot_count)]
    last_move = [[plan[j * PLAN + 4 + d] for d in range(2)] for j in range(slot_count)]
    offsets = [[(0, 0) if s == 1 else last_move[j] for s in range(STEPS)] for j in range(slot_count)]
    earlier = [[whole_move[j], last_move[j]] for j in range(slot_count)]

    total = zone_self[0:own, :]
    for got in zone_gots:
        total = total + got[0:own, :]
    zone[...] = jnp.zeros_like(zone)
    zone[0:own, :] = total
    second = row_iota(both) >= rim
    col_base = lev_at * (strip_cols // 3 - 3)
    col_from = lev_at * strip_cols
    gap = (half + LANES) // 2
    owner = jnp.zeros((1, LANES), jnp.int32)
    for f in range(1, fields):
        owner = owner + (lane >= f * SLOT).astype(jnp.int32)
    side_cols = lane - SLOT * owner + jnp.where(lev_at == 0, -8, 2 * strip_cols - 16)
    lane_cols = (
        lane + col_from,
        jnp.where(lane < gap, lane + LANES, lane - LANES) + col_from,
        side_cols,
    )
    for j in range(slot_count):
        block = zone[j * both : (j + 1) * both, :]
        for a in range(3):
            picks = [
                jnp.clip(third(jnp.clip(lane_cols[a] + offsets[j][s][1], 0, SPAN - 1)) - col_base, 0, ZONE_AT - 1)
                for s in range(STEPS)
            ]
            strips[j, a] = jnp.take_along_axis(block, jnp.where(second, picks[1], picks[0]), axis=1)
        picks = [
            jnp.clip(
                third(jnp.clip(lane + (tile_at * strip_rows - 8) + offsets[j][s][0], 0, SPAN - 1))
                - ((strip_rows // 3) * tile_at - 3)
                + ZONE_AT,
                ZONE_AT,
                LANES - 1,
            )
            for s in range(STEPS)
        ]
        turned[j * both : (j + 1) * both, :] = jnp.take_along_axis(
            block, jnp.where(second, picks[1], picks[0]), axis=1
        )
    sides[...] = turned[...].T

    chunk = 16 if height % 16 == 0 else 8
    lats = [rates[f : f + 1, :] for f in range(fields)]
    vers = [rates[fields + f : fields + f + 1, :] for f in range(fields)]
    lat, ver = lats[0], vers[0]
    for f in range(1, fields):
        lat = jnp.where(owner >= f, lats[f], lat)
        ver = jnp.where(owner >= f, vers[f], ver)
    stay = 4.0 * lat + 2.0 * ver
    for s in range(STEPS):
        insides = {}
        for j in range(slot_count):
            by_row, by_col = offsets[j][s]
            was_row, was_col = earlier[j][s]
            col = side_cols + by_col
            col_gap = gaps(col)
            col_kept = gaps(side_cols + was_col)
            depth = jnp.where((col < 3) | ((col >= SPAN // 2) & (col < SPAN - 3)), 0, 1)
            lines, picks = [], []
            for v in range(2):
                picks.append(jnp.minimum(j * both + s * rim + v * BWP + 2 * BWP * owner + depth, own - 1))
                pair_of = []
                for r in range(BWP):
                    n = s * rim + v * BWP + r
                    line = strips[j, 2, n : n + 1, :]
                    for f in range(1, fields):
                        m = n + 2 * BWP * f
                        line = jnp.where(owner >= f, strips[j, 2, m : m + 1, :], line)
                    pair_of.append(line)
                lines.append(pair_of)
            for c in range(0, height, chunk):
                base = row_iota(chunk) + (tile_at * strip_rows - 8 + c)
                i = base + by_row
                distance = jnp.minimum(gaps(i), col_gap)
                kept = jnp.minimum(gaps(base + was_row), col_kept)
                w = jnp.clip(BORDER - distance, 0, BORDER).astype(jnp.float32) * (1.0 / BORDER)
                w = jnp.where(kept >= 0, w, 1.0)
                in_rows = (i < BORDER) | (i >= SPAN - BORDER)
                early = (i < 3) | ((i >= SPAN // 2) & (i < SPAN - 3))
                insides[j, c] = (distance >= 1).astype(jnp.float32)
                for v in range(2):
                    pick = jnp.broadcast_to(picks[v], (chunk, LANES))
                    side = jnp.take_along_axis(sides[c : c + chunk, :], pick, axis=1)
                    strip = jnp.where(early, lines[v][0], lines[v][1])
                    driving = jnp.where(in_rows, strip, side)
                    x = side_in[v, j, c : c + chunk, :] if s == 0 else side_new[v, j, c : c + chunk, :]
                    mixed[v, j, 8 + c : 8 + c + chunk, :] = (1.0 - w) * x + w * driving
        for j in range(slot_count):
            for c in range(0, height, chunk):
                x = [mixed[v, j, 8 + c : 8 + c + chunk, :] for v in range(2)]
                for v in range(2):
                    near = (
                        pltpu.roll(x[v], 1, 1)
                        + pltpu.roll(x[v], LANES - 1, 1)
                        + mixed[v, j, 7 + c : 7 + c + chunk, :]
                        + mixed[v, j, 9 + c : 9 + c + chunk, :]
                    )
                    change = lat * near + ver * x[1 - v] - stay * x[v]
                    side_new[v, j, c : c + chunk, :] = x[v] + insides[j, c] * change

    outer = (tile_at == 0) | (tile_at == tiles - 1)
    window = jnp.where(tile_at == 0, -8, tile_at * strip_rows + strip_rows - 24)
    row_start = pl.multiple_of(jnp.where(tile_at == 0, 0, strip_rows - 16), 8)
    line = row_iota(16)
    line_from = jnp.where(tile_at == 0, 0, 16 - HALO)
    lows = (0, jnp.where(lev_at > 0, half - HALO, LANES))
    highs = (jnp.where(lev_at == 0, HALO, 0), half)
    along = lane_iota(strip_rows)
    near_col = [(along >= lows[a]) & (along < highs[a]) for a in range(2)]
    across = lane_iota(16)
    near_row = [
        (line >= line_from)
        & (line < line_from + HALO)
        & ((across < lows[a]) | (across >= highs[a]))
        for a in range(2)
    ]

    def one(j, _):
        for f in range(fields):
            back = (2 * LANES + jnp.where(lev_at == 0, -8, half - 16) - f * SLOT) % LANES
            for v in range(2):
                near = pltpu.roll(side_new[v, j, 8 : 8 + strip_rows, :], back, 1)
                whole[j, f, v, :, 0:LANES] = jnp.where(near_col[0], near, inner[j, f, v, :, 0:LANES])
                whole[j, f, v, :, LANES : LANES + half] = jnp.where(
                    near_col[1][:, :half], near[:, :half], inner[j, f, v, :, LANES : LANES + half]
                )

        @pl.when(outer)
        def _():
            full, last = plan[j * PLAN + 2], plan[j * PLAN + 4]
            base = row_iota(32) + window
            for s in range(STEPS):
                i = base + (last if s == 0 else 0)
                kept = gaps(base + (full if s == 0 else last)) >= 0
                w = jnp.clip(BORDER - gaps(i), 0, BORDER).astype(jnp.float32) * (1.0 / BORDER)
                w = jnp.where(kept, w, 1.0)
                rest = 1.0 - w
                inside = (gaps(i) >= 1).astype(jnp.float32)
                early = (i < 3) | ((i >= SPAN // 2) & (i < SPAN - 3))
                for f in range(fields):
                    for v in range(2):
                        n = s * rim + (2 * f + v) * BWP
                        for a in range(2):
                            driving = jnp.where(
                                early, strips[j, a, n : n + 1, :], strips[j, a, n + 1 : n + 2, :]
                            )
                            x = row_in[j, f, v, a] if s == 0 else rows_new[f, v, a]
                            rows_mixed[f, v, a, 8:40, :] = rest * x + w * driving
                for f in range(fields):
                    stay = 4.0 * lats[f] + 2.0 * vers[f]
                    value = [[rows_mixed[f, v, a, 8:40, :] for a in range(2)] for v in range(2)]
                    for v in range(2):
                        sideways = beside(value[v], first_lane, last_lane)
                        for a in range(2):
                            near = (
                                sideways[a]
                                + rows_mixed[f, v, a, 7:39, :]
                                + rows_mixed[f, v, a, 9:41, :]
                            )
                            change = (
                                lats[f] * near + vers[f] * value[1 - v][a] - stay * value[v][a]
                            )
                            rows_new[f, v, a] = value[v][a] + inside * change
            for f in range(fields):
                for v in range(2):
                    target = pl.ds(row_start, 16)
                    whole[j, f, v, target, 0:LANES] = jnp.where(
                        near_row[0], rows_new[f, v, 0, 8:24, :], whole[j, f, v, target, 0:LANES]
                    )
                    whole[j, f, v, target, LANES : LANES + half] = jnp.where(
                        near_row[1][:, :half],
                        rows_new[f, v, 1, 8:24, 0:half],
                        whole[j, f, v, target, LANES : LANES + half],
                    )

        pltpu.make_async_copy(whole.at[j], nest_out.at[j], done.at[j]).start()
        return 0

    lax.fori_loop(0, slot_count, one, 0)

    def wait(j, _):
        pltpu.make_async_copy(whole.at[j], nest_out.at[j], done.at[j]).wait()
        return 0

    lax.fori_loop(0, slot_count, wait, 0)


def per_device(parent_field, nest_fields, lateral_rate, vertical_rate, centres, slot_storm):
    fields, _, rows, cols = parent_field.shape
    slot_count, _, _, strip_rows, strip_cols = nest_fields.shape
    storms = slot_storm.shape[0]
    tiles, groups, levs = lax.axis_size("tile"), lax.axis_size("nest"), lax.axis_size("lev")
    planes = 2 * fields
    rim = planes * BWP
    share = storms * STEPS * rim
    own = slot_count * STEPS * rim
    height = strip_rows + 2 * PAD
    half = strip_cols - LANES
    f32 = jnp.float32

    def shaped(*dims):
        return jax.ShapeDtypeStruct(dims, f32)

    pair_list = [(t, t ^ 1) for t in range(tiles) if t ^ 1 < tiles]
    cross_list = [(t, t - 1 if t % 2 == 0 else t + 1) for t in range(1, tiles - 1)]
    centres = jnp.swapaxes(centres, 1, 2)

    send, keep, ring, to_pair, to_cross, plan, rates = pl.pallas_call(
        lambda *refs: strips_kernel(fields, rows, cols, storms, slot_count, strip_rows, *refs),
        in_specs=[HBM_SPEC] * 6,
        out_specs=[VMEM_SPEC] * 5 + [SMEM_SPEC, VMEM_SPEC],
        out_shape=[
            shaped(2 * share + 2 * rim, LANES),
            shaped(2 * share, LANES),
            shaped(planes, cols, LANES),
            shaped(slot_count, 3 * fields * HALO, LANES),
            shaped(slot_count, 3 * fields * HALO, LANES),
            jax.ShapeDtypeStruct((slot_count * PLAN,), jnp.int32),
            shaped(2 * fields, LANES),
        ],
        scratch_shapes=[pltpu.VMEM((planes, 2, rows + 16, LANES), f32)] * 3
        + [pltpu.VMEM((planes, cols + 16, LANES), f32)] * 3
        + [
            pltpu.VMEM((LANES, LANES), f32),
            pltpu.VMEM((2, 24, LANES), f32),
            pltpu.SMEM(centres.shape, jnp.int32),
            pltpu.SMEM(slot_storm.shape, jnp.int32),
            pltpu.SMEM(lateral_rate.shape, f32),
            pltpu.SMEM(vertical_rate.shape, f32),
            pltpu.VMEM(parent_field.shape, f32),
            pltpu.VMEM((slot_count, fields, 2, PAD, strip_cols), f32),
            pltpu.VMEM((slot_count, fields, 2, PAD, strip_cols), f32),
            pltpu.SemaphoreType.DMA((7,)),
        ],
        compiler_params=params(),
        name="strips",
    )(
        *(
            pltpu.with_memory_space_constraint(x, pltpu.HBM)
            for x in (centres, slot_storm, lateral_rate, vertical_rate, parent_field, nest_fields)
        )
    )
    got = lax.ppermute(send, "lev", [(l, l ^ 1) for l in range(levs)])
    pair = lax.ppermute(to_pair, "tile", pair_list)
    cross = lax.ppermute(to_cross, "tile", cross_list)

    kept, *sends = pl.pallas_call(
        lambda *refs: pair_up_kernel(own, share, rim, *refs),
        in_specs=[VMEM_SPEC] * 2,
        out_specs=[VMEM_SPEC] * groups,
        out_shape=[shaped(2 * own, LANES)] + [shaped(2 * own + rim, LANES)] * (groups - 1),
        compiler_params=params(),
        name="pair_up",
    )(keep, got)
    nest_gots = [
        lax.ppermute(x, "nest", [(n, n ^ (i + 1)) for n in range(groups)])
        for i, x in enumerate(sends)
    ]

    def holds(source, dest):
        low = max((strip_rows // 3) * dest - 3, 0)
        high = tiles * rows - FP + min((strip_rows // 3) * (dest + 1) + 3, FP)
        return rows * source - RING < high and rows * (source + 1) + RING > low

    routes = {}
    for k in range(1, tiles):
        pairs = [
            (t, t ^ k)
            for t in range(tiles)
            if t ^ k < tiles and (holds(t, t ^ k) or holds(t ^ k, t) or abs(t - (t ^ k)) == 1)
        ]
        if pairs:
            routes[k] = pairs
    touching = tuple(k for k in routes if any(abs(a - b) == 1 for a, b in routes[k]))
    moves = (0, *routes)
    zone_shapes = [shaped(own + (rim if k in touching else 0), LANES) for k in moves]
    partial, zone_self, *zone_sends = pl.pallas_call(
        lambda *refs: aim_kernel(
            fields, rows, cols, strip_rows, strip_cols, slot_count, moves, share, touching, *refs
        ),
        in_specs=[SMEM_SPEC] + [VMEM_SPEC] * (2 + groups),
        out_specs=[VMEM_SPEC] * (1 + len(moves)),
        out_shape=[shaped(fields, 2, rows, cols), *zone_shapes],
        scratch_shapes=[pltpu.VMEM((2 * own, LANES), f32)],
        compiler_params=params(),
        name="aim",
    )(plan, ring, got, kept, *nest_gots)
    zone_gots = [lax.ppermute(x, "tile", routes[k]) for k, x in zip(moves[1:], zone_sends)]

    bundles = -(-slot_count * planes // 8)
    packed = pl.pallas_call(
        lambda *refs: edge_cols_kernel(fields, strip_rows, slot_count, *refs),
        in_specs=[VMEM_SPEC] * 3 + [ANY_SPEC],
        out_specs=VMEM_SPEC,
        out_shape=shaped(bundles, height, LANES),
        scratch_shapes=[pltpu.VMEM((strip_rows, LANES), f32)],
        compiler_params=params(),
        name="edge_cols",
    )(nest_fields, pair, cross, zone_self)
    packed = lax.ppermute(packed, "lev", [(l, l ^ 1) for l in range(levs)])

    inner, side_in, row_in = pl.pallas_call(
        lambda *refs: advance_kernel(fields, strip_rows, strip_cols, slot_count, *refs),
        in_specs=[SMEM_SPEC] + [VMEM_SPEC] * 5,
        out_specs=[VMEM_SPEC] * 3,
        out_shape=[
            shaped(*nest_fields.shape),
            shaped(2, slot_count, strip_rows + 16, LANES),
            shaped(slot_count, fields, 2, 2, 32, LANES),
        ],
        scratch_shapes=[pltpu.VMEM((fields, 2, 2, strip_rows + 48, LANES), f32)]
        + [pltpu.VMEM((fields, 2, 2, strip_rows + 32, LANES), f32)] * 2,
        compiler_params=params(),
        name="advance",
    )(plan, rates, nest_fields, pair, cross, packed)

    nest_final, parent_final = pl.pallas_call(
        lambda *refs: settle_kernel(
            fields, strip_rows, strip_cols, rows, slot_count, moves, touching, *refs
        ),
        in_specs=[SMEM_SPEC] + [VMEM_SPEC] * (5 + len(moves)),
        out_specs=[ANY_SPEC, VMEM_SPEC],
        out_shape=[shaped(*nest_fields.shape), shaped(*parent_field.shape)],
        scratch_shapes=[
            pltpu.VMEM((LANES, LANES), f32),
            pltpu.VMEM((LANES, LANES), f32),
            pltpu.VMEM((LANES, LANES), f32),
            pltpu.VMEM((slot_count, 3, STEPS * rim, LANES), f32),
            pltpu.VMEM((2, slot_count, strip_rows + 16, LANES), f32),
            pltpu.VMEM((2, slot_count, strip_rows + 32, LANES), f32),
            pltpu.VMEM((fields, 2, 2, 48, LANES), f32),
            pltpu.VMEM((fields, 2, 2, 32, LANES), f32),
            pltpu.VMEM((slot_count, fields, 2, strip_rows, strip_cols), f32),
            pltpu.SemaphoreType.DMA((slot_count,)),
        ],
        compiler_params=params(),
        name="settle",
    )(
        plan, rates, inner, side_in, row_in, partial, zone_self, *zone_gots,
    )
    return (parent_final, nest_final)


def solution(mesh):
    placed = (
        P("member", None, "tile", ("nest", "lev")),
        P(("member", "nest"), None, None, "tile", "lev"),
        P(),
        P(),
        P("member", None, None),
        P("member"),
    )
    return jax.shard_map(
        per_device,
        mesh=mesh,
        in_specs=placed,
        out_specs=(
            P("member", None, "tile", ("nest", "lev")),
            P(("member", "nest"), None, None, "tile", "lev"),
        ),
        check_vma=False,
    )
```

time: 49.1 us -> 38.6 us (0.79)
  waiting for transfers between devices: 9.87 us -> 5.03 us
  local copies, waits for them, and re-layouts: 3.59 us -> 0.01 us
  Pallas kernels: 20 us -> 18.9 us
  starting transfers between devices: 14.7 us -> 13.7 us
    ppermute x3, waiting for transfers between devices: 3.73 us -> 0.01 us  [per_device(): lax.ppermute(x, 'tile', routes[k])]
    unnamed x13 -> x2, local copies, waits for them, and re-layouts: 3.59 us -> 0.01 us
    ppermute x1, waiting for transfers between devices: 1.83 us -> 0.85 us  [per_device(): pair = lax.ppermute(to_pair, 'tile', pair_list)]
    pallas_call x1, Pallas kernels: 1.6 us -> 0.71 us  [per_device(): pl.pallas_call(lambda *refs: edge_cols_kernel(fields, strip_rows, slot_co...]
    ppermute x1, starting transfers between devices: 1.39 us -> 0.67 us  [per_device(): cross = lax.ppermute(to_cross, 'tile', cross_list)]
  transfers between devices with their start and end apart: 8 -> 8, of which waited for: 3 -> 2; matrix products, arithmetic and copies ran while one was open for 2% -> 0% of each run, Pallas kernels for 12% -> 24%
where the time goes in v2:
time: 38.6 us; the launch traced here: 38.4 us
  Pallas kernels  18.9 us (49%)
  starting transfers between devices  13.7 us (35%)
  waiting for transfers between devices  5.03 us (13%)
  between operations  0.74 us (2%)
    ppermute x3, starting transfers between devices, per_device(): lax.ppermute(x, 'tile', routes[k])  8.27 us
    pallas_call x1, Pallas kernels, per_device(): pl.pallas_call(lambda *refs: advance_kernel(fields, strip_rows, strip_col...  7.93 us
    pallas_call x1, Pallas kernels, per_device(): pl.pallas_call(lambda *refs: settle_kernel(fields, strip_rows, strip_cols...  5.08 us
    ppermute x1, waiting for transfers between devices, per_device(): lax.ppermute(x, 'nest', [(n, n ^ i + 1) for n in range(groups)])  4.16 us
    pallas_call x1, Pallas kernels, per_device(): pl.pallas_call(lambda *refs: strips_kernel(fields, rows, cols, storms, sl...  4.06 us
    ppermute x1, starting transfers between devices, per_device(): pair = lax.ppermute(to_pair, 'tile', pair_list)  2.66 us
    ppermute x1, starting transfers between devices, per_device(): lax.ppermute(x, 'nest', [(n, n ^ i + 1) for n in range(groups)])  1.56 us
    pallas_call x1, Pallas kernels, per_device(): pl.pallas_call(lambda *refs: aim_kernel(fields, rows, cols, strip_rows, s...  1.08 us
  transfers between devices with their start and end apart: 8, of which 2 were waited for; matrix products, arithmetic and copies ran while one was open for 0% of the time, Pallas kernels for 24%

profile of v2, /device:TPU:0, one launch (start us, length us, event | category | flops | bytes accessed | tf_op | source)
XLA Modules:
  0.0 38.4 jit_solution(334997429040356101)
XLA Ops:
  0.6 0.0 copy-start
  0.6 4.1 %strips.1 = (f32[520,128]{1,0:T(8,128)S(1)}, f32[480,128]{1,0:T(8,128)S(1)}, f32[10,128,128]{2,1,0:T(8,128)S(1)}, f32[3,210,128]{2,1,0:T(8,128)S(1)}, f32[3,210,...) custom-call(s32[3,2,6]{2,1,0:T(2,128)} %bitcast.1, s32[6]{0:T(128)} %refs_1_.1, f32[5]{0:T(128)} %refs_2_.2, ...), custom_call_target="tpu_custom_call" | custom-call | tf_op jit(solution)/shard_map/strips/pallas_call | solution.py:706
  4.7 0.5 %collective-permute-start.2 = (f32[520,128]{1,0:T(8,128)S(1)}, f32[520,128]{1,0:T(8,128)S(1)}, u32[]{:S(2)}, u32[]{:S(2)}) collective-permute-start(f32[520,128]{1,0:T(8,128)S(1)} %get-tuple-element.26), channel_id=1, source_target_pairs={{0,1},{1,0},{2,3},{3,2},{4,5},{5,4},{6,7},{7,6},{8,9},{9,8},{10,11... | collective-permute-start | bytes 798728 | tf_op jit(solution)/shard_map/ppermute | solution.py:741
  5.2 2.7 %collective-permute-start = (f32[3,210,128]{2,1,0:T(8,128)S(1)}, f32[3,210,128]{2,1,0:T(8,128)S(1)}, u32[]{:S(2)}, u32[]{:S(2)}) collective-permute-start(f32[3,210,128]{2,1,0:T(8,128)S(1)} %get-tuple-element.23), channel_id=1, source_target_pairs={{0,4},{4,0},{8,12},{12,8},{1,5},{5,1},{9,13},{13,9},{2,6},{6,2},{1... | collective-permute-start | bytes 967688 | tf_op jit(solution)/shard_map/ppermute | solution.py:742
  7.9 0.7 %collective-permute-start.1 = (f32[3,210,128]{2,1,0:T(8,128)S(1)}, f32[3,210,128]{2,1,0:T(8,128)S(1)}, u32[]{:S(2)}, u32[]{:S(2)}) collective-permute-start(f32[3,210,128]{2,1,0:T(8,128)S(1)} %get-tuple-element.24), channel_id=1, source_target_pairs={{4,8},{8,4},{5,9},{9,5},{6,10},{10,6},{7,11},{11,7},{20,24},{24,20... | collective-permute-start | bytes 967688 | tf_op jit(solution)/shard_map/ppermute | solution.py:743
  8.6 0.0 collective-permute-done.2.refs_1_.refs_2_
  8.6 1.6 %collective-permute-start.3 = (f32[260,128]{1,0:T(8,128)S(1)}, f32[260,128]{1,0:T(8,128)S(1)}, u32[]{:S(2)}, u32[]{:S(2)}) collective-permute-start(f32[260,128]{1,0:T(8,128)S(1)} %get-tuple-element.29), channel_id=1, source_target_pairs={{0,2},{2,0},{1,3},{3,1},{4,6},{6,4},{5,7},{7,5},{8,10},{10,8},{9,1... | collective-permute-start | bytes 399368 | tf_op jit(solution)/shard_map/ppermute | solution.py:754
  10.2 4.2 %collective-permute-done.3.refs_4_ = f32[260,128]{1,0:T(8,128)S(1)} collective-permute-done((f32[260,128]{1,0:T(8,128)S(1)}, f32[260,128]{1,0:T(8,128)S(1)}, u32[]{:S(2)}, u32[]{:S(2)}) %collective-permute-start.3) | collective-permute-done | bytes 133152 | tf_op jit(solution)/shard_map/ppermute | solution.py:754
  14.3 1.1 %aim.1 = (f32[5,2,64,128]{3,2,1,0:T(8,128)S(1)}, f32[120,128]{1,0:T(8,128)S(1)}, f32[140,128]{1,0:T(8,128)S(1)}, f32[120,128]{1,0:T(8,128)S(1)}, f32[140,128]{1,0:T(8,128)S(1)}) custom-call(s32[24]{0:T(128)S(1)} %get-tuple-element.21.refs_0_, f32[10,128,128]{2,1,0:T(8,128)S(1)} %get-tuple-element.25.refs_1_, ...), custom_call_target="tpu_custom_call" | custom-call | tf_op jit(solution)/shard_map/aim/pallas_call | solution.py:775
  15.4 0.8 %collective-permute-done.refs_1_.refs_3_ = f32[3,210,128]{2,1,0:T(8,128)S(1)} collective-permute-done((f32[3,210,128]{2,1,0:T(8,128)S(1)}, f32[3,210,128]{2,1,0:T(8,128)S(1)}, u32[]{:S(2)}, u32[]{:S(2)}) %collective-permute-start) | collective-permute-done | bytes 322592 | tf_op jit(solution)/shard_map/ppermute | solution.py:742
  16.3 0.0 collective-permute-done.1.refs_2_.refs_4_
  16.3 0.0 copy-done
  16.3 0.7 %edge_cols.1 = f32[4,128,128]{2,1,0:T(8,128)S(1)} custom-call(f32[3,5,2,96,192]{4,3,2,1,0:T(8,128)S(1)} %copy-done, f32[3,210,128]{2,1,0:T(8,128)S(1)} %collective-permute-done.refs_1_.refs_3_, f32[3,210,128]{2,1,0:T(8,128)S(1)} %collective-permute-done.1.refs_2_.refs_4_, f32[120,128]{1,0:T(8,128)S(1)} %get-tuple-element.30.refs_3_.refs_6_), custom_call_target="tpu_custom_call" | custom-call | tf_op jit(solution)/shard_map/edge_cols/pallas_call | solution.py:789
  17.0 0.1 collective-permute-start.4
  17.1 4.8 %collective-permute-start.5 = (f32[140,128]{1,0:T(8,128)S(1)}, f32[140,128]{1,0:T(8,128)S(1)}, u32[]{:S(2)}, u32[]{:S(2)}) collective-permute-start(f32[140,128]{1,0:T(8,128)S(1)} %get-tuple-element.35), channel_id=1, source_target_pairs={{0,4},{4,0},{8,12},{12,8},{1,5},{5,1},{9,13},{13,9},{2,6},{6,2},{1... | collective-permute-start | bytes 215048 | tf_op jit(solution)/shard_map/ppermute | solution.py:786
  21.9 0.7 %collective-permute-start.7 = (f32[140,128]{1,0:T(8,128)S(1)}, f32[140,128]{1,0:T(8,128)S(1)}, u32[]{:S(2)}, u32[]{:S(2)}) collective-permute-start(f32[140,128]{1,0:T(8,128)S(1)} %get-tuple-element.37), channel_id=1, source_target_pairs={{4,8},{8,4},{5,9},{9,5},{6,10},{10,6},{7,11},{11,7},{20,24},{24,20... | collective-permute-start | bytes 215048 | tf_op jit(solution)/shard_map/ppermute | solution.py:786
  22.6 2.8 %collective-permute-start.6 = (f32[120,128]{1,0:T(8,128)S(1)}, f32[120,128]{1,0:T(8,128)S(1)}, u32[]{:S(2)}, u32[]{:S(2)}) collective-permute-start(f32[120,128]{1,0:T(8,128)S(1)} %get-tuple-element.36), channel_id=1, source_target_pairs={{0,8},{4,12},{8,0},{12,4},{1,9},{5,13},{9,1},{13,5},{2,10},{6,14},... | collective-permute-start | bytes 184328 | tf_op jit(solution)/shard_map/ppermute | solution.py:786
  25.4 0.0 collective-permute-done.4.refs_5_
  25.4 7.9 %advance.1 = (f32[3,5,2,96,192]{4,3,2,1,0:T(8,128)S(1)}, f32[2,3,112,128]{3,2,1,0:T(8,128)S(1)}, f32[3,5,2,2,32,128]{5,4,3,2,1,0:T(8,128)S(1)}) custom-call(s32[24]{0:T(128)S(1)} %get-tuple-element.21.refs_0_, f32[10,128]{1,0:T(8,128)S(1)} %get-tuple-element.22.refs_1_, f32[3,5,2,96,192]{4,3,2,1,0:T(8,128)S(1)} %copy-done, ...), custom_call_target="tpu_custom_call" | custom-call | tf_op jit(solution)/shard_map/advance/pallas_call | solution.py:800
  33.3 0.0 collective-permute-done.6.refs_8_
  33.3 0.0 collective-permute-done.5.refs_7_
  33.3 0.0 collective-permute-done.7.refs_9_
  33.3 5.1 %settle.1 = (f32[3,5,2,96,192]{4,3,2,1,0:T(8,128)}, f32[5,2,64,128]{3,2,1,0:T(8,128)}) custom-call(s32[24]{0:T(128)S(1)} %get-tuple-element.21.refs_0_, f32[10,128]{1,0:T(8,128)S(1)} %get-tuple-element.22.refs_1_, f32[3,5,2,96,192]{4,3,2,1,0:T(8,128)S(1)} %get-tuple-element.31.refs_2_, f32[2,3,112,128]{3,2,1,0:T(8,128)S(1)} %get-tuple-element.32.refs_3_, ...), custom_call_target="tpu_custom_call" | custom-call | tf_op jit(solution)/shard_map/settle/pallas_call | solution.py:815
  (1 shorter events, 0.0 us)
Async XLA Ops:
  0.6 15.6 %copy-start = (f32[3,5,2,96,192]{4,3,2,1,0:T(8,128)S(1)}, f32[3,5,2,96,192]{4,3,2,1,0:T(8,128)}, u32[]{:S(2)}) copy-start(f32[3,5,2,96,192]{4,3,2,1,0:T(8,128)} %refs_2_.3) | copy-start | bytes 6635524
  4.7 3.9 %collective-permute-start.2 = (f32[520,128]{1,0:T(8,128)S(1)}, f32[520,128]{1,0:T(8,128)S(1)}, u32[]{:S(2)}, u32[]{:S(2)}) collective-permute-start(f32[520,128]{1,0:T(8,128)S(1)} %get-tuple-element.26), channel_id=1, source_target_pairs={{0,1},{1,0},{2,3},{3,2},{4,5},{5,4},{6,7},{7,6},{8,9},{9,8},{10,11... | collective-permute-start | bytes 798728 | tf_op jit(solution)/shard_map/ppermute | solution.py:741
  5.2 11.0 %collective-permute-start = (f32[3,210,128]{2,1,0:T(8,128)S(1)}, f32[3,210,128]{2,1,0:T(8,128)S(1)}, u32[]{:S(2)}, u32[]{:S(2)}) collective-permute-start(f32[3,210,128]{2,1,0:T(8,128)S(1)} %get-tuple-element.23), channel_id=1, source_target_pairs={{0,4},{4,0},{8,12},{12,8},{1,5},{5,1},{9,13},{13,9},{2,6},{6,2},{1... | collective-permute-start | bytes 967688 | tf_op jit(solution)/shard_map/ppermute | solution.py:742
  7.9 8.4 %collective-permute-start.1 = (f32[3,210,128]{2,1,0:T(8,128)S(1)}, f32[3,210,128]{2,1,0:T(8,128)S(1)}, u32[]{:S(2)}, u32[]{:S(2)}) collective-permute-start(f32[3,210,128]{2,1,0:T(8,128)S(1)} %get-tuple-element.24), channel_id=1, source_target_pairs={{4,8},{8,4},{5,9},{9,5},{6,10},{10,6},{7,11},{11,7},{20,24},{24,20... | collective-permute-start | bytes 967688 | tf_op jit(solution)/shard_map/ppermute | solution.py:743
  8.6 5.7 %collective-permute-start.3 = (f32[260,128]{1,0:T(8,128)S(1)}, f32[260,128]{1,0:T(8,128)S(1)}, u32[]{:S(2)}, u32[]{:S(2)}) collective-permute-start(f32[260,128]{1,0:T(8,128)S(1)} %get-tuple-element.29), channel_id=1, source_target_pairs={{0,2},{2,0},{1,3},{3,1},{4,6},{6,4},{5,7},{7,5},{8,10},{10,8},{9,1... | collective-permute-start | bytes 399368 | tf_op jit(solution)/shard_map/ppermute | solution.py:754
  17.0 8.4 %collective-permute-start.4 = (f32[4,128,128]{2,1,0:T(8,128)S(1)}, f32[4,128,128]{2,1,0:T(8,128)S(1)}, u32[]{:S(2)}, u32[]{:S(2)}) collective-permute-start(f32[4,128,128]{2,1,0:T(8,128)S(1)} %edge_cols.1), channel_id=1, source_target_pairs={{0,1},{1,0},{2,3},{3,2},{4,5},{5,4},{6,7},{7,6},{8,9},{9,8},{10,11... | collective-permute-start | bytes 786440 | tf_op jit(solution)/shard_map/ppermute | solution.py:798
  17.1 16.2 %collective-permute-start.5 = (f32[140,128]{1,0:T(8,128)S(1)}, f32[140,128]{1,0:T(8,128)S(1)}, u32[]{:S(2)}, u32[]{:S(2)}) collective-permute-start(f32[140,128]{1,0:T(8,128)S(1)} %get-tuple-element.35), channel_id=1, source_target_pairs={{0,4},{4,0},{8,12},{12,8},{1,5},{5,1},{9,13},{13,9},{2,6},{6,2},{1... | collective-permute-start | bytes 215048 | tf_op jit(solution)/shard_map/ppermute | solution.py:786
  21.9 11.4 %collective-permute-start.7 = (f32[140,128]{1,0:T(8,128)S(1)}, f32[140,128]{1,0:T(8,128)S(1)}, u32[]{:S(2)}, u32[]{:S(2)}) collective-permute-start(f32[140,128]{1,0:T(8,128)S(1)} %get-tuple-element.37), channel_id=1, source_target_pairs={{4,8},{8,4},{5,9},{9,5},{6,10},{10,6},{7,11},{11,7},{20,24},{24,20... | collective-permute-start | bytes 215048 | tf_op jit(solution)/shard_map/ppermute | solution.py:786
  22.6 10.7 %collective-permute-start.6 = (f32[120,128]{1,0:T(8,128)S(1)}, f32[120,128]{1,0:T(8,128)S(1)}, u32[]{:S(2)}, u32[]{:S(2)}) collective-permute-start(f32[120,128]{1,0:T(8,128)S(1)} %get-tuple-element.36), channel_id=1, source_target_pairs={{0,8},{4,12},{8,0},{12,4},{1,9},{5,13},{9,1},{13,5},{2,10},{6,14},... | collective-permute-start | bytes 184328 | tf_op jit(solution)/shard_map/ppermute | solution.py:786

commit v3 on v2

--- a/solution.py
+++ b/solution.py
@@ -54,11 +54,11 @@
 
 
 def strips_kernel(
-    fields, rows, cols, storms, slot_count, strip_rows,
-    centres_in, slots_in, lateral_in, vertical_in, parent_in, nests,
-    send, keep, ring_out, to_pair, to_cross, plan, rates,
+    fields, rows, cols, storms, slot_count,
+    centres_in, slots_in, lateral_in, vertical_in, parent_in, nests_in,
+    send, keep, ring_out, plan, rates, nests,
     plain0, plain1, plain2, turned0, turned1, turned2, block, gather,
-    centres, slots, lateral, vertical, parent, low_rows, high_rows, arrived,
+    centres, slots, lateral, vertical, parent, arrived,
 ):
     sources = (
         (centres_in, centres),
@@ -66,8 +66,7 @@
         (lateral_in, lateral),
         (vertical_in, vertical),
         (parent_in, parent),
-        (nests.at[:, :, :, pl.ds(0, PAD), :], low_rows),
-        (nests.at[:, :, :, pl.ds(strip_rows - PAD, PAD), :], high_rows),
+        (nests_in, nests),
     )
     copies = [
         pltpu.make_async_copy(source, target, arrived.at[i])
@@ -205,24 +204,7 @@
         at = 2 * share + planes * BWP + BWP * p
         send[at : at + BWP, :] = turned2[p, top + cols : top + cols + RING, :]
         ring_out[p] = turned2[p, top : top + cols, :]
-
-    for copy in copies[5:]:
-        copy.wait()
-    even = lax.rem(tile_at, 2) == 0
-    half = nests.shape[4] - LANES
-    lows, highs, tail = slice(0, HALO), slice(PAD - HALO, PAD), slice(LANES, LANES + half)
-    for j in range(slot_count):
-        for f in range(fields):
-            for v in range(2):
-                low, high = low_rows[j, f, v, lows, 0:LANES], high_rows[j, f, v, highs, 0:LANES]
-                at = (2 * f + v) * HALO
-                to_pair[j, at : at + HALO, :] = jnp.where(even, high, low)
-                to_cross[j, at : at + HALO, :] = jnp.where(even, low, high)
-            low = jnp.concatenate([low_rows[j, f, v, lows, tail] for v in range(2)], 1)
-            high = jnp.concatenate([high_rows[j, f, v, highs, tail] for v in range(2)], 1)
-            at = (2 * fields + f) * HALO
-            to_pair[j, at : at + HALO, :] = jnp.where(even, high, low)
-            to_cross[j, at : at + HALO, :] = jnp.where(even, low, high)
+    copies[5].wait()
 
 
 def pair_up_kernel(own, share, rim, keep, got, kept, *sends):
@@ -313,39 +295,49 @@
                 )
 
 
-def edge_cols_kernel(fields, strip_rows, slot_count, nests, pair, cross, after, packed, wide):
+def edge_cols_kernel(fields, slot_count, nests, after, packed, wide):
     del after
-    even = lax.rem(lax.axis_index("tile"), 2) == 0
     west_most = lax.axis_index("lev") == 0
     planes = 2 * fields
     half = nests.shape[4] - LANES
-    packed[...] = jnp.zeros_like(packed)
     wide[...] = jnp.zeros_like(wide)
     lane = lane_iota()
     for q in range(slot_count * planes):
         j, f, v = q // planes, (q % planes) // 2, q % 2
         spot = (q % 8) * 16
-        mask = (lane >= spot) & (lane < spot + HALO)
-        wide[:, 0:half] = nests[j, f, v, :, LANES : LANES + half]
-        cells = jnp.where(west_most, wide[...], nests[j, f, v, :, 0:LANES])
+        wide[q % 8, :, 0:half] = nests[j, f, v, :, LANES : LANES + half]
+        cells = jnp.where(west_most, wide[q % 8], nests[j, f, v, :, 0:LANES])
         shift = jnp.where(west_most, spot + 2 * LANES - (half - HALO), spot + 2 * LANES) % LANES
         cells = pltpu.roll(cells, shift, 1)
-        rows = slice(PAD, PAD + strip_rows)
-        packed[q // 8, rows, :] = jnp.where(mask, cells, packed[q // 8, rows, :])
-        at, rest = (2 * f + v) * HALO, (2 * fields + f) * HALO
-        shift = (
-            jnp.where(west_most, spot + 2 * LANES - (half - HALO) - half * v, spot + 2 * LANES) % LANES
-        )
-        halos = []
-        for got in (pair, cross):
-            cells = jnp.where(west_most, got[j, rest : rest + HALO, :], got[j, at : at + HALO, :])
-            halos.append(pltpu.roll(cells, shift, 1))
-        high = jnp.where(even, halos[0], halos[1])
-        low = jnp.where(even, halos[1], halos[0])
-        rows = slice(PAD - HALO, PAD)
-        packed[q // 8, rows, :] = jnp.where(mask, low, packed[q // 8, rows, :])
-        rows = slice(PAD + strip_rows, PAD + strip_rows + HALO)
-        packed[q // 8, rows, :] = jnp.where(mask, high, packed[q // 8, rows, :])
+        row = cells if q % 8 == 0 else jnp.where(lane >= spot, cells, row)
+        if q % 8 == 7 or q == slot_count * planes - 1:
+            packed[q // 8] = row
+
+
+def edge_rows_kernel(fields, strip_rows, slot_count, nests, packed, after, to_pair, to_cross):
+    del after
+    even = lax.rem(lax.axis_index("tile"), 2) == 0
+    half = nests.shape[4] - LANES
+    lows, highs, tail = slice(0, HALO), slice(strip_rows - HALO, strip_rows), slice(LANES, LANES + half)
+
+    def put(at, low, high):
+        to_pair[at : at + HALO, :] = jnp.where(even, high, low)
+        to_cross[at : at + HALO, :] = jnp.where(even, low, high)
+
+    for j in range(slot_count):
+        for f in range(fields):
+            at = (3 * fields * j + 2 * f) * HALO
+            for v in range(2):
+                put(at + v * HALO, nests[j, f, v, lows, 0:LANES], nests[j, f, v, highs, 0:LANES])
+            at = (3 * fields * j + 2 * fields + f) * HALO
+            put(
+                at,
+                jnp.concatenate([nests[j, f, v, lows, tail] for v in range(2)], 1),
+                jnp.concatenate([nests[j, f, v, highs, tail] for v in range(2)], 1),
+            )
+    for g in range(packed.shape[0]):
+        at = (3 * fields * slot_count + g) * HALO
+        put(at, packed[g, lows, :], packed[g, highs, :])
 
 
 def advance_kernel(
@@ -398,24 +390,24 @@
             for v in range(2):
                 cells[f, v, 0, room : room + strip_rows, :] = nests[j, f, v, :, 0:LANES]
                 cells[f, v, 1, room : room + strip_rows, 0:half] = nests[j, f, v, :, LANES : LANES + half]
+                n = j * planes + 2 * f + v
+                goal_shift = (goal - lax.rem(n, 8) * 16 + 2 * LANES) % LANES
                 ends = []
                 for got in (pair, cross):
-                    tail = got[j, (planes + f) * HALO : (planes + f + 1) * HALO, :]
+                    main = got[pl.ds((3 * fields * j + 2 * f + v) * HALO, HALO), :]
+                    tail = got[pl.ds((3 * fields * j + planes + f) * HALO, HALO), :]
                     if v == 1:
                         tail = pltpu.roll(tail, LANES - half, 1)
-                    ends.append((got[j, (2 * f + v) * HALO : (2 * f + v + 1) * HALO, :], tail))
+                    corner = got[pl.ds((3 * fields * slot_count + lax.div(n, 8)) * HALO, HALO), :]
+                    corner = jnp.where(in_goal, pltpu.roll(corner, goal_shift, 1), 0.0)
+                    ends.append((main, jnp.where(lane < half, tail, corner)))
                 for a in range(2):
-                    low = jnp.where(even, ends[1][a], ends[0][a])
-                    high = jnp.where(even, ends[0][a], ends[1][a])
-                    lanes = slice(0, LANES if a == 0 else half)
-                    cells[f, v, a, room - HALO : room, lanes] = low[:, lanes]
-                    cells[f, v, a, room + strip_rows : room + strip_rows + HALO, lanes] = high[:, lanes]
-                n = j * planes + 2 * f + v
-                got = pltpu.roll(
-                    packed[lax.div(n, 8)], (goal - lax.rem(n, 8) * 16 + 2 * LANES) % LANES, 1
-                )
-                got = jnp.where(in_goal, got, 0.0)
-                cells[f, v, 1, room - PAD : room + strip_rows + PAD, half:LANES] = got[:, half:LANES]
+                    cells[f, v, a, room - HALO : room, :] = jnp.where(even, ends[1][a], ends[0][a])
+                    cells[f, v, a, room + strip_rows : room + strip_rows + HALO, :] = jnp.where(
+                        even, ends[0][a], ends[1][a]
+                    )
+                got = jnp.where(in_goal, pltpu.roll(packed[lax.div(n, 8)], goal_shift, 1), 0.0)
+                cells[f, v, 1, room : room + strip_rows, half:LANES] = got[:, half:LANES]
 
         sides = [None, None]
         for f in range(fields):
@@ -703,18 +695,17 @@
     cross_list = [(t, t - 1 if t % 2 == 0 else t + 1) for t in range(1, tiles - 1)]
     centres = jnp.swapaxes(centres, 1, 2)
 
-    send, keep, ring, to_pair, to_cross, plan, rates = pl.pallas_call(
-        lambda *refs: strips_kernel(fields, rows, cols, storms, slot_count, strip_rows, *refs),
+    send, keep, ring, plan, rates, nests = pl.pallas_call(
+        lambda *refs: strips_kernel(fields, rows, cols, storms, slot_count, *refs),
         in_specs=[HBM_SPEC] * 6,
-        out_specs=[VMEM_SPEC] * 5 + [SMEM_SPEC, VMEM_SPEC],
+        out_specs=[VMEM_SPEC] * 3 + [SMEM_SPEC] + [VMEM_SPEC] * 2,
         out_shape=[
             shaped(2 * share + 2 * rim, LANES),
             shaped(2 * share, LANES),
             shaped(planes, cols, LANES),
-            shaped(slot_count, 3 * fields * HALO, LANES),
-            shaped(slot_count, 3 * fields * HALO, LANES),
             jax.ShapeDtypeStruct((slot_count * PLAN,), jnp.int32),
             shaped(2 * fields, LANES),
+            shaped(*nest_fields.shape),
         ],
         scratch_shapes=[pltpu.VMEM((planes, 2, rows + 16, LANES), f32)] * 3
         + [pltpu.VMEM((planes, cols + 16, LANES), f32)] * 3
@@ -726,9 +717,7 @@
             pltpu.SMEM(lateral_rate.shape, f32),
             pltpu.SMEM(vertical_rate.shape, f32),
             pltpu.VMEM(parent_field.shape, f32),
-            pltpu.VMEM((slot_count, fields, 2, PAD, strip_cols), f32),
-            pltpu.VMEM((slot_count, fields, 2, PAD, strip_cols), f32),
-            pltpu.SemaphoreType.DMA((7,)),
+            pltpu.SemaphoreType.DMA((6,)),
         ],
         compiler_params=params(),
         name="strips",
@@ -739,8 +728,18 @@
         )
     )
     got = lax.ppermute(send, "lev", [(l, l ^ 1) for l in range(levs)])
-    pair = lax.ppermute(to_pair, "tile", pair_list)
-    cross = lax.ppermute(to_cross, "tile", cross_list)
+
+    bundles = -(-slot_count * planes // 8)
+    packed = pl.pallas_call(
+        lambda *refs: edge_cols_kernel(fields, slot_count, *refs),
+        in_specs=[VMEM_SPEC, ANY_SPEC],
+        out_specs=VMEM_SPEC,
+        out_shape=shaped(bundles, strip_rows, LANES),
+        scratch_shapes=[pltpu.VMEM((8, strip_rows, LANES), f32)],
+        compiler_params=params(),
+        name="edge_cols",
+    )(nests, keep)
+    packed = lax.ppermute(packed, "lev", [(l, l ^ 1) for l in range(levs)])
 
     kept, *sends = pl.pallas_call(
         lambda *refs: pair_up_kernel(own, share, rim, *refs),
@@ -755,6 +754,18 @@
         for i, x in enumerate(sends)
     ]
 
+    edge_lines = (3 * fields * slot_count + bundles) * HALO
+    to_pair, to_cross = pl.pallas_call(
+        lambda *refs: edge_rows_kernel(fields, strip_rows, slot_count, *refs),
+        in_specs=[VMEM_SPEC] * 2 + [ANY_SPEC],
+        out_specs=[VMEM_SPEC] * 2,
+        out_shape=[shaped(edge_lines, LANES)] * 2,
+        compiler_params=params(),
+        name="edge_rows",
+    )(nests, packed, kept)
+    pair = lax.ppermute(to_pair, "tile", pair_list)
+    cross = lax.ppermute(to_cross, "tile", cross_list)
+
     def holds(source, dest):
         low = max((strip_rows // 3) * dest - 3, 0)
         high = tiles * rows - FP + min((strip_rows // 3) * (dest + 1) + 3, FP)
@@ -771,7 +782,9 @@
             routes[k] = pairs
     touching = tuple(k for k in routes if any(abs(a - b) == 1 for a, b in routes[k]))
     moves = (0, *routes)
-    zone_shapes = [shaped(own + (rim if k in touching else 0), LANES) for k in moves]
+    zone_shapes = [
+        shaped(own + (rim if k in touching else rim + 8 if k > 0 else 0), LANES) for k in moves
+    ]
     partial, zone_self, *zone_sends = pl.pallas_call(
         lambda *refs: aim_kernel(
             fields, rows, cols, strip_rows, strip_cols, slot_count, moves, share, touching, *refs
@@ -784,18 +797,6 @@
         name="aim",
     )(plan, ring, got, kept, *nest_gots)
     zone_gots = [lax.ppermute(x, "tile", routes[k]) for k, x in zip(moves[1:], zone_sends)]
-
-    bundles = -(-slot_count * planes // 8)
-    packed = pl.pallas_call(
-        lambda *refs: edge_cols_kernel(fields, strip_rows, slot_count, *refs),
-        in_specs=[VMEM_SPEC] * 3 + [ANY_SPEC],
-        out_specs=VMEM_SPEC,
-        out_shape=shaped(bundles, height, LANES),
-        scratch_shapes=[pltpu.VMEM((strip_rows, LANES), f32)],
-        compiler_params=params(),
-        name="edge_cols",
-    )(nest_fields, pair, cross, zone_self)
-    packed = lax.ppermute(packed, "lev", [(l, l ^ 1) for l in range(levs)])
 
     inner, side_in, row_in = pl.pallas_call(
         lambda *refs: advance_kernel(fields, strip_rows, strip_cols, slot_count, *refs),
@@ -810,7 +811,7 @@
         + [pltpu.VMEM((fields, 2, 2, strip_rows + 32, LANES), f32)] * 2,
         compiler_params=params(),
         name="advance",
-    )(plan, rates, nest_fields, pair, cross, packed)
+    )(plan, rates, nests, pair, cross, packed)
 
     nest_final, parent_final = pl.pallas_call(
         lambda *refs: settle_kernel(

time: 38.6 us -> 36.4 us (0.943)
  the two profiles are of different devices: /device:TPU:0 before, /device:TPU:10 now
where the time goes in v3:
time: 36.4 us; the launch traced here: 36.2 us
  Pallas kernels  17.9 us (49%)
  starting transfers between devices  11.8 us (32%)
  waiting for transfers between devices  5.8 us (16%)
  between operations  0.74 us (2%)
    pallas_call x1, Pallas kernels, per_device(): pl.pallas_call(lambda *refs: advance_kernel(fields, strip_rows, strip_col...  7.98 us
    ppermute x3, starting transfers between devices, per_device(): lax.ppermute(x, 'tile', routes[k])  5.44 us
    ppermute x1, waiting for transfers between devices, per_device(): lax.ppermute(x, 'nest', [(n, n ^ i + 1) for n in range(groups)])  4.75 us
    ppermute x1, starting transfers between devices, per_device(): cross = lax.ppermute(to_cross, 'tile', cross_list)  4.58 us
    pallas_call x1, Pallas kernels, per_device(): pl.pallas_call(lambda *refs: settle_kernel(fields, strip_rows, strip_cols...  4.17 us
    pallas_call x1, Pallas kernels, per_device(): pl.pallas_call(lambda *refs: strips_kernel(fields, rows, cols, storms, sl...  3.89 us
    pallas_call x1, Pallas kernels, per_device(): pl.pallas_call(lambda *refs: aim_kernel(fields, rows, cols, strip_rows, s...  1.08 us
  transfers between devices with their start and end apart: 8, of which 3 were waited for; matrix products, arithmetic and copies ran while one was open for 0% of the time, Pallas kernels for 27%

profile of v3, /device:TPU:10, one launch (start us, length us, event | category | flops | bytes accessed | tf_op | source)
XLA Modules:
  0.0 36.2 jit_solution(18252685291873876668)
XLA Ops:
  0.6 3.9 %strips.1 = (f32[520,128]{1,0:T(8,128)S(1)}, f32[480,128]{1,0:T(8,128)S(1)}, f32[10,128,128]{2,1,0:T(8,128)S(1)}, s32[24]{0:T(128)S(1)}, f32[10,128]{1,0:T(8,128)S(1)}, /*index=5*/f32[3,5,2,96,192]{4,3,2,1,0:T(8,128)S(1)}) custom-call(s32[3,2,6]{2,1,0:T(2,128)} %bitcast.1, s32[6]{0:T(128)} %refs_1_.1, f32[5]{0:T(128)} %refs_2_.1, f32[5]{0:T(128)} %refs_3_.1, ...), custom_call_target="tpu_custom_call" | custom-call | tf_op jit(solution)/shard_map/strips/pallas_call | solution.py:698
  4.5 0.1 collective-permute-start.1
  4.6 0.6 %edge_cols.1 = f32[4,96,128]{2,1,0:T(8,128)S(1)} custom-call(f32[3,5,2,96,192]{4,3,2,1,0:T(8,128)S(1)} %get-tuple-element.24.refs_0_.refs_2_, f32[480,128]{1,0:T(8,128)S(1)} %get-tuple-element.25.refs_1_.refs_0_), custom_call_target="tpu_custom_call" | custom-call | tf_op jit(solution)/shard_map/edge_cols/pallas_call | solution.py:733
  5.2 0.6 %collective-permute-start = (f32[4,96,128]{2,1,0:T(8,128)S(1)}, f32[4,96,128]{2,1,0:T(8,128)S(1)}, u32[]{:S(2)}, u32[]{:S(2)}) collective-permute-start(f32[4,96,128]{2,1,0:T(8,128)S(1)} %edge_cols.1), channel_id=1, source_target_pairs={{0,1},{1,0},{2,3},{3,2},{4,5},{5,4},{6,7},{7,6},{8,9},{9,8},{10,11... | collective-permute-start | bytes 589832 | tf_op jit(solution)/shard_map/ppermute | solution.py:742
  5.7 0.4 %collective-permute-done.1.refs_1_.refs_2_ = f32[520,128]{1,0:T(8,128)S(1)} collective-permute-done((f32[520,128]{1,0:T(8,128)S(1)}, f32[520,128]{1,0:T(8,128)S(1)}, u32[]{:S(2)}, u32[]{:S(2)}) %collective-permute-start.1) | collective-permute-done | bytes 266272 | tf_op jit(solution)/shard_map/ppermute | solution.py:730
  6.2 0.6 %collective-permute-done.refs_1_.refs_5_ = f32[4,96,128]{2,1,0:T(8,128)S(1)} collective-permute-done((f32[4,96,128]{2,1,0:T(8,128)S(1)}, f32[4,96,128]{2,1,0:T(8,128)S(1)}, u32[]{:S(2)}, u32[]{:S(2)}) %collective-permute-start) | collective-permute-done | bytes 196640 | tf_op jit(solution)/shard_map/ppermute | solution.py:742
  6.8 0.2 edge_rows.1
  7.0 0.5 %collective-permute-start.2 = (f32[686,128]{1,0:T(8,128)S(1)}, f32[686,128]{1,0:T(8,128)S(1)}, u32[]{:S(2)}, u32[]{:S(2)}) collective-permute-start(f32[686,128]{1,0:T(8,128)S(1)} %get-tuple-element.28), channel_id=1, source_target_pairs={{0,4},{4,0},{8,12},{12,8},{1,5},{5,1},{9,13},{13,9},{2,6},{6,2},{1... | collective-permute-start | bytes 1053704 | tf_op jit(solution)/shard_map/ppermute | solution.py:766
  7.5 4.6 %collective-permute-start.3 = (f32[686,128]{1,0:T(8,128)S(1)}, f32[686,128]{1,0:T(8,128)S(1)}, u32[]{:S(2)}, u32[]{:S(2)}) collective-permute-start(f32[686,128]{1,0:T(8,128)S(1)} %get-tuple-element.29), channel_id=1, source_target_pairs={{4,8},{8,4},{5,9},{9,5},{6,10},{10,6},{7,11},{11,7},{20,24},{24,20... | collective-permute-start | bytes 1053704 | tf_op jit(solution)/shard_map/ppermute | solution.py:767
  12.1 0.6 %collective-permute-start.4 = (f32[260,128]{1,0:T(8,128)S(1)}, f32[260,128]{1,0:T(8,128)S(1)}, u32[]{:S(2)}, u32[]{:S(2)}) collective-permute-start(f32[260,128]{1,0:T(8,128)S(1)} %get-tuple-element.34), channel_id=1, source_target_pairs={{0,2},{2,0},{1,3},{3,1},{4,6},{6,4},{5,7},{7,5},{8,10},{10,8},{9,1... | collective-permute-start | bytes 399368 | tf_op jit(solution)/shard_map/ppermute | solution.py:753
  12.7 4.8 %collective-permute-done.4.refs_4_ = f32[260,128]{1,0:T(8,128)S(1)} collective-permute-done((f32[260,128]{1,0:T(8,128)S(1)}, f32[260,128]{1,0:T(8,128)S(1)}, u32[]{:S(2)}, u32[]{:S(2)}) %collective-permute-start.4) | collective-permute-done | bytes 133152 | tf_op jit(solution)/shard_map/ppermute | solution.py:753
  17.4 1.1 %aim.1 = (f32[5,2,64,128]{3,2,1,0:T(8,128)S(1)}, f32[120,128]{1,0:T(8,128)S(1)}, f32[140,128]{1,0:T(8,128)S(1)}, f32[148,128]{1,0:T(8,128)S(1)}, f32[140,128]{1,0:T(8,128)S(1)}) custom-call(s32[24]{0:T(128)S(1)} %get-tuple-element.22.refs_0_, f32[10,128,128]{2,1,0:T(8,128)S(1)} %get-tuple-element.33.refs_1_, ...), custom_call_target="tpu_custom_call" | custom-call | tf_op jit(solution)/shard_map/aim/pallas_call | solution.py:788
  18.5 0.1 collective-permute-start.6
  18.6 1.7 %collective-permute-start.5 = (f32[140,128]{1,0:T(8,128)S(1)}, f32[140,128]{1,0:T(8,128)S(1)}, u32[]{:S(2)}, u32[]{:S(2)}) collective-permute-start(f32[140,128]{1,0:T(8,128)S(1)} %get-tuple-element.37), channel_id=1, source_target_pairs={{0,4},{4,0},{8,12},{12,8},{1,5},{5,1},{9,13},{13,9},{2,6},{6,2},{1... | collective-permute-start | bytes 215048 | tf_op jit(solution)/shard_map/ppermute | solution.py:799
  20.4 3.6 %collective-permute-start.7 = (f32[140,128]{1,0:T(8,128)S(1)}, f32[140,128]{1,0:T(8,128)S(1)}, u32[]{:S(2)}, u32[]{:S(2)}) collective-permute-start(f32[140,128]{1,0:T(8,128)S(1)} %get-tuple-element.39), channel_id=1, source_target_pairs={{4,8},{8,4},{5,9},{9,5},{6,10},{10,6},{7,11},{11,7},{20,24},{24,20... | collective-permute-start | bytes 215048 | tf_op jit(solution)/shard_map/ppermute | solution.py:799
  24.0 0.0 collective-permute-done.2.refs_3_
  24.0 0.0 collective-permute-done.3.refs_4_
  24.0 8.0 %advance.1 = (f32[3,5,2,96,192]{4,3,2,1,0:T(8,128)S(1)}, f32[2,3,112,128]{3,2,1,0:T(8,128)S(1)}, f32[3,5,2,2,32,128]{5,4,3,2,1,0:T(8,128)S(1)}) custom-call(s32[24]{0:T(128)S(1)} %get-tuple-element.22.refs_0_, f32[10,128]{1,0:T(8,128)S(1)} %get-tuple-element.23.refs_1_, f32[3,5,2,96,192]{4,3,2,1,0:T(8,128)S(1)} %get-tuple-element.24.refs_0_.refs_2_, ...), custom_call_target="tpu_custom_call" | custom-call | tf_op jit(solution)/shard_map/advance/pallas_call | solution.py:801
  32.0 0.0 collective-permute-done.5.refs_7_
  32.0 0.0 collective-permute-done.7.refs_9_
  32.0 0.0 collective-permute-done.6.refs_8_
  32.0 4.2 %settle.1 = (f32[3,5,2,96,192]{4,3,2,1,0:T(8,128)}, f32[5,2,64,128]{3,2,1,0:T(8,128)}) custom-call(s32[24]{0:T(128)S(1)} %get-tuple-element.22.refs_0_, f32[10,128]{1,0:T(8,128)S(1)} %get-tuple-element.23.refs_1_, f32[3,5,2,96,192]{4,3,2,1,0:T(8,128)S(1)} %get-tuple-element.30.refs_2_, f32[2,3,112,128]{3,2,1,0:T(8,128)S(1)} %get-tuple-element.31.refs_3_, ...), custom_call_target="tpu_custom_call" | custom-call | tf_op jit(solution)/shard_map/settle/pallas_call | solution.py:816
  (1 shorter events, 0.0 us)
Async XLA Ops:
  4.5 1.6 %collective-permute-start.1 = (f32[520,128]{1,0:T(8,128)S(1)}, f32[520,128]{1,0:T(8,128)S(1)}, u32[]{:S(2)}, u32[]{:S(2)}) collective-permute-start(f32[520,128]{1,0:T(8,128)S(1)} %get-tuple-element.26), channel_id=1, source_target_pairs={{0,1},{1,0},{2,3},{3,2},{4,5},{5,4},{6,7},{7,6},{8,9},{9,8},{10,11... | collective-permute-start | bytes 798728 | tf_op jit(solution)/shard_map/ppermute | solution.py:730
  5.2 1.6 %collective-permute-start = (f32[4,96,128]{2,1,0:T(8,128)S(1)}, f32[4,96,128]{2,1,0:T(8,128)S(1)}, u32[]{:S(2)}, u32[]{:S(2)}) collective-permute-start(f32[4,96,128]{2,1,0:T(8,128)S(1)} %edge_cols.1), channel_id=1, source_target_pairs={{0,1},{1,0},{2,3},{3,2},{4,5},{5,4},{6,7},{7,6},{8,9},{9,8},{10,11... | collective-permute-start | bytes 589832 | tf_op jit(solution)/shard_map/ppermute | solution.py:742
  7.0 17.0 %collective-permute-start.2 = (f32[686,128]{1,0:T(8,128)S(1)}, f32[686,128]{1,0:T(8,128)S(1)}, u32[]{:S(2)}, u32[]{:S(2)}) collective-permute-start(f32[686,128]{1,0:T(8,128)S(1)} %get-tuple-element.28), channel_id=1, source_target_pairs={{0,4},{4,0},{8,12},{12,8},{1,5},{5,1},{9,13},{13,9},{2,6},{6,2},{1... | collective-permute-start | bytes 1053704 | tf_op jit(solution)/shard_map/ppermute | solution.py:766
  7.5 16.5 %collective-permute-start.3 = (f32[686,128]{1,0:T(8,128)S(1)}, f32[686,128]{1,0:T(8,128)S(1)}, u32[]{:S(2)}, u32[]{:S(2)}) collective-permute-start(f32[686,128]{1,0:T(8,128)S(1)} %get-tuple-element.29), channel_id=1, source_target_pairs={{4,8},{8,4},{5,9},{9,5},{6,10},{10,6},{7,11},{11,7},{20,24},{24,20... | collective-permute-start | bytes 1053704 | tf_op jit(solution)/shard_map/ppermute | solution.py:767
  12.1 5.4 %collective-permute-start.4 = (f32[260,128]{1,0:T(8,128)S(1)}, f32[260,128]{1,0:T(8,128)S(1)}, u32[]{:S(2)}, u32[]{:S(2)}) collective-permute-start(f32[260,128]{1,0:T(8,128)S(1)} %get-tuple-element.34), channel_id=1, source_target_pairs={{0,2},{2,0},{1,3},{3,1},{4,6},{6,4},{5,7},{7,5},{8,10},{10,8},{9,1... | collective-permute-start | bytes 399368 | tf_op jit(solution)/shard_map/ppermute | solution.py:753
  18.5 13.5 %collective-permute-start.6 = (f32[148,128]{1,0:T(8,128)S(1)}, f32[148,128]{1,0:T(8,128)S(1)}, u32[]{:S(2)}, u32[]{:S(2)}) collective-permute-start(f32[148,128]{1,0:T(8,128)S(1)} %get-tuple-element.38), channel_id=1, source_target_pairs={{0,8},{4,12},{8,0},{12,4},{1,9},{5,13},{9,1},{13,5},{2,10},{6,14},... | collective-permute-start | bytes 227336 | tf_op jit(solution)/shard_map/ppermute | solution.py:799
  18.6 13.4 %collective-permute-start.5 = (f32[140,128]{1,0:T(8,128)S(1)}, f32[140,128]{1,0:T(8,128)S(1)}, u32[]{:S(2)}, u32[]{:S(2)}) collective-permute-start(f32[140,128]{1,0:T(8,128)S(1)} %get-tuple-element.37), channel_id=1, source_target_pairs={{0,4},{4,0},{8,12},{12,8},{1,5},{5,1},{9,13},{13,9},{2,6},{6,2},{1... | collective-permute-start | bytes 215048 | tf_op jit(solution)/shard_map/ppermute | solution.py:799
  20.4 11.7 %collective-permute-start.7 = (f32[140,128]{1,0:T(8,128)S(1)}, f32[140,128]{1,0:T(8,128)S(1)}, u32[]{:S(2)}, u32[]{:S(2)}) collective-permute-start(f32[140,128]{1,0:T(8,128)S(1)} %get-tuple-element.39), channel_id=1, source_target_pairs={{4,8},{8,4},{5,9},{9,5},{6,10},{10,6},{7,11},{11,7},{20,24},{24,20... | collective-permute-start | bytes 215048 | tf_op jit(solution)/shard_map/ppermute | solution.py:799

commit v4 on v3

--- a/solution.py
+++ b/solution.py
@@ -14,6 +14,7 @@
 HALO = STEPS * (3 * MOVE + 1)
 PAD = 16
 LANES = 128
+FRAME = 32
 PLAN = 8
 RING = STEPS
 ROW_AT = 32
@@ -227,7 +228,7 @@
     plan, ring, first_got, kept, *refs,
 ):
     crossing = lax.axis_size("nest") - 1
-    nest_gots, rest = refs[:crossing], refs[crossing:]
+    nest_gots, rest = refs[:crossing], refs[crossing + 1 :]
     partial, zone_self, zone_sends, total = rest[0], rest[1], rest[2:-1], rest[-1]
     planes = 2 * fields
     rim = planes * BWP
@@ -340,17 +341,50 @@
         put(at, packed[g, lows, :], packed[g, highs, :])
 
 
-def advance_kernel(
-    fields, strip_rows, strip_cols, slot_count,
-    plan, rates, nests, pair, cross, packed,
-    inner_out, side_out, row_out, cells, first, second,
-):
+def shift_kernel(fields, strip_rows, strip_cols, slot_count, plan, nests, packed, moved, cells):
     planes = 2 * fields
     half = strip_cols - LANES
     room = PAD + 8
     height = strip_rows + 16
-    tile_at, tiles = lax.axis_index("tile"), lax.axis_size("tile")
-    nest_at = lax.axis_index("nest")
+    lane = lane_iota()
+    goal = jnp.where(lax.axis_index("lev") == 0, half, LANES - HALO)
+    in_goal = (lane >= goal) & (lane < goal + HALO)
+    cells[...] = jnp.zeros_like(cells)
+
+    def one(j, _):
+        down, right = plan[j * PLAN + 2], plan[j * PLAN + 3]
+        shift = (LANES - right) % LANES
+        same = (lane + right >= 0) & (lane + right < LANES)
+        start = room - 8 + down
+        for f in range(fields):
+            for v in range(2):
+                cells[f, v, 0, room : room + strip_rows, :] = nests[j, f, v, :, 0:LANES]
+                cells[f, v, 1, room : room + strip_rows, 0:half] = nests[j, f, v, :, LANES : LANES + half]
+                n = j * planes + 2 * f + v
+                goal_shift = (goal - lax.rem(n, 8) * 16 + 2 * LANES) % LANES
+                got = jnp.where(in_goal, pltpu.roll(packed[lax.div(n, 8)], goal_shift, 1), 0.0)
+                cells[f, v, 1, room : room + strip_rows, half:LANES] = got[:, half:LANES]
+        for f in range(fields):
+            for v in range(2):
+                both = [
+                    pltpu.roll(cells[f, v, a, pl.ds(start, height), :], shift, 1) for a in range(2)
+                ]
+                for a in range(2):
+                    moved[j, f, v, a] = jnp.where(same, both[a], both[1 - a])
+        return 0
+
+    lax.fori_loop(0, slot_count, one, 0)
+
+
+def advance_kernel(
+    fields, strip_rows, strip_cols, slot_count,
+    plan, rates, moved, pair, cross,
+    inner_out, side_out, row_out, first, second,
+):
+    planes = 2 * fields
+    half = strip_cols - LANES
+    height = strip_rows + 16
+    tile_at = lax.axis_index("tile")
     lev_at = lax.axis_index("lev")
     even = lax.rem(tile_at, 2) == 0
     lane = lane_iota()
@@ -358,8 +392,8 @@
     chunk = 16 if height % 16 == 0 and strip_rows % 16 == 0 else 8
     row_start = pl.multiple_of(jnp.where(tile_at == 0, 0, strip_rows - 16), 8)
     west_lanes = lane < jnp.where(lev_at == 0, LANES // 2, 0)
-
-    cells[...] = jnp.zeros_like(cells)
+    goal = jnp.where(lev_at == 0, half, LANES - HALO)
+    in_goal = (lane >= goal) & (lane < goal + HALO)
 
     lats = [rates[f : f + 1, :] for f in range(fields)]
     vers = [rates[fields + f : fields + f + 1, :] for f in range(fields)]
@@ -383,13 +417,8 @@
         down, right = plan[j * PLAN + 2], plan[j * PLAN + 3]
         shift = (LANES - right) % LANES
         same = (lane + right >= 0) & (lane + right < LANES)
-        start = room - 8 + down
-        goal = jnp.where(lev_at == 0, half, LANES - HALO)
-        in_goal = (lane >= goal) & (lane < goal + HALO)
-        for f in range(fields):
-            for v in range(2):
-                cells[f, v, 0, room : room + strip_rows, :] = nests[j, f, v, :, 0:LANES]
-                cells[f, v, 1, room : room + strip_rows, 0:half] = nests[j, f, v, :, LANES : LANES + half]
+        for f in range(fields):
+            for v in range(2):
                 n = j * planes + 2 * f + v
                 goal_shift = (goal - lax.rem(n, 8) * 16 + 2 * LANES) % LANES
                 ends = []
@@ -400,24 +429,20 @@
                         tail = pltpu.roll(tail, LANES - half, 1)
                     corner = got[pl.ds((3 * fields * slot_count + lax.div(n, 8)) * HALO, HALO), :]
                     corner = jnp.where(in_goal, pltpu.roll(corner, goal_shift, 1), 0.0)
-                    ends.append((main, jnp.where(lane < half, tail, corner)))
+                    tail = jnp.where(lane < half, tail, corner)
+                    turned = [pltpu.roll(main, shift, 1), pltpu.roll(tail, shift, 1)]
+                    ends.append([jnp.where(same, turned[a], turned[1 - a]) for a in range(2)])
                 for a in range(2):
-                    cells[f, v, a, room - HALO : room, :] = jnp.where(even, ends[1][a], ends[0][a])
-                    cells[f, v, a, room + strip_rows : room + strip_rows + HALO, :] = jnp.where(
-                        even, ends[0][a], ends[1][a]
-                    )
-                got = jnp.where(in_goal, pltpu.roll(packed[lax.div(n, 8)], goal_shift, 1), 0.0)
-                cells[f, v, 1, room : room + strip_rows, half:LANES] = got[:, half:LANES]
+                    first[f, v, a, FRAME - 8 : FRAME - 8 + height, :] = moved[j, f, v, a]
+                    low = jnp.where(even, ends[1][a], ends[0][a])
+                    high = jnp.where(even, ends[0][a], ends[1][a])
+                    first[f, v, a, pl.ds(FRAME - HALO - down, HALO), :] = low
+                    first[f, v, a, pl.ds(FRAME + strip_rows - down, HALO), :] = high
 
         sides = [None, None]
         for f in range(fields):
             for v in range(2):
-                both = [
-                    pltpu.roll(cells[f, v, a, pl.ds(start, height), :], shift, 1) for a in range(2)
-                ]
-                both = [jnp.where(same, both[a], both[1 - a]) for a in range(2)]
-                for a in range(2):
-                    first[f, v, a, 8 : 8 + height, :] = both[a]
+                both = [first[f, v, a, FRAME - 8 : FRAME - 8 + height, :] for a in range(2)]
                 near = jnp.where(west_lanes, both[0], both[1])
                 turn = jnp.where(lev_at == 0, 8, LANES + 16 - half) + f * SLOT
                 near = pltpu.roll(near, turn % LANES, 1)
@@ -427,9 +452,9 @@
         for f in range(fields):
             for v in range(2):
                 for a in range(2):
-                    row_out[j, f, v, a] = first[f, v, a, pl.ds(8 + row_start, 32), :]
+                    row_out[j, f, v, a] = first[f, v, a, pl.ds(FRAME - 8 + row_start, 32), :]
             for c in range(0, height, chunk):
-                new = stencil(f, first, 8 + c, chunk)
+                new = stencil(f, first, FRAME - 8 + c, chunk)
                 for v in range(2):
                     for a in range(2):
                         second[f, v, a, 8 + c : 8 + c + chunk, :] = new[v][a]
@@ -766,6 +791,17 @@
     pair = lax.ppermute(to_pair, "tile", pair_list)
     cross = lax.ppermute(to_cross, "tile", cross_list)
 
+    moved = pl.pallas_call(
+        lambda *refs: shift_kernel(fields, strip_rows, strip_cols, slot_count, *refs),
+        in_specs=[SMEM_SPEC] + [VMEM_SPEC] * 2,
+        out_specs=VMEM_SPEC,
+        out_shape=shaped(slot_count, fields, 2, 2, strip_rows + 16, LANES),
+        scratch_shapes=[pltpu.VMEM((fields, 2, 2, strip_rows + 48, LANES), f32)],
+        compiler_params=params(),
+        cost_estimate=pl.CostEstimate(flops=3_000_000_000, bytes_accessed=10_000_000, transcendentals=0),
+        name="shift",
+    )(plan, nests, packed)
+
     def holds(source, dest):
         low = max((strip_rows // 3) * dest - 3, 0)
         high = tiles * rows - FP + min((strip_rows // 3) * (dest + 1) + 3, FP)
@@ -789,29 +825,31 @@
         lambda *refs: aim_kernel(
             fields, rows, cols, strip_rows, strip_cols, slot_count, moves, share, touching, *refs
         ),
-        in_specs=[SMEM_SPEC] + [VMEM_SPEC] * (2 + groups),
+        in_specs=[SMEM_SPEC] + [VMEM_SPEC] * (2 + groups) + [ANY_SPEC],
         out_specs=[VMEM_SPEC] * (1 + len(moves)),
         out_shape=[shaped(fields, 2, rows, cols), *zone_shapes],
         scratch_shapes=[pltpu.VMEM((2 * own, LANES), f32)],
         compiler_params=params(),
         name="aim",
-    )(plan, ring, got, kept, *nest_gots)
+    )(plan, ring, got, kept, *nest_gots, moved)
     zone_gots = [lax.ppermute(x, "tile", routes[k]) for k, x in zip(moves[1:], zone_sends)]
 
     inner, side_in, row_in = pl.pallas_call(
         lambda *refs: advance_kernel(fields, strip_rows, strip_cols, slot_count, *refs),
-        in_specs=[SMEM_SPEC] + [VMEM_SPEC] * 5,
+        in_specs=[SMEM_SPEC] + [VMEM_SPEC] * 4,
         out_specs=[VMEM_SPEC] * 3,
         out_shape=[
             shaped(*nest_fields.shape),
             shaped(2, slot_count, strip_rows + 16, LANES),
             shaped(slot_count, fields, 2, 2, 32, LANES),
         ],
-        scratch_shapes=[pltpu.VMEM((fields, 2, 2, strip_rows + 48, LANES), f32)]
-        + [pltpu.VMEM((fields, 2, 2, strip_rows + 32, LANES), f32)] * 2,
+        scratch_shapes=[
+            pltpu.VMEM((fields, 2, 2, strip_rows + 2 * FRAME, LANES), f32),
+            pltpu.VMEM((fields, 2, 2, strip_rows + 32, LANES), f32),
+        ],
         compiler_params=params(),
         name="advance",
-    )(plan, rates, nests, pair, cross, packed)
+    )(plan, rates, moved, pair, cross)
 
     nest_final, parent_final = pl.pallas_call(
         lambda *refs: settle_kernel(

time: 36.4 us -> 35.8 us (0.984)
  the two profiles are of different devices: /device:TPU:10 before, /device:TPU:16 now
where the time goes in v4:
time: 35.8 us; the launch traced here: 35.6 us
  Pallas kernels  19.3 us (54%)
  starting transfers between devices  11.2 us (31%)
  waiting for transfers between devices  4.3 us (12%)
  between operations  0.75 us (2%)
    pallas_call x1, Pallas kernels, per_device(): pl.pallas_call(lambda *refs: advance_kernel(fields, strip_rows, strip_col...  7.12 us
    ppermute x3, starting transfers between devices, per_device(): lax.ppermute(x, 'tile', routes[k])  5.44 us
    pallas_call x1, Pallas kernels, per_device(): pl.pallas_call(lambda *refs: settle_kernel(fields, strip_rows, strip_cols...  4.17 us
    pallas_call x1, Pallas kernels, per_device(): pl.pallas_call(lambda *refs: strips_kernel(fields, rows, cols, storms, sl...  3.9 us
    ppermute x1, waiting for transfers between devices, per_device(): cross = lax.ppermute(to_cross, 'tile', cross_list)  3.89 us
    pallas_call x1, Pallas kernels, per_device(): pl.pallas_call(lambda *refs: shift_kernel(fields, strip_rows, strip_cols,...  2.33 us
    ppermute x1, starting transfers between devices, per_device(): cross = lax.ppermute(to_cross, 'tile', cross_list)  1.91 us
    ppermute x1, starting transfers between devices, per_device(): pair = lax.ppermute(to_pair, 'tile', pair_list)  1.64 us
  transfers between devices with their start and end apart: 8, of which 2 were waited for; matrix products, arithmetic and copies ran while one was open for 0% of the time, Pallas kernels for 32%

profile of v4, /device:TPU:16, one launch (start us, length us, event | category | flops | bytes accessed | tf_op | source)
XLA Modules:
  0.0 35.6 jit_solution(10160490394610444879)
XLA Ops:
  0.6 3.9 %strips.1 = (f32[520,128]{1,0:T(8,128)S(1)}, f32[480,128]{1,0:T(8,128)S(1)}, f32[10,128,128]{2,1,0:T(8,128)S(1)}, s32[24]{0:T(128)S(1)}, f32[10,128]{1,0:T(8,128)S(1)}, /*index=5*/f32[3,5,2,96,192]{4,3,2,1,0:T(8,128)S(1)}) custom-call(s32[3,2,6]{2,1,0:T(2,128)} %bitcast.1, s32[6]{0:T(128)} %refs_1_.1, f32[5]{0:T(128)} %refs_2_.1, f32[5]{0:T(128)} %refs_3_.1, ...), custom_call_target="tpu_custom_call" | custom-call | tf_op jit(solution)/shard_map/strips/pallas_call | solution.py:723
  4.5 0.1 collective-permute-start.1
  4.6 0.6 %edge_cols.1 = f32[4,96,128]{2,1,0:T(8,128)S(1)} custom-call(f32[3,5,2,96,192]{4,3,2,1,0:T(8,128)S(1)} %get-tuple-element.24.refs_0_.refs_1_, f32[480,128]{1,0:T(8,128)S(1)} %get-tuple-element.25.refs_1_.refs_0_), custom_call_target="tpu_custom_call" | custom-call | tf_op jit(solution)/shard_map/edge_cols/pallas_call | solution.py:758
  5.2 0.6 %collective-permute-start = (f32[4,96,128]{2,1,0:T(8,128)S(1)}, f32[4,96,128]{2,1,0:T(8,128)S(1)}, u32[]{:S(2)}, u32[]{:S(2)}) collective-permute-start(f32[4,96,128]{2,1,0:T(8,128)S(1)} %edge_cols.1), channel_id=1, source_target_pairs={{0,1},{1,0},{2,3},{3,2},{4,5},{5,4},{6,7},{7,6},{8,9},{9,8},{10,11... | collective-permute-start | bytes 589832 | tf_op jit(solution)/shard_map/ppermute | solution.py:767
  5.7 0.4 %collective-permute-done.1.refs_1_.refs_2_ = f32[520,128]{1,0:T(8,128)S(1)} collective-permute-done((f32[520,128]{1,0:T(8,128)S(1)}, f32[520,128]{1,0:T(8,128)S(1)}, u32[]{:S(2)}, u32[]{:S(2)}) %collective-permute-start.1) | collective-permute-done | bytes 266272 | tf_op jit(solution)/shard_map/ppermute | solution.py:755
  6.2 1.6 %collective-permute-start.4 = (f32[260,128]{1,0:T(8,128)S(1)}, f32[260,128]{1,0:T(8,128)S(1)}, u32[]{:S(2)}, u32[]{:S(2)}) collective-permute-start(f32[260,128]{1,0:T(8,128)S(1)} %get-tuple-element.34), channel_id=1, source_target_pairs={{0,2},{2,0},{1,3},{3,1},{4,6},{6,4},{5,7},{7,5},{8,10},{10,8},{9,1... | collective-permute-start | bytes 399368 | tf_op jit(solution)/shard_map/ppermute | solution.py:778
  7.7 0.0 collective-permute-done.refs_2_.refs_1_
  7.7 0.2 edge_rows.1
  7.9 1.6 %collective-permute-start.2 = (f32[686,128]{1,0:T(8,128)S(1)}, f32[686,128]{1,0:T(8,128)S(1)}, u32[]{:S(2)}, u32[]{:S(2)}) collective-permute-start(f32[686,128]{1,0:T(8,128)S(1)} %get-tuple-element.28), channel_id=1, source_target_pairs={{0,4},{4,0},{8,12},{12,8},{1,5},{5,1},{9,13},{13,9},{2,6},{6,2},{1... | collective-permute-start | bytes 1053704 | tf_op jit(solution)/shard_map/ppermute | solution.py:791
  9.5 1.9 %collective-permute-start.3 = (f32[686,128]{1,0:T(8,128)S(1)}, f32[686,128]{1,0:T(8,128)S(1)}, u32[]{:S(2)}, u32[]{:S(2)}) collective-permute-start(f32[686,128]{1,0:T(8,128)S(1)} %get-tuple-element.29), channel_id=1, source_target_pairs={{4,8},{8,4},{5,9},{9,5},{6,10},{10,6},{7,11},{11,7},{20,24},{24,20... | collective-permute-start | bytes 1053704 | tf_op jit(solution)/shard_map/ppermute | solution.py:792
  11.5 2.3 %shift.1.refs_2_.refs_5_ = f32[3,5,2,2,112,128]{5,4,3,2,1,0:T(8,128)S(1)} custom-call(s32[24]{0:T(128)S(1)} %get-tuple-element.22.refs_0_, f32[3,5,2,96,192]{4,3,2,1,0:T(8,128)S(1)} %get-tuple-element.24.refs_0_.refs_1_, f32[4,96,128]{2,1,0:T(8,128)S(1)} %collective-permute-done.refs_2_.refs_1_), custom_call_target="tpu_custom_call" | custom-call | flops 3000000000 | bytes 10000000 | tf_op jit(solution)/shard_map/shift/pallas_call | solution.py:794
  13.8 0.0 collective-permute-done.4.refs_4_
  13.8 1.1 %aim.1 = (f32[5,2,64,128]{3,2,1,0:T(8,128)S(1)}, f32[120,128]{1,0:T(8,128)S(1)}, f32[140,128]{1,0:T(8,128)S(1)}, f32[148,128]{1,0:T(8,128)S(1)}, f32[140,128]{1,0:T(8,128)S(1)}) custom-call(s32[24]{0:T(128)S(1)} %get-tuple-element.22.refs_0_, f32[10,128,128]{2,1,0:T(8,128)S(1)} %get-tuple-element.33.refs_1_, ...), custom_call_target="tpu_custom_call" | custom-call | tf_op jit(solution)/shard_map/aim/pallas_call | solution.py:824
  14.9 0.1 collective-permute-start.6
  15.0 3.5 %collective-permute-start.5 = (f32[140,128]{1,0:T(8,128)S(1)}, f32[140,128]{1,0:T(8,128)S(1)}, u32[]{:S(2)}, u32[]{:S(2)}) collective-permute-start(f32[140,128]{1,0:T(8,128)S(1)} %get-tuple-element.37), channel_id=1, source_target_pairs={{0,4},{4,0},{8,12},{12,8},{1,5},{5,1},{9,13},{13,9},{2,6},{6,2},{1... | collective-permute-start | bytes 215048 | tf_op jit(solution)/shard_map/ppermute | solution.py:835
  18.4 1.9 %collective-permute-start.7 = (f32[140,128]{1,0:T(8,128)S(1)}, f32[140,128]{1,0:T(8,128)S(1)}, u32[]{:S(2)}, u32[]{:S(2)}) collective-permute-start(f32[140,128]{1,0:T(8,128)S(1)} %get-tuple-element.39), channel_id=1, source_target_pairs={{4,8},{8,4},{5,9},{9,5},{6,10},{10,6},{7,11},{11,7},{20,24},{24,20... | collective-permute-start | bytes 215048 | tf_op jit(solution)/shard_map/ppermute | solution.py:835
  20.4 0.0 collective-permute-done.2.refs_3_
  20.4 3.9 %collective-permute-done.3.refs_4_ = f32[686,128]{1,0:T(8,128)S(1)} collective-permute-done((f32[686,128]{1,0:T(8,128)S(1)}, f32[686,128]{1,0:T(8,128)S(1)}, u32[]{:S(2)}, u32[]{:S(2)}) %collective-permute-start.3) | collective-permute-done | bytes 351264 | tf_op jit(solution)/shard_map/ppermute | solution.py:792
  24.3 7.1 %advance.1 = (f32[3,5,2,96,192]{4,3,2,1,0:T(8,128)S(1)}, f32[2,3,112,128]{3,2,1,0:T(8,128)S(1)}, f32[3,5,2,2,32,128]{5,4,3,2,1,0:T(8,128)S(1)}) custom-call(s32[24]{0:T(128)S(1)} %get-tuple-element.22.refs_0_, f32[10,128]{1,0:T(8,128)S(1)} %get-tuple-element.23.refs_1_, f32[3,5,2,2,112,128]{5,4,3,2,1,0:T(8,128)S(1)} %shift.1.refs_2_.refs_5_, ...), custom_call_target="tpu_custom_call" | custom-call | tf_op jit(solution)/shard_map/advance/pallas_call | solution.py:837
  31.4 0.0 collective-permute-done.5.refs_7_
  31.4 0.0 collective-permute-done.7.refs_9_
  31.4 0.0 collective-permute-done.6.refs_8_
  31.4 4.2 %settle.1 = (f32[3,5,2,96,192]{4,3,2,1,0:T(8,128)}, f32[5,2,64,128]{3,2,1,0:T(8,128)}) custom-call(s32[24]{0:T(128)S(1)} %get-tuple-element.22.refs_0_, f32[10,128]{1,0:T(8,128)S(1)} %get-tuple-element.23.refs_1_, f32[3,5,2,96,192]{4,3,2,1,0:T(8,128)S(1)} %get-tuple-element.30.refs_2_, f32[2,3,112,128]{3,2,1,0:T(8,128)S(1)} %get-tuple-element.31.refs_3_, ...), custom_call_target="tpu_custom_call" | custom-call | tf_op jit(solution)/shard_map/settle/pallas_call | solution.py:854
  (1 shorter events, 0.0 us)
Async XLA Ops:
  4.5 1.6 %collective-permute-start.1 = (f32[520,128]{1,0:T(8,128)S(1)}, f32[520,128]{1,0:T(8,128)S(1)}, u32[]{:S(2)}, u32[]{:S(2)}) collective-permute-start(f32[520,128]{1,0:T(8,128)S(1)} %get-tuple-element.26), channel_id=1, source_target_pairs={{0,1},{1,0},{2,3},{3,2},{4,5},{5,4},{6,7},{7,6},{8,9},{9,8},{10,11... | collective-permute-start | bytes 798728 | tf_op jit(solution)/shard_map/ppermute | solution.py:755
  5.2 2.6 %collective-permute-start = (f32[4,96,128]{2,1,0:T(8,128)S(1)}, f32[4,96,128]{2,1,0:T(8,128)S(1)}, u32[]{:S(2)}, u32[]{:S(2)}) collective-permute-start(f32[4,96,128]{2,1,0:T(8,128)S(1)} %edge_cols.1), channel_id=1, source_target_pairs={{0,1},{1,0},{2,3},{3,2},{4,5},{5,4},{6,7},{7,6},{8,9},{9,8},{10,11... | collective-permute-start | bytes 589832 | tf_op jit(solution)/shard_map/ppermute | solution.py:767
  6.2 7.6 %collective-permute-start.4 = (f32[260,128]{1,0:T(8,128)S(1)}, f32[260,128]{1,0:T(8,128)S(1)}, u32[]{:S(2)}, u32[]{:S(2)}) collective-permute-start(f32[260,128]{1,0:T(8,128)S(1)} %get-tuple-element.34), channel_id=1, source_target_pairs={{0,2},{2,0},{1,3},{3,1},{4,6},{6,4},{5,7},{7,5},{8,10},{10,8},{9,1... | collective-permute-start | bytes 399368 | tf_op jit(solution)/shard_map/ppermute | solution.py:778
  7.9 12.5 %collective-permute-start.2 = (f32[686,128]{1,0:T(8,128)S(1)}, f32[686,128]{1,0:T(8,128)S(1)}, u32[]{:S(2)}, u32[]{:S(2)}) collective-permute-start(f32[686,128]{1,0:T(8,128)S(1)} %get-tuple-element.28), channel_id=1, source_target_pairs={{0,4},{4,0},{8,12},{12,8},{1,5},{5,1},{9,13},{13,9},{2,6},{6,2},{1... | collective-permute-start | bytes 1053704 | tf_op jit(solution)/shard_map/ppermute | solution.py:791
  9.5 14.7 %collective-permute-start.3 = (f32[686,128]{1,0:T(8,128)S(1)}, f32[686,128]{1,0:T(8,128)S(1)}, u32[]{:S(2)}, u32[]{:S(2)}) collective-permute-start(f32[686,128]{1,0:T(8,128)S(1)} %get-tuple-element.29), channel_id=1, source_target_pairs={{4,8},{8,4},{5,9},{9,5},{6,10},{10,6},{7,11},{11,7},{20,24},{24,20... | collective-permute-start | bytes 1053704 | tf_op jit(solution)/shard_map/ppermute | solution.py:792
  14.9 16.5 %collective-permute-start.6 = (f32[148,128]{1,0:T(8,128)S(1)}, f32[148,128]{1,0:T(8,128)S(1)}, u32[]{:S(2)}, u32[]{:S(2)}) collective-permute-start(f32[148,128]{1,0:T(8,128)S(1)} %get-tuple-element.38), channel_id=1, source_target_pairs={{0,8},{4,12},{8,0},{12,4},{1,9},{5,13},{9,1},{13,5},{2,10},{6,14},... | collective-permute-start | bytes 227336 | tf_op jit(solution)/shard_map/ppermute | solution.py:835
  15.0 16.4 %collective-permute-start.5 = (f32[140,128]{1,0:T(8,128)S(1)}, f32[140,128]{1,0:T(8,128)S(1)}, u32[]{:S(2)}, u32[]{:S(2)}) collective-permute-start(f32[140,128]{1,0:T(8,128)S(1)} %get-tuple-element.37), channel_id=1, source_target_pairs={{0,4},{4,0},{8,12},{12,8},{1,5},{5,1},{9,13},{13,9},{2,6},{6,2},{1... | collective-permute-start | bytes 215048 | tf_op jit(solution)/shard_map/ppermute | solution.py:835
  18.4 13.0 %collective-permute-start.7 = (f32[140,128]{1,0:T(8,128)S(1)}, f32[140,128]{1,0:T(8,128)S(1)}, u32[]{:S(2)}, u32[]{:S(2)}) collective-permute-start(f32[140,128]{1,0:T(8,128)S(1)} %get-tuple-element.39), channel_id=1, source_target_pairs={{4,8},{8,4},{5,9},{9,5},{6,10},{10,6},{7,11},{11,7},{20,24},{24,20... | collective-permute-start | bytes 215048 | tf_op jit(solution)/shard_map/ppermute | solution.py:835

commit v5 on v4

--- a/solution.py
+++ b/solution.py
@@ -391,7 +391,7 @@
     first_lane, last_lane = lane == 0, lane == LANES - 1
     chunk = 16 if height % 16 == 0 and strip_rows % 16 == 0 else 8
     row_start = pl.multiple_of(jnp.where(tile_at == 0, 0, strip_rows - 16), 8)
-    west_lanes = lane < jnp.where(lev_at == 0, LANES // 2, 0)
+    outer = (tile_at == 0) | (tile_at == lax.axis_size("tile") - 1)
     goal = jnp.where(lev_at == 0, half, LANES - HALO)
     in_goal = (lane >= goal) & (lane < goal + HALO)
 
@@ -439,20 +439,30 @@
                     first[f, v, a, pl.ds(FRAME - HALO - down, HALO), :] = low
                     first[f, v, a, pl.ds(FRAME + strip_rows - down, HALO), :] = high
 
-        sides = [None, None]
+        for west in (True, False):
+
+            @pl.when(lev_at == 0 if west else lev_at > 0)
+            def _(west=west):
+                turn = 8 if west else LANES + 16 - half
+                for v in range(2):
+                    side = None
+                    for f in range(fields):
+                        near = first[f, v, 1, FRAME - 8 : FRAME - 8 + height, :]
+                        if west:
+                            low = first[f, v, 0, FRAME - 8 : FRAME - 8 + height, :]
+                            near = jnp.where(lane < LANES // 2, low, near)
+                        near = pltpu.roll(near, (turn + f * SLOT) % LANES, 1)
+                        side = near if f == 0 else jnp.where(lane >= f * SLOT, near, side)
+                    side_out[v, j] = side
+
+        @pl.when(outer)
+        def _():
+            for f in range(fields):
+                for v in range(2):
+                    for a in range(2):
+                        row_out[j, f, v, a] = first[f, v, a, pl.ds(FRAME - 8 + row_start, 32), :]
+
         for f in range(fields):
-            for v in range(2):
-                both = [first[f, v, a, FRAME - 8 : FRAME - 8 + height, :] for a in range(2)]
-                near = jnp.where(west_lanes, both[0], both[1])
-                turn = jnp.where(lev_at == 0, 8, LANES + 16 - half) + f * SLOT
-                near = pltpu.roll(near, turn % LANES, 1)
-                sides[v] = near if f == 0 else jnp.where(lane >= f * SLOT, near, sides[v])
-        for v in range(2):
-            side_out[v, j] = sides[v]
-        for f in range(fields):
-            for v in range(2):
-                for a in range(2):
-                    row_out[j, f, v, a] = first[f, v, a, pl.ds(FRAME - 8 + row_start, 32), :]
             for c in range(0, height, chunk):
                 new = stencil(f, first, FRAME - 8 + c, chunk)
                 for v in range(2):
@@ -620,8 +630,6 @@
     line_from = jnp.where(tile_at == 0, 0, 16 - HALO)
     lows = (0, jnp.where(lev_at > 0, half - HALO, LANES))
     highs = (jnp.where(lev_at == 0, HALO, 0), half)
-    along = lane_iota(strip_rows)
-    near_col = [(along >= lows[a]) & (along < highs[a]) for a in range(2)]
     across = lane_iota(16)
     near_row = [
         (line >= line_from)
@@ -631,14 +639,22 @@
     ]
 
     def one(j, _):
-        for f in range(fields):
-            back = (2 * LANES + jnp.where(lev_at == 0, -8, half - 16) - f * SLOT) % LANES
-            for v in range(2):
-                near = pltpu.roll(side_new[v, j, 8 : 8 + strip_rows, :], back, 1)
-                whole[j, f, v, :, 0:LANES] = jnp.where(near_col[0], near, inner[j, f, v, :, 0:LANES])
-                whole[j, f, v, :, LANES : LANES + half] = jnp.where(
-                    near_col[1][:, :half], near[:, :half], inner[j, f, v, :, LANES : LANES + half]
-                )
+        for west in (True, False):
+
+            @pl.when(lev_at == 0 if west else lev_at > 0)
+            def _(west=west):
+                for f in range(fields):
+                    back = (2 * LANES + (-8 if west else half - 16) - f * SLOT) % LANES
+                    for v in range(2):
+                        near = pltpu.roll(side_new[v, j, 8 : 8 + strip_rows, :], back, 1)
+                        first = inner[j, f, v, :, 0:LANES]
+                        second = inner[j, f, v, :, LANES : LANES + half]
+                        if west:
+                            first = jnp.where(lane < HALO, near, first)
+                        else:
+                            second = jnp.where(lane[:, :half] >= half - HALO, near[:, :half], second)
+                        whole[j, f, v, :, 0:LANES] = first
+                        whole[j, f, v, :, LANES : LANES + half] = second
 
         @pl.when(outer)
         def _():

time: 35.8 us -> 34.2 us (0.955)
  Pallas kernels: 19.3 us -> 17.8 us
    pallas_call x1, Pallas kernels: 7.12 us -> 5.55 us  [per_device(): pl.pallas_call(lambda *refs: advance_kernel(fields, strip_rows, strip_col...]
  transfers between devices with their start and end apart: 8 -> 8, of which waited for: 2 -> 2; matrix products, arithmetic and copies ran while one was open for 0% -> 0% of each run, Pallas kernels for 32% -> 29%
where the time goes in v5:
time: 34.2 us; the launch traced here: 34 us
  Pallas kernels  17.8 us (52%)
  starting transfers between devices  11.2 us (33%)
  waiting for transfers between devices  4.3 us (13%)
  between operations  0.75 us (2%)
    pallas_call x1, Pallas kernels, per_device(): pl.pallas_call(lambda *refs: advance_kernel(fields, strip_rows, strip_col...  5.55 us
    ppermute x3, starting transfers between devices, per_device(): lax.ppermute(x, 'tile', routes[k])  5.44 us
    pallas_call x1, Pallas kernels, per_device(): pl.pallas_call(lambda *refs: settle_kernel(fields, strip_rows, strip_cols...  4.17 us
    pallas_call x1, Pallas kernels, per_device(): pl.pallas_call(lambda *refs: strips_kernel(fields, rows, cols, storms, sl...  3.9 us
    ppermute x1, waiting for transfers between devices, per_device(): cross = lax.ppermute(to_cross, 'tile', cross_list)  3.89 us
    pallas_call x1, Pallas kernels, per_device(): pl.pallas_call(lambda *refs: shift_kernel(fields, strip_rows, strip_cols,...  2.33 us
    ppermute x1, starting transfers between devices, per_device(): cross = lax.ppermute(to_cross, 'tile', cross_list)  1.91 us
    ppermute x1, starting transfers between devices, per_device(): pair = lax.ppermute(to_pair, 'tile', pair_list)  1.63 us
  transfers between devices with their start and end apart: 8, of which 2 were waited for; matrix products, arithmetic and copies ran while one was open for 0% of the time, Pallas kernels for 29%

profile of v5, /device:TPU:16, one launch (start us, length us, event | category | flops | bytes accessed | tf_op | source)
XLA Modules:
  0.0 34.0 jit_solution(16711968361541702311)
XLA Ops:
  0.6 3.9 %strips.1 = (f32[520,128]{1,0:T(8,128)S(1)}, f32[480,128]{1,0:T(8,128)S(1)}, f32[10,128,128]{2,1,0:T(8,128)S(1)}, s32[24]{0:T(128)S(1)}, f32[10,128]{1,0:T(8,128)S(1)}, /*index=5*/f32[3,5,2,96,192]{4,3,2,1,0:T(8,128)S(1)}) custom-call(s32[3,2,6]{2,1,0:T(2,128)} %bitcast.1, s32[6]{0:T(128)} %refs_1_.1, f32[5]{0:T(128)} %refs_2_.1, f32[5]{0:T(128)} %refs_3_.1, ...), custom_call_target="tpu_custom_call" | custom-call | tf_op jit(solution)/shard_map/strips/pallas_call | solution.py:739
  4.5 0.1 collective-permute-start.1
  4.6 0.6 %edge_cols.1 = f32[4,96,128]{2,1,0:T(8,128)S(1)} custom-call(f32[3,5,2,96,192]{4,3,2,1,0:T(8,128)S(1)} %get-tuple-element.24.refs_0_.refs_1_, f32[480,128]{1,0:T(8,128)S(1)} %get-tuple-element.25.refs_1_.refs_0_), custom_call_target="tpu_custom_call" | custom-call | tf_op jit(solution)/shard_map/edge_cols/pallas_call | solution.py:774
  5.2 0.6 %collective-permute-start = (f32[4,96,128]{2,1,0:T(8,128)S(1)}, f32[4,96,128]{2,1,0:T(8,128)S(1)}, u32[]{:S(2)}, u32[]{:S(2)}) collective-permute-start(f32[4,96,128]{2,1,0:T(8,128)S(1)} %edge_cols.1), channel_id=1, source_target_pairs={{0,1},{1,0},{2,3},{3,2},{4,5},{5,4},{6,7},{7,6},{8,9},{9,8},{10,11... | collective-permute-start | bytes 589832 | tf_op jit(solution)/shard_map/ppermute | solution.py:783
  5.7 0.4 %collective-permute-done.1.refs_1_.refs_2_ = f32[520,128]{1,0:T(8,128)S(1)} collective-permute-done((f32[520,128]{1,0:T(8,128)S(1)}, f32[520,128]{1,0:T(8,128)S(1)}, u32[]{:S(2)}, u32[]{:S(2)}) %collective-permute-start.1) | collective-permute-done | bytes 266272 | tf_op jit(solution)/shard_map/ppermute | solution.py:771
  6.2 1.6 %collective-permute-start.4 = (f32[260,128]{1,0:T(8,128)S(1)}, f32[260,128]{1,0:T(8,128)S(1)}, u32[]{:S(2)}, u32[]{:S(2)}) collective-permute-start(f32[260,128]{1,0:T(8,128)S(1)} %get-tuple-element.34), channel_id=1, source_target_pairs={{0,2},{2,0},{1,3},{3,1},{4,6},{6,4},{5,7},{7,5},{8,10},{10,8},{9,1... | collective-permute-start | bytes 399368 | tf_op jit(solution)/shard_map/ppermute | solution.py:794
  7.7 0.0 collective-permute-done.refs_2_.refs_1_
  7.7 0.2 edge_rows.1
  7.9 1.6 %collective-permute-start.2 = (f32[686,128]{1,0:T(8,128)S(1)}, f32[686,128]{1,0:T(8,128)S(1)}, u32[]{:S(2)}, u32[]{:S(2)}) collective-permute-start(f32[686,128]{1,0:T(8,128)S(1)} %get-tuple-element.28), channel_id=1, source_target_pairs={{0,4},{4,0},{8,12},{12,8},{1,5},{5,1},{9,13},{13,9},{2,6},{6,2},{1... | collective-permute-start | bytes 1053704 | tf_op jit(solution)/shard_map/ppermute | solution.py:807
  9.5 1.9 %collective-permute-start.3 = (f32[686,128]{1,0:T(8,128)S(1)}, f32[686,128]{1,0:T(8,128)S(1)}, u32[]{:S(2)}, u32[]{:S(2)}) collective-permute-start(f32[686,128]{1,0:T(8,128)S(1)} %get-tuple-element.29), channel_id=1, source_target_pairs={{4,8},{8,4},{5,9},{9,5},{6,10},{10,6},{7,11},{11,7},{20,24},{24,20... | collective-permute-start | bytes 1053704 | tf_op jit(solution)/shard_map/ppermute | solution.py:808
  11.5 2.3 %shift.1.refs_2_.refs_5_ = f32[3,5,2,2,112,128]{5,4,3,2,1,0:T(8,128)S(1)} custom-call(s32[24]{0:T(128)S(1)} %get-tuple-element.22.refs_0_, f32[3,5,2,96,192]{4,3,2,1,0:T(8,128)S(1)} %get-tuple-element.24.refs_0_.refs_1_, f32[4,96,128]{2,1,0:T(8,128)S(1)} %collective-permute-done.refs_2_.refs_1_), custom_call_target="tpu_custom_call" | custom-call | flops 3000000000 | bytes 10000000 | tf_op jit(solution)/shard_map/shift/pallas_call | solution.py:810
  13.8 0.0 collective-permute-done.4.refs_4_
  13.8 1.1 %aim.1 = (f32[5,2,64,128]{3,2,1,0:T(8,128)S(1)}, f32[120,128]{1,0:T(8,128)S(1)}, f32[140,128]{1,0:T(8,128)S(1)}, f32[148,128]{1,0:T(8,128)S(1)}, f32[140,128]{1,0:T(8,128)S(1)}) custom-call(s32[24]{0:T(128)S(1)} %get-tuple-element.22.refs_0_, f32[10,128,128]{2,1,0:T(8,128)S(1)} %get-tuple-element.33.refs_1_, ...), custom_call_target="tpu_custom_call" | custom-call | tf_op jit(solution)/shard_map/aim/pallas_call | solution.py:840
  14.9 0.1 collective-permute-start.6
  15.0 3.5 %collective-permute-start.5 = (f32[140,128]{1,0:T(8,128)S(1)}, f32[140,128]{1,0:T(8,128)S(1)}, u32[]{:S(2)}, u32[]{:S(2)}) collective-permute-start(f32[140,128]{1,0:T(8,128)S(1)} %get-tuple-element.37), channel_id=1, source_target_pairs={{0,4},{4,0},{8,12},{12,8},{1,5},{5,1},{9,13},{13,9},{2,6},{6,2},{1... | collective-permute-start | bytes 215048 | tf_op jit(solution)/shard_map/ppermute | solution.py:851
  18.4 1.9 %collective-permute-start.7 = (f32[140,128]{1,0:T(8,128)S(1)}, f32[140,128]{1,0:T(8,128)S(1)}, u32[]{:S(2)}, u32[]{:S(2)}) collective-permute-start(f32[140,128]{1,0:T(8,128)S(1)} %get-tuple-element.39), channel_id=1, source_target_pairs={{4,8},{8,4},{5,9},{9,5},{6,10},{10,6},{7,11},{11,7},{20,24},{24,20... | collective-permute-start | bytes 215048 | tf_op jit(solution)/shard_map/ppermute | solution.py:851
  20.4 0.0 collective-permute-done.2.refs_3_
  20.4 3.9 %collective-permute-done.3.refs_4_ = f32[686,128]{1,0:T(8,128)S(1)} collective-permute-done((f32[686,128]{1,0:T(8,128)S(1)}, f32[686,128]{1,0:T(8,128)S(1)}, u32[]{:S(2)}, u32[]{:S(2)}) %collective-permute-start.3) | collective-permute-done | bytes 351264 | tf_op jit(solution)/shard_map/ppermute | solution.py:808
  24.3 5.5 %advance.1 = (f32[3,5,2,96,192]{4,3,2,1,0:T(8,128)S(1)}, f32[2,3,112,128]{3,2,1,0:T(8,128)S(1)}, f32[3,5,2,2,32,128]{5,4,3,2,1,0:T(8,128)S(1)}) custom-call(s32[24]{0:T(128)S(1)} %get-tuple-element.22.refs_0_, f32[10,128]{1,0:T(8,128)S(1)} %get-tuple-element.23.refs_1_, f32[3,5,2,2,112,128]{5,4,3,2,1,0:T(8,128)S(1)} %shift.1.refs_2_.refs_5_, ...), custom_call_target="tpu_custom_call" | custom-call | tf_op jit(solution)/shard_map/advance/pallas_call | solution.py:853
  29.8 0.0 collective-permute-done.5.refs_7_
  29.8 0.0 collective-permute-done.7.refs_9_
  29.8 0.0 collective-permute-done.6.refs_8_
  29.8 4.2 %settle.1 = (f32[3,5,2,96,192]{4,3,2,1,0:T(8,128)}, f32[5,2,64,128]{3,2,1,0:T(8,128)}) custom-call(s32[24]{0:T(128)S(1)} %get-tuple-element.22.refs_0_, f32[10,128]{1,0:T(8,128)S(1)} %get-tuple-element.23.refs_1_, f32[3,5,2,96,192]{4,3,2,1,0:T(8,128)S(1)} %get-tuple-element.30.refs_2_, f32[2,3,112,128]{3,2,1,0:T(8,128)S(1)} %get-tuple-element.31.refs_3_, ...), custom_call_target="tpu_custom_call" | custom-call | tf_op jit(solution)/shard_map/settle/pallas_call | solution.py:870
  (1 shorter events, 0.0 us)
Async XLA Ops:
  4.5 1.6 %collective-permute-start.1 = (f32[520,128]{1,0:T(8,128)S(1)}, f32[520,128]{1,0:T(8,128)S(1)}, u32[]{:S(2)}, u32[]{:S(2)}) collective-permute-start(f32[520,128]{1,0:T(8,128)S(1)} %get-tuple-element.26), channel_id=1, source_target_pairs={{0,1},{1,0},{2,3},{3,2},{4,5},{5,4},{6,7},{7,6},{8,9},{9,8},{10,11... | collective-permute-start | bytes 798728 | tf_op jit(solution)/shard_map/ppermute | solution.py:771
  5.2 2.6 %collective-permute-start = (f32[4,96,128]{2,1,0:T(8,128)S(1)}, f32[4,96,128]{2,1,0:T(8,128)S(1)}, u32[]{:S(2)}, u32[]{:S(2)}) collective-permute-start(f32[4,96,128]{2,1,0:T(8,128)S(1)} %edge_cols.1), channel_id=1, source_target_pairs={{0,1},{1,0},{2,3},{3,2},{4,5},{5,4},{6,7},{7,6},{8,9},{9,8},{10,11... | collective-permute-start | bytes 589832 | tf_op jit(solution)/shard_map/ppermute | solution.py:783
  6.2 7.6 %collective-permute-start.4 = (f32[260,128]{1,0:T(8,128)S(1)}, f32[260,128]{1,0:T(8,128)S(1)}, u32[]{:S(2)}, u32[]{:S(2)}) collective-permute-start(f32[260,128]{1,0:T(8,128)S(1)} %get-tuple-element.34), channel_id=1, source_target_pairs={{0,2},{2,0},{1,3},{3,1},{4,6},{6,4},{5,7},{7,5},{8,10},{10,8},{9,1... | collective-permute-start | bytes 399368 | tf_op jit(solution)/shard_map/ppermute | solution.py:794
  7.9 12.5 %collective-permute-start.2 = (f32[686,128]{1,0:T(8,128)S(1)}, f32[686,128]{1,0:T(8,128)S(1)}, u32[]{:S(2)}, u32[]{:S(2)}) collective-permute-start(f32[686,128]{1,0:T(8,128)S(1)} %get-tuple-element.28), channel_id=1, source_target_pairs={{0,4},{4,0},{8,12},{12,8},{1,5},{5,1},{9,13},{13,9},{2,6},{6,2},{1... | collective-permute-start | bytes 1053704 | tf_op jit(solution)/shard_map/ppermute | solution.py:807
  9.5 14.7 %collective-permute-start.3 = (f32[686,128]{1,0:T(8,128)S(1)}, f32[686,128]{1,0:T(8,128)S(1)}, u32[]{:S(2)}, u32[]{:S(2)}) collective-permute-start(f32[686,128]{1,0:T(8,128)S(1)} %get-tuple-element.29), channel_id=1, source_target_pairs={{4,8},{8,4},{5,9},{9,5},{6,10},{10,6},{7,11},{11,7},{20,24},{24,20... | collective-permute-start | bytes 1053704 | tf_op jit(solution)/shard_map/ppermute | solution.py:808
  14.9 14.9 %collective-permute-start.6 = (f32[148,128]{1,0:T(8,128)S(1)}, f32[148,128]{1,0:T(8,128)S(1)}, u32[]{:S(2)}, u32[]{:S(2)}) collective-permute-start(f32[148,128]{1,0:T(8,128)S(1)} %get-tuple-element.38), channel_id=1, source_target_pairs={{0,8},{4,12},{8,0},{12,4},{1,9},{5,13},{9,1},{13,5},{2,10},{6,14},... | collective-permute-start | bytes 227336 | tf_op jit(solution)/shard_map/ppermute | solution.py:851
  15.0 14.8 %collective-permute-start.5 = (f32[140,128]{1,0:T(8,128)S(1)}, f32[140,128]{1,0:T(8,128)S(1)}, u32[]{:S(2)}, u32[]{:S(2)}) collective-permute-start(f32[140,128]{1,0:T(8,128)S(1)} %get-tuple-element.37), channel_id=1, source_target_pairs={{0,4},{4,0},{8,12},{12,8},{1,5},{5,1},{9,13},{13,9},{2,6},{6,2},{1... | collective-permute-start | bytes 215048 | tf_op jit(solution)/shard_map/ppermute | solution.py:851
  18.4 11.4 %collective-permute-start.7 = (f32[140,128]{1,0:T(8,128)S(1)}, f32[140,128]{1,0:T(8,128)S(1)}, u32[]{:S(2)}, u32[]{:S(2)}) collective-permute-start(f32[140,128]{1,0:T(8,128)S(1)} %get-tuple-element.39), channel_id=1, source_target_pairs={{4,8},{8,4},{5,9},{9,5},{6,10},{10,6},{7,11},{11,7},{20,24},{24,20... | collective-permute-start | bytes 215048 | tf_op jit(solution)/shard_map/ppermute | solution.py:851

commit v6 on v5

--- a/solution.py
+++ b/solution.py
@@ -14,6 +14,7 @@
 HALO = STEPS * (3 * MOVE + 1)
 PAD = 16
 LANES = 128
+SLIM = 40
 FRAME = 32
 PLAN = 8
 RING = STEPS
@@ -224,7 +225,7 @@
 
 
 def aim_kernel(
-    fields, rows, cols, strip_rows, strip_cols, slot_count, moves, share, touching,
+    fields, rows, cols, strip_rows, strip_cols, slot_count, moves, share, touching, slims,
     plan, ring, first_got, kept, *refs,
 ):
     crossing = lax.axis_size("nest") - 1
@@ -257,16 +258,23 @@
             for s in range(STEPS):
                 south = origins[s] >= SPLIT
                 wanted = ((dest == 0) & south) | ((dest == tiles - 1) & jnp.logical_not(south))
-                offset = ROW_AT + origins[s] + (strip_rows // 3) * dest - 3 - ZONE_AT
+                at_lane = SLIM * j if k in slims else ZONE_AT
+                offset = ROW_AT + origins[s] + (strip_rows // 3) * dest - 3 - at_lane
                 source = lane + offset
                 fits = (source >= ROW_AT - RING) & (source < ROW_AT + rows + RING)
                 turned = pltpu.roll(side, (64 * LANES - offset) % LANES, 1)
                 turned = jnp.where(fits, turned, 0.0)
-                parts.append(
-                    jnp.where(lane < ZONE_AT, strip * wanted.astype(jnp.float32), turned)
-                )
+                if k not in slims:
+                    turned = jnp.where(lane < ZONE_AT, strip * wanted.astype(jnp.float32), turned)
+                parts.append(turned)
             target = zone_self if k == 0 else zone_sends[moves.index(k) - 1]
-            target[at : at + both, :] = jnp.where(second, parts[1], parts[0])
+            value = jnp.where(second, parts[1], parts[0])
+            if k not in slims:
+                target[at : at + both, :] = value
+            elif j == 0:
+                target[0:both, :] = value
+            else:
+                target[0:both, :] = jnp.where(lane >= SLIM * j, value, target[0:both, :])
 
     from_west = first_got[2 * share + rim : 2 * share + 2 * rim, :]
     from_east = first_got[2 * share : 2 * share + rim, :]
@@ -291,7 +299,8 @@
         for i, k in enumerate(moves[1:]):
             if k in touching:
                 dest = lax.bitwise_xor(tile_at, k)
-                zone_sends[i][own + BWP * p : own + BWP * (p + 1), :] = jnp.where(
+                start = (STEPS * rim if k in slims else own) + BWP * p
+                zone_sends[i][start : start + BWP, :] = jnp.where(
                     dest > tile_at, above, below
                 )
 
@@ -484,7 +493,7 @@
 
 
 def settle_kernel(
-    fields, strip_rows, strip_cols, rows, slot_count, moves, touching,
+    fields, strip_rows, strip_cols, rows, slot_count, moves, touching, slims,
     plan, rates, inner, side_in, row_in, partial, zone_self, *refs,
 ):
     count = len(moves) - 1
@@ -508,7 +517,8 @@
     for i, k in enumerate(moves[1:]):
         if k in touching:
             other = lax.bitwise_xor(tile_at, k)
-            edge = zone_gots[i][own : own + rim, :]
+            start = both if k in slims else own
+            edge = zone_gots[i][start : start + rim, :]
             below = below + jnp.where(other == tile_at - 1, edge, 0.0)
             above = above + jnp.where(other == tile_at + 1, edge, 0.0)
     for p in range(planes):
@@ -524,10 +534,17 @@
     earlier = [[whole_move[j], last_move[j]] for j in range(slot_count)]
 
     total = zone_self[0:own, :]
-    for got in zone_gots:
-        total = total + got[0:own, :]
+    for k, got in zip(moves[1:], zone_gots):
+        if k not in slims:
+            total = total + got[0:own, :]
     zone[...] = jnp.zeros_like(zone)
     zone[0:own, :] = total
+    for k, got in zip(moves[1:], zone_gots):
+        if k in slims:
+            for j in range(slot_count):
+                part = pltpu.roll(got[0:both, :], (LANES + ZONE_AT - SLIM * j) % LANES, 1)
+                part = jnp.where((lane >= ZONE_AT) & (lane < ZONE_AT + SLIM), part, 0.0)
+                zone[j * both : (j + 1) * both, :] = zone[j * both : (j + 1) * both, :] + part
     second = row_iota(both) >= rim
     col_base = lev_at * (strip_cols // 3 - 3)
     col_from = lev_at * strip_cols
@@ -834,12 +851,22 @@
             routes[k] = pairs
     touching = tuple(k for k in routes if any(abs(a - b) == 1 for a, b in routes[k]))
     moves = (0, *routes)
-    zone_shapes = [
-        shaped(own + (rim if k in touching else rim + 8 if k > 0 else 0), LANES) for k in moves
-    ]
+    fits = slot_count * SLIM <= LANES and strip_rows // 3 + 6 <= SLIM
+    slims = tuple(
+        k for k in routes if fits and not any(b in (0, tiles - 1) for _, b in routes[k])
+    )
+
+    def message(k):
+        if k == 0:
+            return own
+        if k not in touching:
+            return own + rim + 8
+        return (STEPS * rim if k in slims else own) + rim
+
+    zone_shapes = [shaped(message(k), LANES) for k in moves]
     partial, zone_self, *zone_sends = pl.pallas_call(
         lambda *refs: aim_kernel(
-            fields, rows, cols, strip_rows, strip_cols, slot_count, moves, share, touching, *refs
+            fields, rows, cols, strip_rows, strip_cols, slot_count, moves, share, touching, slims, *refs
         ),
         in_specs=[SMEM_SPEC] + [VMEM_SPEC] * (2 + groups) + [ANY_SPEC],
         out_specs=[VMEM_SPEC] * (1 + len(moves)),
@@ -869,7 +896,7 @@
 
     nest_final, parent_final = pl.pallas_call(
         lambda *refs: settle_kernel(
-            fields, strip_rows, strip_cols, rows, slot_count, moves, touching, *refs
+            fields, strip_rows, strip_cols, rows, slot_count, moves, touching, slims, *refs
         ),
         in_specs=[SMEM_SPEC] + [VMEM_SPEC] * (5 + len(moves)),
         out_specs=[ANY_SPEC, VMEM_SPEC],

time: 34.2 us -> 34 us (level)
  no operation moved by 1% of the time
where the time goes in v6:
time: 34 us; the launch traced here: 33.8 us
  Pallas kernels  17.9 us (53%)
  starting transfers between devices  11.2 us (33%)
  waiting for transfers between devices  4.04 us (12%)
  between operations  0.75 us (2%)
    pallas_call x1, Pallas kernels, per_device(): pl.pallas_call(lambda *refs: advance_kernel(fields, strip_rows, strip_col...  5.55 us
    ppermute x3, starting transfers between devices, per_device(): lax.ppermute(x, 'tile', routes[k])  5.44 us
    pallas_call x1, Pallas kernels, per_device(): pl.pallas_call(lambda *refs: settle_kernel(fields, strip_rows, strip_cols...  4.24 us
    pallas_call x1, Pallas kernels, per_device(): pl.pallas_call(lambda *refs: strips_kernel(fields, rows, cols, storms, sl...  3.9 us
    ppermute x1, waiting for transfers between devices, per_device(): cross = lax.ppermute(to_cross, 'tile', cross_list)  3.63 us
    pallas_call x1, Pallas kernels, per_device(): pl.pallas_call(lambda *refs: shift_kernel(fields, strip_rows, strip_cols,...  2.33 us
    ppermute x1, starting transfers between devices, per_device(): cross = lax.ppermute(to_cross, 'tile', cross_list)  1.91 us
    ppermute x1, starting transfers between devices, per_device(): pair = lax.ppermute(to_pair, 'tile', pair_list)  1.65 us
  transfers between devices with their start and end apart: 8, of which 2 were waited for; matrix products, arithmetic and copies ran while one was open for 0% of the time, Pallas kernels for 29%

profile of v6, /device:TPU:16, one launch (start us, length us, event | category | flops | bytes accessed | tf_op | source)
XLA Modules:
  0.0 33.8 jit_solution(8864656815425010182)
XLA Ops:
  0.6 3.9 %strips.1 = (f32[520,128]{1,0:T(8,128)S(1)}, f32[480,128]{1,0:T(8,128)S(1)}, f32[10,128,128]{2,1,0:T(8,128)S(1)}, s32[24]{0:T(128)S(1)}, f32[10,128]{1,0:T(8,128)S(1)}, /*index=5*/f32[3,5,2,96,192]{4,3,2,1,0:T(8,128)S(1)}) custom-call(s32[3,2,6]{2,1,0:T(2,128)} %bitcast.1, s32[6]{0:T(128)} %refs_1_.1, f32[5]{0:T(128)} %refs_2_.1, f32[5]{0:T(128)} %refs_3_.1, ...), custom_call_target="tpu_custom_call" | custom-call | tf_op jit(solution)/shard_map/strips/pallas_call | solution.py:756
  4.5 0.1 collective-permute-start.1
  4.6 0.6 %edge_cols.1 = f32[4,96,128]{2,1,0:T(8,128)S(1)} custom-call(f32[3,5,2,96,192]{4,3,2,1,0:T(8,128)S(1)} %get-tuple-element.24.refs_0_.refs_1_, f32[480,128]{1,0:T(8,128)S(1)} %get-tuple-element.25.refs_1_.refs_0_), custom_call_target="tpu_custom_call" | custom-call | tf_op jit(solution)/shard_map/edge_cols/pallas_call | solution.py:791
  5.2 0.6 %collective-permute-start = (f32[4,96,128]{2,1,0:T(8,128)S(1)}, f32[4,96,128]{2,1,0:T(8,128)S(1)}, u32[]{:S(2)}, u32[]{:S(2)}) collective-permute-start(f32[4,96,128]{2,1,0:T(8,128)S(1)} %edge_cols.1), channel_id=1, source_target_pairs={{0,1},{1,0},{2,3},{3,2},{4,5},{5,4},{6,7},{7,6},{8,9},{9,8},{10,11... | collective-permute-start | bytes 589832 | tf_op jit(solution)/shard_map/ppermute | solution.py:800
  5.7 0.4 %collective-permute-done.1.refs_1_.refs_2_ = f32[520,128]{1,0:T(8,128)S(1)} collective-permute-done((f32[520,128]{1,0:T(8,128)S(1)}, f32[520,128]{1,0:T(8,128)S(1)}, u32[]{:S(2)}, u32[]{:S(2)}) %collective-permute-start.1) | collective-permute-done | bytes 266272 | tf_op jit(solution)/shard_map/ppermute | solution.py:788
  6.2 1.6 %collective-permute-start.4 = (f32[260,128]{1,0:T(8,128)S(1)}, f32[260,128]{1,0:T(8,128)S(1)}, u32[]{:S(2)}, u32[]{:S(2)}) collective-permute-start(f32[260,128]{1,0:T(8,128)S(1)} %get-tuple-element.34), channel_id=1, source_target_pairs={{0,2},{2,0},{1,3},{3,1},{4,6},{6,4},{5,7},{7,5},{8,10},{10,8},{9,1... | collective-permute-start | bytes 399368 | tf_op jit(solution)/shard_map/ppermute | solution.py:811
  7.7 0.0 collective-permute-done.refs_2_.refs_1_
  7.7 0.2 edge_rows.1
  7.9 1.6 %collective-permute-start.2 = (f32[686,128]{1,0:T(8,128)S(1)}, f32[686,128]{1,0:T(8,128)S(1)}, u32[]{:S(2)}, u32[]{:S(2)}) collective-permute-start(f32[686,128]{1,0:T(8,128)S(1)} %get-tuple-element.28), channel_id=1, source_target_pairs={{0,4},{4,0},{8,12},{12,8},{1,5},{5,1},{9,13},{13,9},{2,6},{6,2},{1... | collective-permute-start | bytes 1053704 | tf_op jit(solution)/shard_map/ppermute | solution.py:824
  9.5 1.9 %collective-permute-start.3 = (f32[686,128]{1,0:T(8,128)S(1)}, f32[686,128]{1,0:T(8,128)S(1)}, u32[]{:S(2)}, u32[]{:S(2)}) collective-permute-start(f32[686,128]{1,0:T(8,128)S(1)} %get-tuple-element.29), channel_id=1, source_target_pairs={{4,8},{8,4},{5,9},{9,5},{6,10},{10,6},{7,11},{11,7},{20,24},{24,20... | collective-permute-start | bytes 1053704 | tf_op jit(solution)/shard_map/ppermute | solution.py:825
  11.5 2.3 %shift.1.refs_2_.refs_5_ = f32[3,5,2,2,112,128]{5,4,3,2,1,0:T(8,128)S(1)} custom-call(s32[24]{0:T(128)S(1)} %get-tuple-element.22.refs_0_, f32[3,5,2,96,192]{4,3,2,1,0:T(8,128)S(1)} %get-tuple-element.24.refs_0_.refs_1_, f32[4,96,128]{2,1,0:T(8,128)S(1)} %collective-permute-done.refs_2_.refs_1_), custom_call_target="tpu_custom_call" | custom-call | flops 3000000000 | bytes 10000000 | tf_op jit(solution)/shard_map/shift/pallas_call | solution.py:827
  13.8 0.0 collective-permute-done.4.refs_4_
  13.8 1.1 %aim.1 = (f32[5,2,64,128]{3,2,1,0:T(8,128)S(1)}, f32[120,128]{1,0:T(8,128)S(1)}, f32[140,128]{1,0:T(8,128)S(1)}, f32[148,128]{1,0:T(8,128)S(1)}, f32[60,128]{1,0:T(8,128)S(1)}) custom-call(s32[24]{0:T(128)S(1)} %get-tuple-element.22.refs_0_, f32[10,128,128]{2,1,0:T(8,128)S(1)} %get-tuple-element.33.refs_1_, ...), custom_call_target="tpu_custom_call" | custom-call | tf_op jit(solution)/shard_map/aim/pallas_call | solution.py:867
  14.9 0.1 collective-permute-start.6
  15.0 3.5 %collective-permute-start.5 = (f32[140,128]{1,0:T(8,128)S(1)}, f32[140,128]{1,0:T(8,128)S(1)}, u32[]{:S(2)}, u32[]{:S(2)}) collective-permute-start(f32[140,128]{1,0:T(8,128)S(1)} %get-tuple-element.37), channel_id=1, source_target_pairs={{0,4},{4,0},{8,12},{12,8},{1,5},{5,1},{9,13},{13,9},{2,6},{6,2},{1... | collective-permute-start | bytes 215048 | tf_op jit(solution)/shard_map/ppermute | solution.py:878
  18.4 1.9 %collective-permute-start.7 = (f32[60,128]{1,0:T(8,128)S(1)}, f32[60,128]{1,0:T(8,128)S(1)}, u32[]{:S(2)}, u32[]{:S(2)}) collective-permute-start(f32[60,128]{1,0:T(8,128)S(1)} %get-tuple-element.39), channel_id=1, source_target_pairs={{4,8},{8,4},{5,9},{9,5},{6,10},{10,6},{7,11},{11,7},{20,24},{24,20... | collective-permute-start | bytes 92168 | tf_op jit(solution)/shard_map/ppermute | solution.py:878
  20.4 0.0 collective-permute-done.2.refs_3_
  20.4 3.6 %collective-permute-done.3.refs_4_ = f32[686,128]{1,0:T(8,128)S(1)} collective-permute-done((f32[686,128]{1,0:T(8,128)S(1)}, f32[686,128]{1,0:T(8,128)S(1)}, u32[]{:S(2)}, u32[]{:S(2)}) %collective-permute-start.3) | collective-permute-done | bytes 351264 | tf_op jit(solution)/shard_map/ppermute | solution.py:825
  24.0 5.5 %advance.1 = (f32[3,5,2,96,192]{4,3,2,1,0:T(8,128)S(1)}, f32[2,3,112,128]{3,2,1,0:T(8,128)S(1)}, f32[3,5,2,2,32,128]{5,4,3,2,1,0:T(8,128)S(1)}) custom-call(s32[24]{0:T(128)S(1)} %get-tuple-element.22.refs_0_, f32[10,128]{1,0:T(8,128)S(1)} %get-tuple-element.23.refs_1_, f32[3,5,2,2,112,128]{5,4,3,2,1,0:T(8,128)S(1)} %shift.1.refs_2_.refs_5_, ...), custom_call_target="tpu_custom_call" | custom-call | tf_op jit(solution)/shard_map/advance/pallas_call | solution.py:880
  29.6 0.0 collective-permute-done.7.refs_9_
  29.6 0.0 collective-permute-done.5.refs_7_
  29.6 0.0 collective-permute-done.6.refs_8_
  29.6 4.2 %settle.1 = (f32[3,5,2,96,192]{4,3,2,1,0:T(8,128)}, f32[5,2,64,128]{3,2,1,0:T(8,128)}) custom-call(s32[24]{0:T(128)S(1)} %get-tuple-element.22.refs_0_, f32[10,128]{1,0:T(8,128)S(1)} %get-tuple-element.23.refs_1_, f32[3,5,2,96,192]{4,3,2,1,0:T(8,128)S(1)} %get-tuple-element.30.refs_2_, f32[2,3,112,128]{3,2,1,0:T(8,128)S(1)} %get-tuple-element.31.refs_3_, ...), custom_call_target="tpu_custom_call" | custom-call | tf_op jit(solution)/shard_map/settle/pallas_call | solution.py:897
  (1 shorter events, 0.0 us)
Async XLA Ops:
  4.5 1.6 %collective-permute-start.1 = (f32[520,128]{1,0:T(8,128)S(1)}, f32[520,128]{1,0:T(8,128)S(1)}, u32[]{:S(2)}, u32[]{:S(2)}) collective-permute-start(f32[520,128]{1,0:T(8,128)S(1)} %get-tuple-element.26), channel_id=1, source_target_pairs={{0,1},{1,0},{2,3},{3,2},{4,5},{5,4},{6,7},{7,6},{8,9},{9,8},{10,11... | collective-permute-start | bytes 798728 | tf_op jit(solution)/shard_map/ppermute | solution.py:788
  5.2 2.6 %collective-permute-start = (f32[4,96,128]{2,1,0:T(8,128)S(1)}, f32[4,96,128]{2,1,0:T(8,128)S(1)}, u32[]{:S(2)}, u32[]{:S(2)}) collective-permute-start(f32[4,96,128]{2,1,0:T(8,128)S(1)} %edge_cols.1), channel_id=1, source_target_pairs={{0,1},{1,0},{2,3},{3,2},{4,5},{5,4},{6,7},{7,6},{8,9},{9,8},{10,11... | collective-permute-start | bytes 589832 | tf_op jit(solution)/shard_map/ppermute | solution.py:800
  6.2 7.6 %collective-permute-start.4 = (f32[260,128]{1,0:T(8,128)S(1)}, f32[260,128]{1,0:T(8,128)S(1)}, u32[]{:S(2)}, u32[]{:S(2)}) collective-permute-start(f32[260,128]{1,0:T(8,128)S(1)} %get-tuple-element.34), channel_id=1, source_target_pairs={{0,2},{2,0},{1,3},{3,1},{4,6},{6,4},{5,7},{7,5},{8,10},{10,8},{9,1... | collective-permute-start | bytes 399368 | tf_op jit(solution)/shard_map/ppermute | solution.py:811
  7.9 12.5 %collective-permute-start.2 = (f32[686,128]{1,0:T(8,128)S(1)}, f32[686,128]{1,0:T(8,128)S(1)}, u32[]{:S(2)}, u32[]{:S(2)}) collective-permute-start(f32[686,128]{1,0:T(8,128)S(1)} %get-tuple-element.28), channel_id=1, source_target_pairs={{0,4},{4,0},{8,12},{12,8},{1,5},{5,1},{9,13},{13,9},{2,6},{6,2},{1... | collective-permute-start | bytes 1053704 | tf_op jit(solution)/shard_map/ppermute | solution.py:824
  9.5 14.5 %collective-permute-start.3 = (f32[686,128]{1,0:T(8,128)S(1)}, f32[686,128]{1,0:T(8,128)S(1)}, u32[]{:S(2)}, u32[]{:S(2)}) collective-permute-start(f32[686,128]{1,0:T(8,128)S(1)} %get-tuple-element.29), channel_id=1, source_target_pairs={{4,8},{8,4},{5,9},{9,5},{6,10},{10,6},{7,11},{11,7},{20,24},{24,20... | collective-permute-start | bytes 1053704 | tf_op jit(solution)/shard_map/ppermute | solution.py:825
  14.9 14.7 %collective-permute-start.6 = (f32[148,128]{1,0:T(8,128)S(1)}, f32[148,128]{1,0:T(8,128)S(1)}, u32[]{:S(2)}, u32[]{:S(2)}) collective-permute-start(f32[148,128]{1,0:T(8,128)S(1)} %get-tuple-element.38), channel_id=1, source_target_pairs={{0,8},{4,12},{8,0},{12,4},{1,9},{5,13},{9,1},{13,5},{2,10},{6,14},... | collective-permute-start | bytes 227336 | tf_op jit(solution)/shard_map/ppermute | solution.py:878
  15.0 14.6 %collective-permute-start.5 = (f32[140,128]{1,0:T(8,128)S(1)}, f32[140,128]{1,0:T(8,128)S(1)}, u32[]{:S(2)}, u32[]{:S(2)}) collective-permute-start(f32[140,128]{1,0:T(8,128)S(1)} %get-tuple-element.37), channel_id=1, source_target_pairs={{0,4},{4,0},{8,12},{12,8},{1,5},{5,1},{9,13},{13,9},{2,6},{6,2},{1... | collective-permute-start | bytes 215048 | tf_op jit(solution)/shard_map/ppermute | solution.py:878
  18.4 11.1 %collective-permute-start.7 = (f32[60,128]{1,0:T(8,128)S(1)}, f32[60,128]{1,0:T(8,128)S(1)}, u32[]{:S(2)}, u32[]{:S(2)}) collective-permute-start(f32[60,128]{1,0:T(8,128)S(1)} %get-tuple-element.39), channel_id=1, source_target_pairs={{4,8},{8,4},{5,9},{9,5},{6,10},{10,6},{7,11},{11,7},{20,24},{24,20... | collective-permute-start | bytes 92168 | tf_op jit(solution)/shard_map/ppermute | solution.py:878

commit v7 on v6

--- a/solution.py
+++ b/solution.py
@@ -312,16 +312,24 @@
     half = nests.shape[4] - LANES
     wide[...] = jnp.zeros_like(wide)
     lane = lane_iota()
-    for q in range(slot_count * planes):
-        j, f, v = q // planes, (q % planes) // 2, q % 2
-        spot = (q % 8) * 16
-        wide[q % 8, :, 0:half] = nests[j, f, v, :, LANES : LANES + half]
-        cells = jnp.where(west_most, wide[q % 8], nests[j, f, v, :, 0:LANES])
-        shift = jnp.where(west_most, spot + 2 * LANES - (half - HALO), spot + 2 * LANES) % LANES
-        cells = pltpu.roll(cells, shift, 1)
-        row = cells if q % 8 == 0 else jnp.where(lane >= spot, cells, row)
-        if q % 8 == 7 or q == slot_count * planes - 1:
-            packed[q // 8] = row
+    for west in (True, False):
+
+        @pl.when(west_most if west else jnp.logical_not(west_most))
+        def _(west=west):
+            row = None
+            for q in range(slot_count * planes):
+                j, f, v = q // planes, (q % planes) // 2, q % 2
+                spot = (q % 8) * 16
+                if west:
+                    wide[q % 8, :, 0:half] = nests[j, f, v, :, LANES : LANES + half]
+                    cells = wide[q % 8]
+                else:
+                    cells = nests[j, f, v, :, 0:LANES]
+                turn = (spot + (2 * LANES - (half - HALO) if west else 0)) % LANES
+                cells = pltpu.roll(cells, turn, 1) if turn else cells
+                row = cells if q % 8 == 0 else jnp.where(lane >= spot, cells, row)
+                if q % 8 == 7 or q == slot_count * planes - 1:
+                    packed[q // 8] = row
 
 
 def edge_rows_kernel(fields, strip_rows, slot_count, nests, packed, after, to_pair, to_cross):

time: 34 us -> 34 us (level)
  no operation moved by 1% of the time
where the time goes in v7:
time: 34 us; the launch traced here: 33.8 us
  Pallas kernels  17.8 us (52%)
  starting transfers between devices  11.1 us (33%)
  waiting for transfers between devices  4.17 us (12%)
  between operations  0.75 us (2%)
    pallas_call x1, Pallas kernels, per_device(): pl.pallas_call(lambda *refs: advance_kernel(fields, strip_rows, strip_col...  5.55 us
    ppermute x3, starting transfers between devices, per_device(): lax.ppermute(x, 'tile', routes[k])  5.44 us
    pallas_call x1, Pallas kernels, per_device(): pl.pallas_call(lambda *refs: settle_kernel(fields, strip_rows, strip_cols...  4.24 us
    pallas_call x1, Pallas kernels, per_device(): pl.pallas_call(lambda *refs: strips_kernel(fields, rows, cols, storms, sl...  3.89 us
    ppermute x1, waiting for transfers between devices, per_device(): cross = lax.ppermute(to_cross, 'tile', cross_list)  3.63 us
    pallas_call x1, Pallas kernels, per_device(): pl.pallas_call(lambda *refs: shift_kernel(fields, strip_rows, strip_cols,...  2.33 us
    ppermute x1, starting transfers between devices, per_device(): cross = lax.ppermute(to_cross, 'tile', cross_list)  1.91 us
    ppermute x1, starting transfers between devices, per_device(): pair = lax.ppermute(to_pair, 'tile', pair_list)  1.63 us
  transfers between devices with their start and end apart: 8, of which 2 were waited for; matrix products, arithmetic and copies ran while one was open for 0% of the time, Pallas kernels for 29%

profile of v7, /device:TPU:16, one launch (start us, length us, event | category | flops | bytes accessed | tf_op | source)
XLA Modules:
  0.0 33.8 jit_solution(11710583310743873766)
XLA Ops:
  0.6 3.9 %strips.1 = (f32[520,128]{1,0:T(8,128)S(1)}, f32[480,128]{1,0:T(8,128)S(1)}, f32[10,128,128]{2,1,0:T(8,128)S(1)}, s32[24]{0:T(128)S(1)}, f32[10,128]{1,0:T(8,128)S(1)}, /*index=5*/f32[3,5,2,96,192]{4,3,2,1,0:T(8,128)S(1)}) custom-call(s32[3,2,6]{2,1,0:T(2,128)} %bitcast.1, s32[6]{0:T(128)} %refs_1_.1, f32[5]{0:T(128)} %refs_2_.1, f32[5]{0:T(128)} %refs_3_.1, ...), custom_call_target="tpu_custom_call" | custom-call | tf_op jit(solution)/shard_map/strips/pallas_call | solution.py:764
  4.5 0.1 collective-permute-start.1
  4.6 0.5 %edge_cols.1 = f32[4,96,128]{2,1,0:T(8,128)S(1)} custom-call(f32[3,5,2,96,192]{4,3,2,1,0:T(8,128)S(1)} %get-tuple-element.24.refs_0_.refs_1_, f32[480,128]{1,0:T(8,128)S(1)} %get-tuple-element.25.refs_1_.refs_0_), custom_call_target="tpu_custom_call" | custom-call | tf_op jit(solution)/shard_map/edge_cols/pallas_call | solution.py:799
  5.2 0.5 %collective-permute-start = (f32[4,96,128]{2,1,0:T(8,128)S(1)}, f32[4,96,128]{2,1,0:T(8,128)S(1)}, u32[]{:S(2)}, u32[]{:S(2)}) collective-permute-start(f32[4,96,128]{2,1,0:T(8,128)S(1)} %edge_cols.1), channel_id=1, source_target_pairs={{0,1},{1,0},{2,3},{3,2},{4,5},{5,4},{6,7},{7,6},{8,9},{9,8},{10,11... | collective-permute-start | bytes 589832 | tf_op jit(solution)/shard_map/ppermute | solution.py:808
  5.6 0.5 %collective-permute-done.1.refs_1_.refs_2_ = f32[520,128]{1,0:T(8,128)S(1)} collective-permute-done((f32[520,128]{1,0:T(8,128)S(1)}, f32[520,128]{1,0:T(8,128)S(1)}, u32[]{:S(2)}, u32[]{:S(2)}) %collective-permute-start.1) | collective-permute-done | bytes 266272 | tf_op jit(solution)/shard_map/ppermute | solution.py:796
  6.2 1.6 %collective-permute-start.4 = (f32[260,128]{1,0:T(8,128)S(1)}, f32[260,128]{1,0:T(8,128)S(1)}, u32[]{:S(2)}, u32[]{:S(2)}) collective-permute-start(f32[260,128]{1,0:T(8,128)S(1)} %get-tuple-element.34), channel_id=1, source_target_pairs={{0,2},{2,0},{1,3},{3,1},{4,6},{6,4},{5,7},{7,5},{8,10},{10,8},{9,1... | collective-permute-start | bytes 399368 | tf_op jit(solution)/shard_map/ppermute | solution.py:819
  7.7 0.0 collective-permute-done.refs_2_.refs_1_
  7.7 0.2 edge_rows.1
  7.9 1.6 %collective-permute-start.2 = (f32[686,128]{1,0:T(8,128)S(1)}, f32[686,128]{1,0:T(8,128)S(1)}, u32[]{:S(2)}, u32[]{:S(2)}) collective-permute-start(f32[686,128]{1,0:T(8,128)S(1)} %get-tuple-element.28), channel_id=1, source_target_pairs={{0,4},{4,0},{8,12},{12,8},{1,5},{5,1},{9,13},{13,9},{2,6},{6,2},{1... | collective-permute-start | bytes 1053704 | tf_op jit(solution)/shard_map/ppermute | solution.py:832
  9.5 1.9 %collective-permute-start.3 = (f32[686,128]{1,0:T(8,128)S(1)}, f32[686,128]{1,0:T(8,128)S(1)}, u32[]{:S(2)}, u32[]{:S(2)}) collective-permute-start(f32[686,128]{1,0:T(8,128)S(1)} %get-tuple-element.29), channel_id=1, source_target_pairs={{4,8},{8,4},{5,9},{9,5},{6,10},{10,6},{7,11},{11,7},{20,24},{24,20... | collective-permute-start | bytes 1053704 | tf_op jit(solution)/shard_map/ppermute | solution.py:833
  11.4 2.3 %shift.1.refs_2_.refs_5_ = f32[3,5,2,2,112,128]{5,4,3,2,1,0:T(8,128)S(1)} custom-call(s32[24]{0:T(128)S(1)} %get-tuple-element.22.refs_0_, f32[3,5,2,96,192]{4,3,2,1,0:T(8,128)S(1)} %get-tuple-element.24.refs_0_.refs_1_, f32[4,96,128]{2,1,0:T(8,128)S(1)} %collective-permute-done.refs_2_.refs_1_), custom_call_target="tpu_custom_call" | custom-call | flops 3000000000 | bytes 10000000 | tf_op jit(solution)/shard_map/shift/pallas_call | solution.py:835
  13.8 0.0 collective-permute-done.4.refs_4_
  13.8 1.1 %aim.1 = (f32[5,2,64,128]{3,2,1,0:T(8,128)S(1)}, f32[120,128]{1,0:T(8,128)S(1)}, f32[140,128]{1,0:T(8,128)S(1)}, f32[148,128]{1,0:T(8,128)S(1)}, f32[60,128]{1,0:T(8,128)S(1)}) custom-call(s32[24]{0:T(128)S(1)} %get-tuple-element.22.refs_0_, f32[10,128,128]{2,1,0:T(8,128)S(1)} %get-tuple-element.33.refs_1_, ...), custom_call_target="tpu_custom_call" | custom-call | tf_op jit(solution)/shard_map/aim/pallas_call | solution.py:875
  14.9 0.1 collective-permute-start.6
  15.0 3.5 %collective-permute-start.5 = (f32[140,128]{1,0:T(8,128)S(1)}, f32[140,128]{1,0:T(8,128)S(1)}, u32[]{:S(2)}, u32[]{:S(2)}) collective-permute-start(f32[140,128]{1,0:T(8,128)S(1)} %get-tuple-element.37), channel_id=1, source_target_pairs={{0,4},{4,0},{8,12},{12,8},{1,5},{5,1},{9,13},{13,9},{2,6},{6,2},{1... | collective-permute-start | bytes 215048 | tf_op jit(solution)/shard_map/ppermute | solution.py:886
  18.4 1.9 %collective-permute-start.7 = (f32[60,128]{1,0:T(8,128)S(1)}, f32[60,128]{1,0:T(8,128)S(1)}, u32[]{:S(2)}, u32[]{:S(2)}) collective-permute-start(f32[60,128]{1,0:T(8,128)S(1)} %get-tuple-element.39), channel_id=1, source_target_pairs={{4,8},{8,4},{5,9},{9,5},{6,10},{10,6},{7,11},{11,7},{20,24},{24,20... | collective-permute-start | bytes 92168 | tf_op jit(solution)/shard_map/ppermute | solution.py:886
  20.3 0.0 collective-permute-done.2.refs_3_
  20.4 3.6 %collective-permute-done.3.refs_4_ = f32[686,128]{1,0:T(8,128)S(1)} collective-permute-done((f32[686,128]{1,0:T(8,128)S(1)}, f32[686,128]{1,0:T(8,128)S(1)}, u32[]{:S(2)}, u32[]{:S(2)}) %collective-permute-start.3) | collective-permute-done | bytes 351264 | tf_op jit(solution)/shard_map/ppermute | solution.py:833
  24.0 5.5 %advance.1 = (f32[3,5,2,96,192]{4,3,2,1,0:T(8,128)S(1)}, f32[2,3,112,128]{3,2,1,0:T(8,128)S(1)}, f32[3,5,2,2,32,128]{5,4,3,2,1,0:T(8,128)S(1)}) custom-call(s32[24]{0:T(128)S(1)} %get-tuple-element.22.refs_0_, f32[10,128]{1,0:T(8,128)S(1)} %get-tuple-element.23.refs_1_, f32[3,5,2,2,112,128]{5,4,3,2,1,0:T(8,128)S(1)} %shift.1.refs_2_.refs_5_, ...), custom_call_target="tpu_custom_call" | custom-call | tf_op jit(solution)/shard_map/advance/pallas_call | solution.py:888
  29.5 0.0 collective-permute-done.7.refs_9_
  29.5 0.0 collective-permute-done.5.refs_7_
  29.6 0.0 collective-permute-done.6.refs_8_
  29.6 4.2 %settle.1 = (f32[3,5,2,96,192]{4,3,2,1,0:T(8,128)}, f32[5,2,64,128]{3,2,1,0:T(8,128)}) custom-call(s32[24]{0:T(128)S(1)} %get-tuple-element.22.refs_0_, f32[10,128]{1,0:T(8,128)S(1)} %get-tuple-element.23.refs_1_, f32[3,5,2,96,192]{4,3,2,1,0:T(8,128)S(1)} %get-tuple-element.30.refs_2_, f32[2,3,112,128]{3,2,1,0:T(8,128)S(1)} %get-tuple-element.31.refs_3_, ...), custom_call_target="tpu_custom_call" | custom-call | tf_op jit(solution)/shard_map/settle/pallas_call | solution.py:905
  (1 shorter events, 0.0 us)
Async XLA Ops:
  4.5 1.6 %collective-permute-start.1 = (f32[520,128]{1,0:T(8,128)S(1)}, f32[520,128]{1,0:T(8,128)S(1)}, u32[]{:S(2)}, u32[]{:S(2)}) collective-permute-start(f32[520,128]{1,0:T(8,128)S(1)} %get-tuple-element.26), channel_id=1, source_target_pairs={{0,1},{1,0},{2,3},{3,2},{4,5},{5,4},{6,7},{7,6},{8,9},{9,8},{10,11... | collective-permute-start | bytes 798728 | tf_op jit(solution)/shard_map/ppermute | solution.py:796
  5.2 2.6 %collective-permute-start = (f32[4,96,128]{2,1,0:T(8,128)S(1)}, f32[4,96,128]{2,1,0:T(8,128)S(1)}, u32[]{:S(2)}, u32[]{:S(2)}) collective-permute-start(f32[4,96,128]{2,1,0:T(8,128)S(1)} %edge_cols.1), channel_id=1, source_target_pairs={{0,1},{1,0},{2,3},{3,2},{4,5},{5,4},{6,7},{7,6},{8,9},{9,8},{10,11... | collective-permute-start | bytes 589832 | tf_op jit(solution)/shard_map/ppermute | solution.py:808
  6.2 7.6 %collective-permute-start.4 = (f32[260,128]{1,0:T(8,128)S(1)}, f32[260,128]{1,0:T(8,128)S(1)}, u32[]{:S(2)}, u32[]{:S(2)}) collective-permute-start(f32[260,128]{1,0:T(8,128)S(1)} %get-tuple-element.34), channel_id=1, source_target_pairs={{0,2},{2,0},{1,3},{3,1},{4,6},{6,4},{5,7},{7,5},{8,10},{10,8},{9,1... | collective-permute-start | bytes 399368 | tf_op jit(solution)/shard_map/ppermute | solution.py:819
  7.9 12.5 %collective-permute-start.2 = (f32[686,128]{1,0:T(8,128)S(1)}, f32[686,128]{1,0:T(8,128)S(1)}, u32[]{:S(2)}, u32[]{:S(2)}) collective-permute-start(f32[686,128]{1,0:T(8,128)S(1)} %get-tuple-element.28), channel_id=1, source_target_pairs={{0,4},{4,0},{8,12},{12,8},{1,5},{5,1},{9,13},{13,9},{2,6},{6,2},{1... | collective-permute-start | bytes 1053704 | tf_op jit(solution)/shard_map/ppermute | solution.py:832
  9.5 14.5 %collective-permute-start.3 = (f32[686,128]{1,0:T(8,128)S(1)}, f32[686,128]{1,0:T(8,128)S(1)}, u32[]{:S(2)}, u32[]{:S(2)}) collective-permute-start(f32[686,128]{1,0:T(8,128)S(1)} %get-tuple-element.29), channel_id=1, source_target_pairs={{4,8},{8,4},{5,9},{9,5},{6,10},{10,6},{7,11},{11,7},{20,24},{24,20... | collective-permute-start | bytes 1053704 | tf_op jit(solution)/shard_map/ppermute | solution.py:833
  14.9 14.7 %collective-permute-start.6 = (f32[148,128]{1,0:T(8,128)S(1)}, f32[148,128]{1,0:T(8,128)S(1)}, u32[]{:S(2)}, u32[]{:S(2)}) collective-permute-start(f32[148,128]{1,0:T(8,128)S(1)} %get-tuple-element.38), channel_id=1, source_target_pairs={{0,8},{4,12},{8,0},{12,4},{1,9},{5,13},{9,1},{13,5},{2,10},{6,14},... | collective-permute-start | bytes 227336 | tf_op jit(solution)/shard_map/ppermute | solution.py:886
  15.0 14.6 %collective-permute-start.5 = (f32[140,128]{1,0:T(8,128)S(1)}, f32[140,128]{1,0:T(8,128)S(1)}, u32[]{:S(2)}, u32[]{:S(2)}) collective-permute-start(f32[140,128]{1,0:T(8,128)S(1)} %get-tuple-element.37), channel_id=1, source_target_pairs={{0,4},{4,0},{8,12},{12,8},{1,5},{5,1},{9,13},{13,9},{2,6},{6,2},{1... | collective-permute-start | bytes 215048 | tf_op jit(solution)/shard_map/ppermute | solution.py:886
  18.4 11.1 %collective-permute-start.7 = (f32[60,128]{1,0:T(8,128)S(1)}, f32[60,128]{1,0:T(8,128)S(1)}, u32[]{:S(2)}, u32[]{:S(2)}) collective-permute-start(f32[60,128]{1,0:T(8,128)S(1)} %get-tuple-element.39), channel_id=1, source_target_pairs={{4,8},{8,4},{5,9},{9,5},{6,10},{10,6},{7,11},{11,7},{20,24},{24,20... | collective-permute-start | bytes 92168 | tf_op jit(solution)/shard_map/ppermute | solution.py:886
